TPU v7x, 512 devices: a whole 4x8x8 slice. The times are simulated.
512 devices in a mesh: lat: 8 (over x, core), lon: 16 (over y, z_hi), mem: 4 (over z_lo).
Axes of the slice: x: 4, y: 8, z: 8 (z_hi: 2, z_lo: 4; z = z_hi * 4 + z_lo), core: 2. Of those that a mesh axis runs over, the one named last changes fastest.
Arguments:
- perturbations: bfloat16 [32, 512, 4096], P('mem', 'lat', 'lon'), may hold values from -6 to 6
- diffusivity: float32 [512, 4096], P('lat', 'lon'), may hold values from 0.19 to 0.249
- sea_mask: int32 [512, 4096], P('lat', 'lon'), may hold values from 0 to 1
- obs_owner: int32 [1048576, 1], P(('lat', 'lon', 'mem')), may hold values from 0 to 127; in each aligned block of 2048 rows (0 to 2047, 2048 to 4095, ...) at most 32 rows name the same one
- obs_cell: int32 [1048576], P(('lat', 'lon', 'mem')), may hold values from 0 to 16383
- obs_depart: float32 [1048576], P(('lat', 'lon', 'mem')), may hold values from -6 to 6
- obs_weight: float32 [1048576], P(('lat', 'lon', 'mem')), may hold values from 0.25 to 2
Outputs:
- increment: float32 [512, 4096], P('lat', 'lon')
- obs_residual: float32 [1048576], P(('lat', 'lon', 'mem'))
Inputs may be any that keep to these rules, and one draw needn't show every extreme that they name: `obs_owner`: within each device's aligned block of 2048 rows no tile is named by more than 32 rows, a bound that some block reaches.
All inputs are finite; a program needn't handle non-finite values.
Results may differ from a plain program's by a relative error of at most 0.0003.
Values sent between devices are 32-bit elements; how exact they have to be, the bound alone decides.
No kernel may reach another device: no remote copies, remote signals or barrier semaphores. Data moves between devices by JAX's collectives and lax.ppermute only.
A program may use at most 64 MiB of HBM per device.

v0:
```python
import jax
import jax.numpy as jnp
from jax import lax
from jax.sharding import PartitionSpec as P

STEPS = 4


def extended(array, sides, width):
    for axis, dim in sides:
        size, length = (lax.axis_size(axis), array.shape[dim])
        up = [(i, (i + 1) % size) for i in range(size)]
        down = [(j, i) for i, j in up]
        last = lax.slice_in_dim(array, length - width, length, axis=dim)
        first = lax.slice_in_dim(array, 0, width, axis=dim)
        before = lax.ppermute(last, axis, up)
        after = lax.ppermute(first, axis, down)
        array = jnp.concatenate([before, array, after], axis=dim)
    return array


def face_weights(rate_padded, sea_padded):
    north_face = 0.5 * (rate_padded[:-1] + rate_padded[1:]) * sea_padded[:-1] * sea_padded[1:]
    east_face = (
        0.5 * (rate_padded[:, :-1] + rate_padded[:, 1:]) * sea_padded[:, :-1] * sea_padded[:, 1:]
    )
    return (north_face, east_face)


def diffuse_once(padded, north_face, east_face):
    centre = padded[:, 1:-1, 1:-1]
    result = centre + north_face[1:, 1:-1] * (padded[:, 2:, 1:-1] - centre)
    result = result - north_face[:-1, 1:-1] * (centre - padded[:, :-2, 1:-1])
    result = result + east_face[1:-1, 1:] * (padded[:, 1:-1, 2:] - centre)
    return result - east_face[1:-1, :-1] * (centre - padded[:, 1:-1, :-2])


def member_total(partial_value):
    return lax.psum(partial_value, "mem")


def covariance(source, member_values, north_face, east_face, sea_cover, divisor):
    spread = member_values * source[None]
    for sweep_index in range(STEPS):
        padded = extended(spread, (("lat", 1), ("lon", 2)), 1)
        spread = diffuse_once(padded, north_face, east_face)
    partial_value = jnp.sum(member_values * spread, axis=0)
    return sea_cover * member_total(partial_value) / divisor


def per_device(perturbations, diffusivity, sea_mask, obs_owner, obs_cell, obs_depart, obs_weight):
    members, tile_rows, tile_cols = perturbations.shape
    divisor = members * lax.axis_size("mem") - 1
    sea_cover = sea_mask.astype(jnp.float32)
    rim_width = 1
    stacked = jnp.stack([diffusivity, sea_cover])
    padded_coef = extended(stacked, (("lat", 1), ("lon", 2)), rim_width)
    lat_index = lax.axis_index("lat")
    row_ids = jnp.arange(tile_rows + 2 * rim_width)
    outside = (row_ids < rim_width) & (lat_index == 0) | (row_ids >= tile_rows + rim_width) & (
        lat_index == lax.axis_size("lat") - 1
    )
    sea_padded = jnp.where(outside[:, None], 0.0, padded_coef[1])
    north_face, east_face = face_weights(padded_coef[0], sea_padded)
    member_values = perturbations.astype(jnp.float32)
    obs_dest = obs_owner[:, 0]
    places = lax.axis_size("lat") * lax.axis_size("lon")
    capacity = max(2, 2 * obs_dest.shape[0] // places)
    matches = (obs_dest[:, None] == jnp.arange(places, dtype=jnp.int32)[None, :]).astype(jnp.int32)
    bucket_rank = jnp.sum((jnp.cumsum(matches, axis=0) - 1) * matches, axis=1)
    send_slot = obs_dest * capacity + bucket_rank
    outgoing = (
        jnp.zeros((2, places * capacity), jnp.float32)
        .at[:, send_slot]
        .set(jnp.stack([obs_depart, obs_weight]))
    )
    cell_slots = jnp.zeros((1, places * capacity), jnp.int32).at[0, send_slot].set(obs_cell)
    got_values, got_cells = (
        lax.all_to_all(outgoing, ("lat", "lon"), split_axis=1, concat_axis=1, tiled=True),
        lax.all_to_all(cell_slots, ("lat", "lon"), split_axis=1, concat_axis=1, tiled=True),
    )
    got_depart = got_values[0]
    got_weight = got_values[1]
    got_cell = got_cells[0]
    tile_cells = tile_rows * tile_cols
    innovation_part = jax.ops.segment_sum(
        got_weight * got_depart, got_cell, num_segments=tile_cells
    ).reshape(tile_rows, tile_cols)
    innovation = member_total(innovation_part)
    first_pass = covariance(innovation, member_values, north_face, east_face, sea_cover, divisor)
    at_obs = first_pass.reshape(-1)[got_cell]
    removed_part = jax.ops.segment_sum(
        got_weight * at_obs, got_cell, num_segments=tile_cells
    ).reshape(tile_rows, tile_cols)
    corrected = member_total(innovation_part - removed_part)
    increment = covariance(corrected, member_values, north_face, east_face, sea_cover, divisor)
    answer = got_depart - increment.reshape(-1)[got_cell]
    returned = lax.all_to_all(
        answer[None], ("lat", "lon"), split_axis=1, concat_axis=1, tiled=True
    )[0]
    obs_residual = returned[send_slot]
    return (increment, obs_residual)


def solution(mesh):
    return jax.shard_map(
        per_device,
        mesh=mesh,
        in_specs=(
            P("mem", "lat", "lon"),
            P("lat", "lon"),
            P("lat", "lon"),
            P(("lat", "lon", "mem"), None),
            P(("lat", "lon", "mem")),
            P(("lat", "lon", "mem")),
            P(("lat", "lon", "mem")),
        ),
        out_specs=(P("lat", "lon"), P(("lat", "lon", "mem"))),
        check_vma=False,
    )
```

profile of v0, /device:TPU:1, one launch (start us, length us, event | category | flops | bytes accessed | tf_op | source)
XLA Modules:
  0.0 772.5 jit_solution(9406048251367164243)
XLA Ops:
  9.9 8.2 %scatter_custom_fusion.3 = s32[4096]{0:T(1024)S(1)} fusion(s32[2048]{0:T(1024)S(1)} %broadcast_select_fusion, s32[2048]{0:T(1024)} %param.11, s32[]{:T(128)} %constant.14.clone.1), kind=kCustom, calls=%fused_computation.221 | custom fusion | bytes 16896
  18.9 21.3 %all-to-all-start = ((s32[1,128,32]{2,0,1:T(1,128)}), s32[1,128,32]{2,0,1:T(1,128)}, u32[]{:S(2)}, u32[]{:S(2)}) async-start(s32[1,128,32]{2,0,1:T(1,128)} %bitcast.6), calls=%async_computation | async-start | bytes 131072 | tf_op jit(solution)/shard_map/all_to_all | solution.py:80
  45.2 9.2 %collective-permute-start.3 = (f32[2,66,1]{2,1,0:T(8,128)}, f32[2,66,1]{2,1,0:T(8,128)}, u32[]{:S(2)}, u32[]{:S(2)}) collective-permute-start(f32[2,66,1]{2,1,0:T(8,128)} %get-tuple-element.35), channel_id=1, source_target_pairs={{4,0},{8,4},{12,8},{16,12},{20,16},{24,20},{28,24},{32,28},{36,32}... | collective-permute-start | bytes 1592 | tf_op jit(solution)/shard_map/ppermute | solution.py:17
  67.9 14.2 %all-to-all-start.1 = ((f32[2,128,32]{2,0,1:T(2,128)}), f32[2,128,32]{2,0,1:T(2,128)S(1)}, u32[]{:S(2)}, u32[]{:S(2)}) async-start(f32[2,128,32]{2,0,1:T(2,128)} %copy.18), calls=%async_computation.1 | async-start | bytes 262144 | tf_op jit(solution)/shard_map/all_to_all | solution.py:79
  84.4 13.1 %all-to-all-done.1 = f32[2,128,32]{2,0,1:T(2,128)S(1)} async-done(((f32[2,128,32]{2,0,1:T(2,128)}), f32[2,128,32]{2,0,1:T(2,128)S(1)}, u32[]{:S(2)}, u32[]{:S(2)}) %all-to-all-start.1) | async-done | bytes 32800 | tf_op jit(solution)/shard_map/all_to_all | solution.py:79
  97.9 25.0 %scatter_custom_fusion.1 = f32[16384]{0:T(1024)S(1)} fusion(s32[4096]{0:T(1024)S(1)} %reshape.146, f32[4096]{0:T(1024)S(1)} %mul.121, f32[]{:T(128)} %constant.13.clone.1), kind=kCustom, calls=%fused_computation.213 | custom fusion | flops 4096 | bytes 65540 | tf_op jit(solution)/shard_map/scatter-add | solution.py:86
  123.6 44.9 %all-reduce.6.cloned.1.call-done = f32[64,256]{1,0:T(8,128)} async-done(((f32[64,256]{1,0:T(8,128)}), f32[64,256]{1,0:T(8,128)}) %all-reduce.6.cloned.1.call-update) | async-done | bytes 65552 | tf_op jit(solution)/shard_map/psum | solution.py:39
  193.7 17.4 %collective-permute-done.6 = f32[8,66,1]{2,1,0:T(8,128)S(1)} collective-permute-done((f32[8,66,1]{2,1,0:T(8,128)S(1)}, f32[8,66,1]{2,1,0:T(8,128)S(1)}, u32[]{:S(2)}, u32[]{:S(2)}) %collective-permute-start.6) | collective-permute-done | bytes 2144 | tf_op jit(solution)/shard_map/ppermute | solution.py:17
  226.4 16.7 %collective-permute-done.11 = f32[8,66,1]{2,1,0:T(8,128)S(1)} collective-permute-done((f32[8,66,1]{2,1,0:T(8,128)S(1)}, f32[8,66,1]{2,1,0:T(8,128)S(1)}, u32[]{:S(2)}, u32[]{:S(2)}) %collective-permute-start.11) | collective-permute-done | bytes 2144 | tf_op jit(solution)/shard_map/ppermute | solution.py:16
  264.0 17.1 %collective-permute-done.15 = f32[8,66,1]{2,1,0:T(8,128)S(1)} collective-permute-done((f32[8,66,1]{2,1,0:T(8,128)S(1)}, f32[8,66,1]{2,1,0:T(8,128)S(1)}, u32[]{:S(2)}, u32[]{:S(2)}) %collective-permute-start.15) | collective-permute-done | bytes 2144 | tf_op jit(solution)/shard_map/ppermute | solution.py:16
  305.8 17.5 %collective-permute-done.18 = f32[8,66,1]{2,1,0:T(8,128)S(1)} collective-permute-done((f32[8,66,1]{2,1,0:T(8,128)S(1)}, f32[8,66,1]{2,1,0:T(8,128)S(1)}, u32[]{:S(2)}, u32[]{:S(2)}) %collective-permute-start.18) | collective-permute-done | bytes 2144 | tf_op jit(solution)/shard_map/ppermute | solution.py:17
  324.5 52.7 %all-reduce.8.cloned.1.call-done = f32[64,256]{1,0:T(8,128)} async-done(((f32[64,256]{1,0:T(8,128)}), f32[64,256]{1,0:T(8,128)}) %all-reduce.8.cloned.1.call-update) | async-done | bytes 65552 | tf_op jit(solution)/shard_map/psum | solution.py:39
  378.1 23.0 %gather_fusion = f32[4096]{0:T(1024)S(1)} fusion(f32[16384]{0:T(1024)S(1)} %bitcast.42, s32[4096]{0:T(1024)S(1)} %broadcast_clamp_fusion), kind=kCustom, calls=%fused_computation | custom fusion | bytes 49152 | tf_op jit(solution)/shard_map/gather | solution.py:91
  401.2 25.0 %scatter_custom_fusion.2 = f32[16384]{0:T(1024)S(1)} fusion(s32[4096]{0:T(1024)S(1)} %reshape.146, f32[4096]{0:T(1024)S(1)} %mul.308, f32[]{:T(128)} %constant.13.clone.1), kind=kCustom, calls=%fused_computation.211 | custom fusion | flops 4096 | bytes 65540 | tf_op jit(solution)/shard_map/scatter-add | solution.py:92
  427.0 53.3 %all-reduce.10.cloned.1.call-done = f32[64,256]{1,0:T(8,128)} async-done(((f32[64,256]{1,0:T(8,128)}), f32[64,256]{1,0:T(8,128)}) %all-reduce.10.cloned.1.call-update) | async-done | bytes 65552 | tf_op jit(solution)/shard_map/psum | solution.py:39
  505.3 17.4 %collective-permute-done.22 = f32[8,66,1]{2,1,0:T(8,128)S(1)} collective-permute-done((f32[8,66,1]{2,1,0:T(8,128)S(1)}, f32[8,66,1]{2,1,0:T(8,128)S(1)}, u32[]{:S(2)}, u32[]{:S(2)}) %collective-permute-start.22) | collective-permute-done | bytes 2144 | tf_op jit(solution)/shard_map/ppermute | solution.py:17
  538.1 16.7 %collective-permute-done.27 = f32[8,66,1]{2,1,0:T(8,128)S(1)} collective-permute-done((f32[8,66,1]{2,1,0:T(8,128)S(1)}, f32[8,66,1]{2,1,0:T(8,128)S(1)}, u32[]{:S(2)}, u32[]{:S(2)}) %collective-permute-start.27) | collective-permute-done | bytes 2144 | tf_op jit(solution)/shard_map/ppermute | solution.py:16
  575.7 17.1 %collective-permute-done.31 = f32[8,66,1]{2,1,0:T(8,128)S(1)} collective-permute-done((f32[8,66,1]{2,1,0:T(8,128)S(1)}, f32[8,66,1]{2,1,0:T(8,128)S(1)}, u32[]{:S(2)}, u32[]{:S(2)}) %collective-permute-start.31) | collective-permute-done | bytes 2144 | tf_op jit(solution)/shard_map/ppermute | solution.py:16
  617.4 17.5 %collective-permute-done.34 = f32[8,66,1]{2,1,0:T(8,128)S(1)} collective-permute-done((f32[8,66,1]{2,1,0:T(8,128)S(1)}, f32[8,66,1]{2,1,0:T(8,128)S(1)}, u32[]{:S(2)}, u32[]{:S(2)}) %collective-permute-start.34) | collective-permute-done | bytes 2144 | tf_op jit(solution)/shard_map/ppermute | solution.py:17
  636.2 52.8 %all-reduce.12.cloned.1.call-done = f32[64,256]{1,0:T(8,128)} async-done(((f32[64,256]{1,0:T(8,128)}), f32[64,256]{1,0:T(8,128)}) %all-reduce.12.cloned.1.call-update) | async-done | bytes 65552 | tf_op jit(solution)/shard_map/psum | solution.py:39
  689.8 23.0 %gather_fusion.1 = f32[4096]{0:T(1024)S(1)} fusion(f32[16384]{0:T(1024)S(1)} %bitcast.43, s32[4096]{0:T(1024)S(1)} %broadcast_clamp_fusion), kind=kCustom, calls=%fused_computation.1 | custom fusion | bytes 49152 | tf_op jit(solution)/shard_map/gather | solution.py:97
  713.6 16.0 %all-to-all-start.2 = ((f32[1,128,32]{2,0,1:T(1,128)}), f32[1,128,32]{2,0,1:T(1,128)S(1)}, u32[]{:S(2)}, u32[]{:S(2)}) async-start(f32[1,128,32]{2,0,1:T(1,128)} %bitcast.18), calls=%async_computation.2 | async-start | bytes 131072 | tf_op jit(solution)/shard_map/all_to_all | solution.py:98
  729.6 14.4 %all-to-all-done.2 = f32[1,128,32]{2,0,1:T(1,128)S(1)} async-done(((f32[1,128,32]{2,0,1:T(1,128)}), f32[1,128,32]{2,0,1:T(1,128)S(1)}, u32[]{:S(2)}, u32[]{:S(2)}) %all-to-all-start.2) | async-done | bytes 16416 | tf_op jit(solution)/shard_map/all_to_all | solution.py:98
  745.4 20.5 %gather_fusion.2 = f32[2048]{0:T(1024)} fusion(f32[4096]{0:T(1024)S(1)} %squeeze.21, s32[2048]{0:T(1024)S(1)} %broadcast_clamp_fusion.1), kind=kCustom, calls=%fused_computation.2 | custom fusion | bytes 24576 | tf_op jit(solution)/shard_map/gather | solution.py:101
  (182 shorter events, 203.7 us)
Async XLA Ops:
  18.9 49.0 %all-to-all-start = ((s32[1,128,32]{2,0,1:T(1,128)}), s32[1,128,32]{2,0,1:T(1,128)}, u32[]{:S(2)}, u32[]{:S(2)}) async-start(s32[1,128,32]{2,0,1:T(1,128)} %bitcast.6), calls=%async_computation | async-start | bytes 131072 | tf_op jit(solution)/shard_map/all_to_all | solution.py:80
  45.2 19.6 %collective-permute-start.3 = (f32[2,66,1]{2,1,0:T(8,128)}, f32[2,66,1]{2,1,0:T(8,128)}, u32[]{:S(2)}, u32[]{:S(2)}) collective-permute-start(f32[2,66,1]{2,1,0:T(8,128)} %get-tuple-element.35), channel_id=1, source_target_pairs={{4,0},{8,4},{12,8},{16,12},{20,16},{24,20},{28,24},{32,28},{36,32}... | collective-permute-start | bytes 1592 | tf_op jit(solution)/shard_map/ppermute | solution.py:17
  67.9 29.6 %all-to-all-start.1 = ((f32[2,128,32]{2,0,1:T(2,128)}), f32[2,128,32]{2,0,1:T(2,128)S(1)}, u32[]{:S(2)}, u32[]{:S(2)}) async-start(f32[2,128,32]{2,0,1:T(2,128)} %copy.18), calls=%async_computation.1 | async-start | bytes 262144 | tf_op jit(solution)/shard_map/all_to_all | solution.py:79
  82.0 86.5 %all-reduce.6.cloned.1.call-start = ((), (), s32[]{:S(2)}) async-start(), calls=%async_computation.3 | async-start | bytes 131072 | tf_op jit(solution)/shard_map/psum | solution.py:39
  123.6 253.6 %all-reduce.8.cloned.1.call-start = ((), (), s32[]{:S(2)}) async-start(), calls=%async_computation.4 | async-start | bytes 131072 | tf_op jit(solution)/shard_map/psum | solution.py:39
  174.8 18.9 %collective-permute-start.7 = (f32[8,66,1]{2,1,0:T(8,128)S(1)}, f32[8,66,1]{2,1,0:T(8,128)S(1)}, u32[]{:S(2)}, u32[]{:S(2)}) collective-permute-start(f32[8,66,1]{2,1,0:T(8,128)S(1)} %get-tuple-element.17), channel_id=1, source_target_pairs={{0,4},{4,8},{8,12},{12,16},{16,20},{20,24},{24,28},{28,32},{32,36}... | collective-permute-start | bytes 6344 | tf_op jit(solution)/shard_map/ppermute | solution.py:16
  179.8 31.2 %collective-permute-start.6 = (f32[8,66,1]{2,1,0:T(8,128)S(1)}, f32[8,66,1]{2,1,0:T(8,128)S(1)}, u32[]{:S(2)}, u32[]{:S(2)}) collective-permute-start(f32[8,66,1]{2,1,0:T(8,128)S(1)} %get-tuple-element.16), channel_id=1, source_target_pairs={{4,0},{8,4},{12,8},{16,12},{20,16},{24,20},{28,24},{32,28},{36,32}... | collective-permute-start | bytes 6344 | tf_op jit(solution)/shard_map/ppermute | solution.py:17
  215.1 28.0 %collective-permute-start.11 = (f32[8,66,1]{2,1,0:T(8,128)S(1)}, f32[8,66,1]{2,1,0:T(8,128)S(1)}, u32[]{:S(2)}, u32[]{:S(2)}) collective-permute-start(f32[8,66,1]{2,1,0:T(8,128)S(1)} %get-tuple-element.15), channel_id=1, source_target_pairs={{0,4},{4,8},{8,12},{12,16},{16,20},{20,24},{24,28},{28,32},{32,36}... | collective-permute-start | bytes 6344 | tf_op jit(solution)/shard_map/ppermute | solution.py:16
  218.4 30.3 %collective-permute-start.10 = (f32[8,66,1]{2,1,0:T(8,128)S(1)}, f32[8,66,1]{2,1,0:T(8,128)S(1)}, u32[]{:S(2)}, u32[]{:S(2)}) collective-permute-start(f32[8,66,1]{2,1,0:T(8,128)S(1)} %get-tuple-element.14), channel_id=1, source_target_pairs={{4,0},{8,4},{12,8},{16,12},{20,16},{24,20},{28,24},{32,28},{36,32}... | collective-permute-start | bytes 6344 | tf_op jit(solution)/shard_map/ppermute | solution.py:17
  252.7 28.5 %collective-permute-start.15 = (f32[8,66,1]{2,1,0:T(8,128)S(1)}, f32[8,66,1]{2,1,0:T(8,128)S(1)}, u32[]{:S(2)}, u32[]{:S(2)}) collective-permute-start(f32[8,66,1]{2,1,0:T(8,128)S(1)} %get-tuple-element.13), channel_id=1, source_target_pairs={{0,4},{4,8},{8,12},{12,16},{16,20},{20,24},{24,28},{28,32},{32,36}... | collective-permute-start | bytes 6344 | tf_op jit(solution)/shard_map/ppermute | solution.py:16
  255.8 28.4 %collective-permute-start.14 = (f32[8,66,1]{2,1,0:T(8,128)S(1)}, f32[8,66,1]{2,1,0:T(8,128)S(1)}, u32[]{:S(2)}, u32[]{:S(2)}) collective-permute-start(f32[8,66,1]{2,1,0:T(8,128)S(1)} %get-tuple-element.12), channel_id=1, source_target_pairs={{4,0},{8,4},{12,8},{16,12},{20,16},{24,20},{28,24},{32,28},{36,32}... | collective-permute-start | bytes 6344 | tf_op jit(solution)/shard_map/ppermute | solution.py:17
  288.3 17.5 %collective-permute-start.19 = (f32[8,66,1]{2,1,0:T(8,128)S(1)}, f32[8,66,1]{2,1,0:T(8,128)S(1)}, u32[]{:S(2)}, u32[]{:S(2)}) collective-permute-start(f32[8,66,1]{2,1,0:T(8,128)S(1)} %get-tuple-element.11), channel_id=1, source_target_pairs={{0,4},{4,8},{8,12},{12,16},{16,20},{20,24},{24,28},{28,32},{32,36}... | collective-permute-start | bytes 6344 | tf_op jit(solution)/shard_map/ppermute | solution.py:16
  294.6 28.6 %collective-permute-start.18 = (f32[8,66,1]{2,1,0:T(8,128)S(1)}, f32[8,66,1]{2,1,0:T(8,128)S(1)}, u32[]{:S(2)}, u32[]{:S(2)}) collective-permute-start(f32[8,66,1]{2,1,0:T(8,128)S(1)} %get-tuple-element.10), channel_id=1, source_target_pairs={{4,0},{8,4},{12,8},{16,12},{20,16},{24,20},{28,24},{32,28},{36,32}... | collective-permute-start | bytes 6344 | tf_op jit(solution)/shard_map/ppermute | solution.py:17
  324.5 155.8 %all-reduce.10.cloned.1.call-start = ((), (), s32[]{:S(2)}) async-start(), calls=%async_computation.5 | async-start | bytes 131072 | tf_op jit(solution)/shard_map/psum | solution.py:39
  426.9 262.0 %all-reduce.12.cloned.1.call-start = ((), (), s32[]{:S(2)}) async-start(), calls=%async_computation.6 | async-start | bytes 131072 | tf_op jit(solution)/shard_map/psum | solution.py:39
  486.5 18.9 %collective-permute-start.23 = (f32[8,66,1]{2,1,0:T(8,128)S(1)}, f32[8,66,1]{2,1,0:T(8,128)S(1)}, u32[]{:S(2)}, u32[]{:S(2)}) collective-permute-start(f32[8,66,1]{2,1,0:T(8,128)S(1)} %get-tuple-element.9), channel_id=1, source_target_pairs={{0,4},{4,8},{8,12},{12,16},{16,20},{20,24},{24,28},{28,32},{32,36}... | collective-permute-start | bytes 6344 | tf_op jit(solution)/shard_map/ppermute | solution.py:16
  491.5 31.2 %collective-permute-start.22 = (f32[8,66,1]{2,1,0:T(8,128)S(1)}, f32[8,66,1]{2,1,0:T(8,128)S(1)}, u32[]{:S(2)}, u32[]{:S(2)}) collective-permute-start(f32[8,66,1]{2,1,0:T(8,128)S(1)} %get-tuple-element.8), channel_id=1, source_target_pairs={{4,0},{8,4},{12,8},{16,12},{20,16},{24,20},{28,24},{32,28},{36,32}... | collective-permute-start | bytes 6344 | tf_op jit(solution)/shard_map/ppermute | solution.py:17
  526.8 28.0 %collective-permute-start.27 = (f32[8,66,1]{2,1,0:T(8,128)S(1)}, f32[8,66,1]{2,1,0:T(8,128)S(1)}, u32[]{:S(2)}, u32[]{:S(2)}) collective-permute-start(f32[8,66,1]{2,1,0:T(8,128)S(1)} %get-tuple-element.7), channel_id=1, source_target_pairs={{0,4},{4,8},{8,12},{12,16},{16,20},{20,24},{24,28},{28,32},{32,36}... | collective-permute-start | bytes 6344 | tf_op jit(solution)/shard_map/ppermute | solution.py:16
  530.1 30.3 %collective-permute-start.26 = (f32[8,66,1]{2,1,0:T(8,128)S(1)}, f32[8,66,1]{2,1,0:T(8,128)S(1)}, u32[]{:S(2)}, u32[]{:S(2)}) collective-permute-start(f32[8,66,1]{2,1,0:T(8,128)S(1)} %get-tuple-element.6), channel_id=1, source_target_pairs={{4,0},{8,4},{12,8},{16,12},{20,16},{24,20},{28,24},{32,28},{36,32}... | collective-permute-start | bytes 6344 | tf_op jit(solution)/shard_map/ppermute | solution.py:17
  564.4 28.5 %collective-permute-start.31 = (f32[8,66,1]{2,1,0:T(8,128)S(1)}, f32[8,66,1]{2,1,0:T(8,128)S(1)}, u32[]{:S(2)}, u32[]{:S(2)}) collective-permute-start(f32[8,66,1]{2,1,0:T(8,128)S(1)} %get-tuple-element.5), channel_id=1, source_target_pairs={{0,4},{4,8},{8,12},{12,16},{16,20},{20,24},{24,28},{28,32},{32,36}... | collective-permute-start | bytes 6344 | tf_op jit(solution)/shard_map/ppermute | solution.py:16
  567.5 28.4 %collective-permute-start.30 = (f32[8,66,1]{2,1,0:T(8,128)S(1)}, f32[8,66,1]{2,1,0:T(8,128)S(1)}, u32[]{:S(2)}, u32[]{:S(2)}) collective-permute-start(f32[8,66,1]{2,1,0:T(8,128)S(1)} %get-tuple-element.4), channel_id=1, source_target_pairs={{4,0},{8,4},{12,8},{16,12},{20,16},{24,20},{28,24},{32,28},{36,32}... | collective-permute-start | bytes 6344 | tf_op jit(solution)/shard_map/ppermute | solution.py:17
  599.9 17.5 %collective-permute-start.35 = (f32[8,66,1]{2,1,0:T(8,128)S(1)}, f32[8,66,1]{2,1,0:T(8,128)S(1)}, u32[]{:S(2)}, u32[]{:S(2)}) collective-permute-start(f32[8,66,1]{2,1,0:T(8,128)S(1)} %get-tuple-element.3), channel_id=1, source_target_pairs={{0,4},{4,8},{8,12},{12,16},{16,20},{20,24},{24,28},{28,32},{32,36}... | collective-permute-start | bytes 6344 | tf_op jit(solution)/shard_map/ppermute | solution.py:16
  606.3 28.6 %collective-permute-start.34 = (f32[8,66,1]{2,1,0:T(8,128)S(1)}, f32[8,66,1]{2,1,0:T(8,128)S(1)}, u32[]{:S(2)}, u32[]{:S(2)}) collective-permute-start(f32[8,66,1]{2,1,0:T(8,128)S(1)} %get-tuple-element.2), channel_id=1, source_target_pairs={{4,0},{8,4},{12,8},{16,12},{20,16},{24,20},{28,24},{32,28},{36,32}... | collective-permute-start | bytes 6344 | tf_op jit(solution)/shard_map/ppermute | solution.py:17
  713.6 30.4 %all-to-all-start.2 = ((f32[1,128,32]{2,0,1:T(1,128)}), f32[1,128,32]{2,0,1:T(1,128)S(1)}, u32[]{:S(2)}, u32[]{:S(2)}) async-start(f32[1,128,32]{2,0,1:T(1,128)} %bitcast.18), calls=%async_computation.2 | async-start | bytes 131072 | tf_op jit(solution)/shard_map/all_to_all | solution.py:98
  (31 other events, 473.4 us)
Sparse Core Ops, SparseCore 0:
  123.7 44.8 all-reduce.5
  324.6 52.5 all-reduce.7
  427.0 53.1 all-reduce.9
  636.3 52.5 all-reduce.11
where the time goes:
time: 774 us; the launch traced here: 772 us
  waiting for transfers between devices  427 us (55%)
  starting transfers between devices  174 us (22%)
  local copies, waits for them, and re-layouts  90.3 us (12%)
  other arithmetic  66.7 us (9%)
  between operations  14.5 us (2%)
    psum x4, waiting for transfers between devices, member_total(): return lax.psum(partial_value, 'mem')  204 us
    ppermute x18, waiting for transfers between devices, extended(): after = lax.ppermute(first, axis, down)  98.2 us
    ppermute x18, waiting for transfers between devices, extended(): before = lax.ppermute(last, axis, up)  97.9 us
    ppermute x18, starting transfers between devices, extended(): after = lax.ppermute(first, axis, down)  73.8 us
    ppermute x18, starting transfers between devices, extended(): before = lax.ppermute(last, axis, up)  48.4 us
    scatter-add x1, other arithmetic, per_device(): jax.ops.segment_sum(got_weight * got_depart, got_cell, num_segments=tile_...  25 us
    scatter-add x1, other arithmetic, per_device(): jax.ops.segment_sum(got_weight * at_obs, got_cell, num_segments=tile_cells)  25 us
    gather x2, local copies, waits for them, and re-layouts, per_device(): answer = got_depart - increment.reshape(-1)[got_cell]  23.1 us
  transfers between devices with their start and end apart: 43, of which 35 were waited for; matrix products, arithmetic and copies ran while one was open for 2% of the time, Pallas kernels for 0%

commit v1 on v0

v1 whole, which is shorter than its diff:
```python
import jax
import jax.numpy as jnp
from jax import lax
from jax.experimental import pallas as pl
from jax.experimental.pallas import tpu as pltpu
from jax.sharding import PartitionSpec as P

STEPS = 4
SLOTS = 32
HALO = 2 * STEPS
LANES = 128
F32 = jnp.float32
BF16 = jnp.bfloat16
I32 = jnp.int32

WHOLE = pl.BlockSpec(memory_space=pltpu.VMEM)


def call(kernel, outs, scratch=(), limit=24 << 20):
    def run(*operands):
        return pl.pallas_call(
            kernel,
            out_shape=outs,
            in_specs=[WHOLE] * len(operands),
            out_specs=jax.tree.map(lambda _: WHOLE, outs),
            scratch_shapes=list(scratch),
            compiler_params=pltpu.CompilerParams(vmem_limit_bytes=limit),
        )(*operands)

    return run


def halves(value):
    high = value.astype(BF16).astype(F32)
    return high, value - high


def nt_dot(a, b):
    return lax.dot_general(a, b, (((1,), (1,)), ((), ())), preferred_element_type=F32)


def pack_kernel(owner_ref, cell_ref, depart_ref, weight_ref, out_ref, rank_ref):
    places = out_ref.shape[0]
    chunks = owner_ref.shape[0]
    dest_ids = lax.broadcasted_iota(I32, (places, LANES), 0)
    slot_ids = lax.broadcasted_iota(I32, (SLOTS, LANES), 0).astype(F32)
    source = lax.broadcasted_iota(I32, (LANES, 2 * LANES), 0)
    target = lax.broadcasted_iota(I32, (LANES, 2 * LANES), 1)
    counter = jnp.where(source <= target, 1.0, 0.0).astype(BF16)
    seen = jnp.full((places, LANES), -1.0, F32)
    packed = jnp.zeros((places, 6 * SLOTS), F32)
    for j in range(chunks):
        hit = dest_ids == owner_ref[j : j + 1, :]
        names = jnp.where(hit, 1.0, 0.0).astype(BF16)
        counts = jnp.dot(names, counter, preferred_element_type=F32)
        rank = jnp.sum(jnp.where(hit, counts[:, :LANES] + seen, 0.0), axis=0, keepdims=True)
        seen = seen + counts[:, LANES:]
        rank_ref[j : j + 1, :] = rank
        weight = weight_ref[j : j + 1, :]
        product_high, product_low = halves(weight * depart_ref[j : j + 1, :])
        weight_high, weight_low = halves(weight)
        cell = cell_ref[j : j + 1, :]
        row = (cell // 256).astype(F32)
        col = (cell % 256).astype(F32)
        chosen = slot_ids == rank
        fields = [
            jnp.where(chosen, field, 0.0)
            for field in (product_high, weight_high, row, col, product_low, weight_low)
        ]
        packed = packed + nt_dot(names, jnp.concatenate(fields, axis=0).astype(BF16))
    low = jnp.concatenate(
        [packed[:, 4 * SLOTS :], jnp.zeros((places, 2 * SLOTS), F32)], axis=1
    )
    out_ref[...] = packed[:, : 4 * SLOTS] + low


def scatter_kernel(got_ref, out_ref, turned_ref):
    rows, cols = 64, 256
    turned_ref[...] = got_ref[...].T
    width = turned_ref.shape[1]
    row_ids = lax.broadcasted_iota(I32, (rows, width), 0).astype(F32)
    col_ids = lax.broadcasted_iota(I32, (cols, width), 0).astype(F32)
    total = jnp.zeros((4 * rows, cols), F32)
    for s in range(0, SLOTS, 2):
        left, right = [], []
        for k in (s, s + 1):
            product_high, product_low = halves(turned_ref[k : k + 1, :])
            weight_high, weight_low = halves(turned_ref[SLOTS + k : SLOTS + k + 1, :])
            in_row = row_ids == turned_ref[2 * SLOTS + k : 2 * SLOTS + k + 1, :]
            in_col = col_ids == turned_ref[3 * SLOTS + k : 3 * SLOTS + k + 1, :]
            left.append(
                jnp.concatenate(
                    [
                        jnp.where(in_row, v, 0.0)
                        for v in (product_high, product_low, weight_high, weight_low)
                    ],
                    axis=0,
                ).astype(BF16)
            )
            right.append(jnp.where(in_col, 1.0, 0.0).astype(BF16))
        total = total + nt_dot(jnp.concatenate(left, axis=1), jnp.concatenate(right, axis=1))
    product = total[:rows] + total[rows : 2 * rows]
    weight = total[2 * rows : 3 * rows] + total[3 * rows :]
    quarters, width = out_ref.shape[0], out_ref.shape[2] // 2
    for q in range(quarters):
        out_ref[q, :, :width] = product[:, q * width : (q + 1) * width]
        out_ref[q, :, width:] = weight[:, q * width : (q + 1) * width]


def reduce_kernel(parts_ref, whole_ref, top_ref, bottom_ref):
    whole = parts_ref[0]
    for q in range(1, parts_ref.shape[0]):
        whole = whole + parts_ref[q]
    whole_ref[...] = whole
    top_ref[...] = whole[:HALO]
    bottom_ref[...] = whole[-HALO:]


def rim_kernel(north_ref, whole_ref, south_ref, out_ref):
    out_ref[:HALO] = north_ref[...]
    out_ref[HALO:-HALO] = whole_ref[...]
    out_ref[-HALO:] = south_ref[...]


def row_rim_kernel(members_ref, rate_ref, sea_ref, top_ref, bottom_ref):
    members, rows, _ = members_ref.shape
    for k in range(members):
        value = members_ref[k].astype(F32)
        top_ref[k] = value[:HALO]
        bottom_ref[k] = value[rows - HALO :]
    top_ref[members] = rate_ref[:HALO]
    bottom_ref[members] = rate_ref[rows - HALO :]
    top_ref[members + 1] = sea_ref[:HALO].astype(F32)
    bottom_ref[members + 1] = sea_ref[rows - HALO :].astype(F32)


def field_of(k, members_ref, rate_ref, sea_ref):
    members = members_ref.shape[0]
    if k < members:
        return members_ref[k].astype(F32)
    return rate_ref[...] if k == members else sea_ref[...].astype(F32)


def col_rim_kernel(members_ref, rate_ref, sea_ref, north_ref, south_ref, first_ref, last_ref):
    fields = members_ref.shape[0] + 2
    rows, cols = rate_ref.shape
    first_ref[...] = jnp.zeros(first_ref.shape, F32)
    last_ref[...] = jnp.zeros(last_ref.shape, F32)
    for k in range(fields):
        value = field_of(k, members_ref, rate_ref, sea_ref)
        at = slice(k * HALO, (k + 1) * HALO)
        for ref, cut in ((first_ref, slice(0, HALO)), (last_ref, slice(cols - HALO, cols))):
            ref[:HALO, at] = north_ref[k, :, cut]
            ref[HALO : HALO + rows, at] = value[:, cut]
            ref[HALO + rows :, at] = south_ref[k, :, cut]


def piece_kernel(
    members_ref, rate_ref, sea_ref, north_ref, south_ref, west_ref, east_ref,
    pieces_ref, coef_ref, wide_ref, kept_ref,
):
    members = members_ref.shape[0]
    rows, cols = rate_ref.shape
    quarters = pieces_ref.shape[0]
    width = cols // quarters
    span = width + 2 * HALO
    for k in range(members + 2):
        value = field_of(k, members_ref, rate_ref, sea_ref)
        at = slice(k * HALO, (k + 1) * HALO)
        wide_ref[:, :HALO] = west_ref[:, at]
        wide_ref[:HALO, HALO : HALO + cols] = north_ref[k]
        wide_ref[HALO : HALO + rows, HALO : HALO + cols] = value
        wide_ref[HALO + rows :, HALO : HALO + cols] = south_ref[k]
        wide_ref[:, HALO + cols : 2 * HALO + cols] = east_ref[:, at]
        for q in range(quarters):
            piece = wide_ref[:, q * width : q * width + span]
            if k < members:
                pieces_ref[q, :, k * span : (k + 1) * span] = piece
            else:
                kept_ref[q, k - members, :, :span] = piece
    mine = lax.axis_index("mem")
    lat, last = lax.axis_index("lat"), lax.axis_size("lat") - 1
    coef_ref[0] = kept_ref[mine, 0]
    row_ids = lax.broadcasted_iota(I32, (rows + 2 * HALO, coef_ref.shape[2]), 0)
    outside = ((row_ids < HALO) & (lat == 0)) | ((row_ids >= HALO + rows) & (lat == last))
    coef_ref[1] = jnp.where(outside, 0.0, kept_ref[mine, 1])


def product_kernel(
    own_ref, west_ref, east_ref, members_ref, coef_ref, out_ref,
    state_ref, weights_ref, tiled_ref, field_ref,
):
    groups, height, lanes = members_ref.shape
    width = own_ref.shape[1] // 2
    span = width + 2 * HALO
    windows = lanes // span
    divisor = groups * windows - 1
    pad = 8

    def tile_lanes(value):
        for k in range(windows):
            tiled_ref[:, k * span : (k + 1) * span] = value
        return tiled_ref[...]

    for f in range(2):
        low = f * width
        field_ref[f, :, :HALO] = west_ref[:, low + width - HALO : low + width]
        field_ref[f, :, HALO : HALO + width] = own_ref[:, low : low + width]
        field_ref[f, :, HALO + width : span] = east_ref[:, low : low + HALO]
    innovation = field_ref[0, :, :span]
    weight_sum = field_ref[1, :, :span]
    sea_cover = coef_ref[1, :, :span]

    rate = tile_lanes(coef_ref[0, :, :span])
    sea = tile_lanes(sea_cover)
    north = 0.5 * (rate + pltpu.roll(rate, height - 1, 0)) * sea * pltpu.roll(sea, height - 1, 0)
    east = 0.5 * (rate + pltpu.roll(rate, lanes - 1, 1)) * sea * pltpu.roll(sea, lanes - 1, 1)
    south = pltpu.roll(north, 1, 0)
    west = pltpu.roll(east, 1, 1)
    weights_ref[0] = 1.0 - (north + south + east + west)
    weights_ref[1] = north
    weights_ref[2] = south
    weights_ref[3] = east
    weights_ref[4] = west
    state_ref[...] = jnp.zeros(state_ref.shape, F32)

    def sweep(source, target):
        for r in range(0, height, 8):
            centre_w, north_w, south_w, east_w, west_w = (
                weights_ref[i, r : r + 8, :] for i in range(5)
            )
            for g in range(groups):
                centre = state_ref[source, g, pad + r : pad + r + 8, :]
                above = state_ref[source, g, pad + r + 1 : pad + r + 9, :]
                below = state_ref[source, g, pad + r - 1 : pad + r + 7, :]
                state_ref[target, g, pad + r : pad + r + 8, :] = (
                    centre_w * centre
                    + (north_w * above + south_w * below)
                    + (east_w * pltpu.roll(centre, lanes - 1, 1) + west_w * pltpu.roll(centre, 1, 1))
                )

    def covariance(source):
        tiled = tile_lanes(source)
        for g in range(groups):
            state_ref[0, g, pad : pad + height, :] = members_ref[g] * tiled

        def pair(_, carry):
            sweep(0, 1)
            sweep(1, 0)
            return carry

        lax.fori_loop(0, STEPS // 2, pair, 0)
        total = members_ref[0] * state_ref[0, 0, pad : pad + height, :]
        for g in range(1, groups):
            total = total + members_ref[g] * state_ref[0, g, pad : pad + height, :]
        tiled_ref[...] = total
        summed = tiled_ref[:, :span]
        for k in range(1, windows):
            summed = summed + tiled_ref[:, k * span : (k + 1) * span]
        return sea_cover * summed / divisor

    first_pass = covariance(innovation)
    increment = covariance(innovation - weight_sum * first_pass)
    field_ref[0, :, :span] = increment
    half = (height - 2 * HALO) // 2
    for q in range(out_ref.shape[0]):
        out_ref[q, :, :width] = field_ref[0, HALO : HALO + half, HALO : HALO + width]
        out_ref[q, :, width:] = field_ref[0, HALO + half : HALO + 2 * half, HALO : HALO + width]


def answer_kernel(pieces_ref, turned_ref, tile_ref, out_ref, reply_ref):
    quarters, half, width = pieces_ref.shape[0], pieces_ref.shape[1], pieces_ref.shape[2] // 2
    rows, cols = tile_ref.shape
    for q in range(quarters):
        tile_ref[:half, q * width : (q + 1) * width] = pieces_ref[q, :, :width]
        tile_ref[half:, q * width : (q + 1) * width] = pieces_ref[q, :, width:]
    high, low = halves(tile_ref[...])
    both = jnp.concatenate([high, low], axis=0).astype(BF16)
    lanes = turned_ref.shape[1]
    row_ids = lax.broadcasted_iota(I32, (rows, lanes), 0).astype(F32)
    col_ids = lax.broadcasted_iota(I32, (cols, lanes), 0).astype(F32)
    reply_ref[...] = jnp.zeros(reply_ref.shape, F32)
    for k in range(SLOTS):
        in_row = row_ids == turned_ref[2 * SLOTS + k : 2 * SLOTS + k + 1, :]
        in_col = col_ids == turned_ref[3 * SLOTS + k : 3 * SLOTS + k + 1, :]
        picked = jnp.dot(both, jnp.where(in_col, 1.0, 0.0).astype(BF16), preferred_element_type=F32)
        picked = picked[:rows] + picked[rows:]
        reply_ref[k : k + 1, :] = jnp.sum(jnp.where(in_row, picked, 0.0), axis=0, keepdims=True)
    out_ref[...] = reply_ref[...].T[:, :SLOTS]


def residual_kernel(owner_ref, rank_ref, depart_ref, got_ref, out_ref, wide_ref):
    places = got_ref.shape[0]
    chunks = owner_ref.shape[0]
    wide_ref[...] = jnp.zeros(wide_ref.shape, F32)
    wide_ref[:places, :SLOTS] = got_ref[...]
    turned = wide_ref[...].T[:SLOTS, :]
    high, low = halves(turned)
    both = jnp.concatenate([high, low], axis=0).astype(BF16)
    dest_ids = lax.broadcasted_iota(I32, (wide_ref.shape[0], LANES), 0)
    slot_ids = lax.broadcasted_iota(I32, (SLOTS, LANES), 0).astype(F32)
    for j in range(chunks):
        names = jnp.where(dest_ids == owner_ref[j : j + 1, :], 1.0, 0.0).astype(BF16)
        picked = jnp.dot(both, names, preferred_element_type=F32)
        picked = picked[:SLOTS] + picked[SLOTS:]
        value = jnp.sum(
            jnp.where(slot_ids == rank_ref[j : j + 1, :], picked, 0.0), axis=0, keepdims=True
        )
        out_ref[j : j + 1, :] = depart_ref[j : j + 1, :] - value


def shape(*dims, dtype=F32):
    return jax.ShapeDtypeStruct(dims, dtype)


def neighbours(axes):
    size = 1
    for axis in axes:
        size *= lax.axis_size(axis)
    up = [(i, (i + 1) % size) for i in range(size)]
    return up, [(j, i) for i, j in up]


def exchange(first, last, axes):
    up, down = neighbours(axes)
    return lax.ppermute(last, axes, up), lax.ppermute(first, axes, down)


def per_device(perturbations, diffusivity, sea_mask, obs_owner, obs_cell, obs_depart, obs_weight):
    members, rows, cols = perturbations.shape
    quarters = lax.axis_size("mem")
    places = lax.axis_size("lat") * lax.axis_size("lon")
    width = cols // quarters
    span = width + 2 * HALO
    height = rows + 2 * HALO
    chunks = obs_cell.shape[0] // LANES
    owner, cell, depart, weight = (
        a.reshape(chunks, LANES) for a in (obs_owner, obs_cell, obs_depart, obs_weight)
    )
    tiles = ("lat", "lon")

    top, bottom = call(
        row_rim_kernel, (shape(members + 2, HALO, cols), shape(members + 2, HALO, cols))
    )(perturbations, diffusivity, sea_mask)
    north, south = exchange(top, bottom, ("lat",))
    outgoing, rank = call(pack_kernel, (shape(places, LANES), shape(chunks, LANES)))(
        owner, cell, depart, weight
    )
    got = lax.all_to_all(outgoing, tiles, split_axis=0, concat_axis=0, tiled=True)

    first, last = call(col_rim_kernel, (shape(height, LANES), shape(height, LANES)))(
        perturbations, diffusivity, sea_mask, north, south
    )
    west, east = exchange(first, last, ("lon",))
    pieces, coef = call(
        piece_kernel,
        (shape(quarters, height, members * span), shape(2, height, LANES)),
        [pltpu.VMEM((height, cols + LANES), F32), pltpu.VMEM((quarters, 2, height, LANES), F32)],
    )(perturbations, diffusivity, sea_mask, north, south, west, east)
    all_members = lax.all_to_all(pieces, "mem", split_axis=0, concat_axis=0, tiled=True)

    parts, turned = call(
        scatter_kernel, (shape(quarters, rows, 2 * width), shape(LANES, places))
    )(got)
    parts = lax.all_to_all(parts, "mem", split_axis=0, concat_axis=0, tiled=True)
    whole, top, bottom = call(
        reduce_kernel,
        (shape(rows, 2 * width), shape(HALO, 2 * width), shape(HALO, 2 * width)),
    )(parts)
    north, south = exchange(top, bottom, ("lat",))
    own = call(rim_kernel, shape(height, 2 * width))(north, whole, south)
    west, east = exchange(own, own, ("lon", "mem"))
    lanes = members * span
    quarter = call(
        product_kernel,
        shape(quarters, rows // 2, 2 * width),
        [
            pltpu.VMEM((2, quarters, height + 16, lanes), F32),
            pltpu.VMEM((5, height, lanes), F32),
            pltpu.VMEM((height, lanes), F32),
            pltpu.VMEM((2, height, LANES), F32),
        ],
    )(own, west, east, all_members, coef)
    quarter = lax.all_to_all(quarter, "mem", split_axis=0, concat_axis=0, tiled=True)
    increment, answers = call(
        answer_kernel, (shape(rows, cols), shape(places, SLOTS)), [pltpu.VMEM((LANES, places), F32)]
    )(quarter, turned)
    returned = lax.all_to_all(answers, tiles, split_axis=0, concat_axis=0, tiled=True)
    residual = call(
        residual_kernel, shape(chunks, LANES), [pltpu.VMEM((max(LANES, places), LANES), F32)]
    )(owner, rank, depart, returned)
    return increment, residual.reshape(chunks * LANES)


def solution(mesh):
    return jax.shard_map(
        per_device,
        mesh=mesh,
        in_specs=(
            P("mem", "lat", "lon"),
            P("lat", "lon"),
            P("lat", "lon"),
            P(("lat", "lon", "mem"), None),
            P(("lat", "lon", "mem")),
            P(("lat", "lon", "mem")),
            P(("lat", "lon", "mem")),
        ),
        out_specs=(P("lat", "lon"), P(("lat", "lon", "mem"))),
        check_vma=False,
    )
```

time: 774 us -> 135 us (0.17)
  waiting for transfers between devices: 427 us -> 13.4 us
  starting transfers between devices: 174 us -> 36.6 us
  local copies, waits for them, and re-layouts: 90.3 us -> 2.84 us
  blocking collectives: 0 us -> 67.9 us
  other arithmetic: 66.7 us -> 0 us
  between operations: 14.5 us -> 0.75 us
  Pallas kernels: 0 us -> 12.9 us
    psum x4 -> x0, waiting for transfers between devices: 204 us -> none  [member_total(): return lax.psum(partial_value, 'mem')]
    ppermute x36 -> x8, waiting for transfers between devices: 196 us -> 13.4 us  [exchange(): return (lax.ppermute(last, axes, up), lax.ppermute(first, axes, down))]
    ppermute x36 -> x8, starting transfers between devices: 122 us -> 26.9 us  [exchange(): return (lax.ppermute(last, axes, up), lax.ppermute(first, axes, down))]
    all_to_all x0 -> x3, blocking collectives: none -> 67.9 us  [the longest x1 35 us: per_device(): lax.all_to_all(outgoing, tiles, split_axis=0, concat_axis=0, tiled=True)]
    gather x4 -> x0, local copies, waits for them, and re-layouts: 66.7 us -> none  [the longest x2 23.1 us: per_device(): answer = got_depart - increment.reshape(-1)[got_cell]]
    scatter-add x2 -> x0, other arithmetic: 50 us -> none  [the longest x1 25 us: per_device(): jax.ops.segment_sum(got_weight * got_depart, got_cell, num_segments=tile_...]
    all_to_all x3 -> x2, starting transfers between devices: 51.5 us -> 9.67 us  [the longest x1 5.26 us: per_device(): lax.all_to_all(pieces, 'mem', split_axis=0, concat_axis=0, tiled=True)]
    all_to_all x3 -> x2, waiting for transfers between devices: 27.5 us -> 0.01 us  [the longest x1 0.01 us: per_device(): lax.all_to_all(parts, 'mem', split_axis=0, concat_axis=0, tiled=True)]
  transfers between devices with their start and end apart: 43 -> 10, of which waited for: 35 -> 6; matrix products, arithmetic and copies ran while one was open for 2% -> 0% of each run, Pallas kernels for 0% -> 2%
where the time goes in v1:
time: 135 us; the launch traced here: 134 us
  blocking collectives  67.9 us (50%)
  starting transfers between devices  36.6 us (27%)
  waiting for transfers between devices  13.4 us (10%)
  Pallas kernels  12.9 us (10%)
  local copies, waits for them, and re-layouts  2.84 us (2%)
    all_to_all x1, blocking collectives, per_device(): lax.all_to_all(outgoing, tiles, split_axis=0, concat_axis=0, tiled=True)  35 us
    ppermute x8, starting transfers between devices, exchange(): return (lax.ppermute(last, axes, up), lax.ppermute(first, axes, down))  26.9 us
    all_to_all x1, blocking collectives, per_device(): lax.all_to_all(answers, tiles, split_axis=0, concat_axis=0, tiled=True)  25.9 us
    ppermute x8, waiting for transfers between devices, exchange(): return (lax.ppermute(last, axes, up), lax.ppermute(first, axes, down))  13.4 us
    pallas_call x10, Pallas kernels, run(): pl.pallas_call(kernel, out_shape=outs, in_specs=[WHOLE] * len(operands),...  12.9 us
    all_to_all x1, blocking collectives, per_device(): lax.all_to_all(quarter, 'mem', split_axis=0, concat_axis=0, tiled=True)  6.96 us
    all_to_all x1, starting transfers between devices, per_device(): lax.all_to_all(pieces, 'mem', split_axis=0, concat_axis=0, tiled=True)  5.26 us
    all_to_all x1, starting transfers between devices, per_device(): lax.all_to_all(parts, 'mem', split_axis=0, concat_axis=0, tiled=True)  4.41 us
  transfers between devices with their start and end apart: 10, of which 6 were waited for; matrix products, arithmetic and copies ran while one was open for 0% of the time, Pallas kernels for 2%

profile of v1, /device:TPU:1, one launch (start us, length us, event | category | flops | bytes accessed | tf_op | source)
XLA Modules:
  0.0 134.3 jit_solution(16588181928904510014)
XLA Ops:
  0.7 0.7 copy-done.3
  3.5 1.6 %shard_map.86 = (f32[128,128]{1,0:T(8,128)S(1)}, f32[16,128]{1,0:T(8,128)S(1)}) custom-call(s32[16,128]{1,0:T(8,128)S(1)} %bitcast.17, s32[16,128]{1,0:T(8,128)S(1)} %bitcast.21, f32[16,128]{1,0:T(8,128)S(1)} %bitcast.19, f32[16,128]{1,0:T(8,128)S(1)} %bitcast.22), custom_call_target="tpu_custom_call" | custom-call | tf_op jit(solution)/shard_map/pallas_call | solution.py:21
  5.0 35.0 %all_to_all.37 = f32[128,1,128]{2,1,0:T(1,128)S(1)} all-to-all(f32[128,1,128]{2,1,0:T(1,128)S(1)} %bitcast.16), channel_id=1, replica_groups=mesh['lat'=8,'lon'=16,'mem'=4] {'lat','lon'}, dimensions={0} | all-to-all | bytes 131072 | tf_op jit(solution)/shard_map/all_to_all | solution.py:349
  40.1 1.6 %shard_map.87 = (f32[4,64,128]{2,1,0:T(8,128)}, f32[128,128]{1,0:T(8,128)S(1)}) custom-call(f32[128,128]{1,0:T(8,128)S(1)} %bitcast.13), custom_call_target="tpu_custom_call" | custom-call | tf_op jit(solution)/shard_map/pallas_call | solution.py:21
  41.7 4.4 %all-to-all-start.1 = ((f32[4,64,128]{2,1,0:T(8,128)}), f32[4,64,128]{2,1,0:T(8,128)S(1)}, u32[]{:S(2)}, u32[]{:S(2)}) async-start(f32[4,64,128]{2,1,0:T(8,128)} %get-tuple-element.18), calls=%async_computation.1 | async-start | bytes 262144 | tf_op jit(solution)/shard_map/all_to_all | solution.py:365
  46.1 0.8 collective-permute-start.4
  46.9 1.5 %collective-permute-done.4.north_ref = f32[10,8,256]{2,1,0:T(8,128)S(1)} collective-permute-done((f32[10,8,256]{2,1,0:T(8,128)S(1)}, f32[10,8,256]{2,1,0:T(8,128)S(1)}, u32[]{:S(2)}, u32[]{:S(2)}) %collective-permute-start.4) | collective-permute-done | bytes 81952 | tf_op jit(solution)/shard_map/ppermute | solution.py:326
  48.4 2.7 %collective-permute-done.5.south_ref = f32[10,8,256]{2,1,0:T(8,128)S(1)} collective-permute-done((f32[10,8,256]{2,1,0:T(8,128)S(1)}, f32[10,8,256]{2,1,0:T(8,128)S(1)}, u32[]{:S(2)}, u32[]{:S(2)}) %collective-permute-start.5) | collective-permute-done | bytes 81952 | tf_op jit(solution)/shard_map/ppermute | solution.py:326
  51.3 2.5 %collective-permute-start.6 = (f32[80,128]{1,0:T(8,128)S(1)}, f32[80,128]{1,0:T(8,128)S(1)}, u32[]{:S(2)}, u32[]{:S(2)}) collective-permute-start(f32[80,128]{1,0:T(8,128)S(1)} %get-tuple-element.24), channel_id=1, source_target_pairs={{0,4},{4,8},{8,12},{12,16},{16,20},{20,24},{24,28},{28,32},{32,36}... | collective-permute-start | bytes 122888 | tf_op jit(solution)/shard_map/ppermute | solution.py:326
  53.8 8.8 %collective-permute-start.7 = (f32[80,128]{1,0:T(8,128)S(1)}, f32[80,128]{1,0:T(8,128)S(1)}, u32[]{:S(2)}, u32[]{:S(2)}) collective-permute-start(f32[80,128]{1,0:T(8,128)S(1)} %get-tuple-element.25), channel_id=1, source_target_pairs={{4,0},{8,4},{12,8},{16,12},{20,16},{24,20},{28,24},{32,28},{36,32}... | collective-permute-start | bytes 122888 | tf_op jit(solution)/shard_map/ppermute | solution.py:326
  62.6 1.1 collective-permute-done.7.east_ref
  63.7 2.2 %shard_map.92 = (f32[4,80,640]{2,1,0:T(8,128)}, f32[2,80,128]{2,1,0:T(8,128)S(1)}) custom-call(bf16[8,64,256]{2,1,0:T(8,128)(2,1)S(1)} %copy-done, f32[64,256]{1,0:T(8,128)S(1)} %copy-done.1, s32[64,256]{1,0:T(8,128)S(1)} %copy-done.2, f32[10,8,256]{2,1,0:T(8,128)S(1)} %collective-permute-done.4.north_ref, ...), custom_call_target="tpu_custom_call" | custom-call | tf_op jit(solution)/shard_map/pallas_call | solution.py:21
  65.9 5.3 %all-to-all-start.2 = ((f32[4,80,640]{2,1,0:T(8,128)}), f32[4,80,640]{2,1,0:T(8,128)S(1)}, u32[]{:S(2)}, u32[]{:S(2)}) async-start(f32[4,80,640]{2,1,0:T(8,128)} %get-tuple-element.26), calls=%async_computation.2 | async-start | bytes 1638400 | tf_op jit(solution)/shard_map/all_to_all | solution.py:360
  71.1 0.8 collective-permute-start
  72.0 1.0 collective-permute-start.1
  73.7 1.4 %collective-permute-done.1.south_ref = f32[8,128]{1,0:T(8,128)S(1)} collective-permute-done((f32[8,128]{1,0:T(8,128)S(1)}, f32[8,128]{1,0:T(8,128)S(1)}, u32[]{:S(2)}, u32[]{:S(2)}) %collective-permute-start.1) | collective-permute-done | bytes 4128 | tf_op jit(solution)/shard_map/ppermute | solution.py:326
  75.0 11.0 %collective-permute-start.3 = (f32[80,128]{1,0:T(8,128)S(1)}, f32[80,128]{1,0:T(8,128)S(1)}, u32[]{:S(2)}, u32[]{:S(2)}) collective-permute-start(f32[80,128]{1,0:T(8,128)S(1)} %shard_map.89.own_ref), channel_id=1, source_target_pairs={{1,0},{2,1},{3,2},{4,3},{5,4},{6,5},{7,6},{8,7},{9,8},{10,9},{11,1... | collective-permute-start | bytes 122888 | tf_op jit(solution)/shard_map/ppermute | solution.py:326
  86.0 1.9 %collective-permute-start.2 = (f32[80,128]{1,0:T(8,128)S(1)}, f32[80,128]{1,0:T(8,128)S(1)}, u32[]{:S(2)}, u32[]{:S(2)}) collective-permute-start(f32[80,128]{1,0:T(8,128)S(1)} %shard_map.89.own_ref), channel_id=1, source_target_pairs={{0,1},{1,2},{2,3},{3,4},{4,5},{5,6},{6,7},{7,8},{8,9},{9,10},{10,1... | collective-permute-start | bytes 122888 | tf_op jit(solution)/shard_map/ppermute | solution.py:326
  87.9 6.1 %collective-permute-done.2.west_ref = f32[80,128]{1,0:T(8,128)S(1)} collective-permute-done((f32[80,128]{1,0:T(8,128)S(1)}, f32[80,128]{1,0:T(8,128)S(1)}, u32[]{:S(2)}, u32[]{:S(2)}) %collective-permute-start.2) | collective-permute-done | bytes 40992 | tf_op jit(solution)/shard_map/ppermute | solution.py:326
  94.1 5.0 %shard_map.93 = f32[4,32,128]{2,1,0:T(8,128)S(1)} custom-call(f32[80,128]{1,0:T(8,128)S(1)} %shard_map.89.own_ref, f32[80,128]{1,0:T(8,128)S(1)} %collective-permute-done.2.west_ref, f32[80,128]{1,0:T(8,128)S(1)} %collective-permute-done.3.east_ref, f32[4,80,640]{2,1,0:T(8,128)S(1)} %all-to-all-done.2.members_ref, f32[2,80,128]{2,1,0:T(8,128)S(1)} %get-tuple-element.27.coef_ref), custom_call_target="tpu_custom_call" | custom-call | tf_op jit(solution)/shard_map/pallas_call | solution.py:21
  99.1 7.0 %all_to_all.38.pieces_ref = f32[4,32,128]{2,1,0:T(8,128)S(1)} all-to-all(f32[4,32,128]{2,1,0:T(8,128)S(1)} %shard_map.93), channel_id=1, replica_groups=mesh['lat'=8,'lon'=16,'mem'=4] {'mem'}, dimensions={0} | all-to-all | bytes 131072 | tf_op jit(solution)/shard_map/all_to_all | solution.py:384
  106.1 1.4 %shard_map.94 = (f32[64,256]{1,0:T(8,128)}, f32[128,32]{1,0:T(8,128)S(1)}) custom-call(f32[4,32,128]{2,1,0:T(8,128)S(1)} %all_to_all.38.pieces_ref, f32[128,128]{1,0:T(8,128)S(1)} %get-tuple-element.28.turned_ref), custom_call_target="tpu_custom_call" | custom-call | tf_op jit(solution)/shard_map/pallas_call | solution.py:21
  107.4 25.9 %all_to_all.39 = f32[128,1,32]{2,1,0:T(1,128)S(1)} all-to-all(f32[128,1,32]{2,1,0:T(1,128)S(1)} %bitcast.15), channel_id=1, replica_groups=mesh['lat'=8,'lon'=16,'mem'=4] {'lat','lon'}, dimensions={0} | all-to-all | bytes 32768 | tf_op jit(solution)/shard_map/all_to_all | solution.py:388
  133.4 1.0 shard_map.95
  (27 shorter events, 3.0 us)
Async XLA Ops:
  0.6 45.4 %copy-start = (bf16[8,64,256]{2,1,0:T(8,128)(2,1)S(1)}, bf16[8,64,256]{2,1,0:T(8,128)(2,1)}, u32[]{:S(2)}) copy-start(bf16[8,64,256]{2,1,0:T(8,128)(2,1)} %members_ref.5) | copy-start | bytes 786436
  0.6 0.7 copy-start.3
  1.4 0.7 copy-start.5
  2.1 0.7 copy-start.7
  2.8 0.7 copy-start.8
  41.6 4.4 %copy-start.1 = (f32[64,256]{1,0:T(8,128)S(1)}, f32[64,256]{1,0:T(8,128)}, u32[]{:S(2)}) copy-start(f32[64,256]{1,0:T(8,128)} %rate_ref.5) | copy-start | bytes 196612
  41.7 4.4 %copy-start.2 = (s32[64,256]{1,0:T(8,128)S(1)}, s32[64,256]{1,0:T(8,128)}, u32[]{:S(2)}) copy-start(s32[64,256]{1,0:T(8,128)} %sea_ref.5) | copy-start | bytes 196612
  41.7 24.2 %all-to-all-start.1 = ((f32[4,64,128]{2,1,0:T(8,128)}), f32[4,64,128]{2,1,0:T(8,128)S(1)}, u32[]{:S(2)}, u32[]{:S(2)}) async-start(f32[4,64,128]{2,1,0:T(8,128)} %get-tuple-element.18), calls=%async_computation.1 | async-start | bytes 262144 | tf_op jit(solution)/shard_map/all_to_all | solution.py:365
  46.1 2.3 %collective-permute-start.4 = (f32[10,8,256]{2,1,0:T(8,128)S(1)}, f32[10,8,256]{2,1,0:T(8,128)S(1)}, u32[]{:S(2)}, u32[]{:S(2)}) collective-permute-start(f32[10,8,256]{2,1,0:T(8,128)S(1)} %get-tuple-element.22), channel_id=1, source_target_pairs={{0,64},{64,128},{128,192},{192,256},{256,320},{320,384},{384,448},... | collective-permute-start | bytes 245768 | tf_op jit(solution)/shard_map/ppermute | solution.py:326
  46.9 4.2 %collective-permute-start.5 = (f32[10,8,256]{2,1,0:T(8,128)S(1)}, f32[10,8,256]{2,1,0:T(8,128)S(1)}, u32[]{:S(2)}, u32[]{:S(2)}) collective-permute-start(f32[10,8,256]{2,1,0:T(8,128)S(1)} %get-tuple-element.23), channel_id=1, source_target_pairs={{64,0},{128,64},{192,128},{256,192},{320,256},{384,320},{448,384},... | collective-permute-start | bytes 245768 | tf_op jit(solution)/shard_map/ppermute | solution.py:326
  51.3 11.3 %collective-permute-start.6 = (f32[80,128]{1,0:T(8,128)S(1)}, f32[80,128]{1,0:T(8,128)S(1)}, u32[]{:S(2)}, u32[]{:S(2)}) collective-permute-start(f32[80,128]{1,0:T(8,128)S(1)} %get-tuple-element.24), channel_id=1, source_target_pairs={{0,4},{4,8},{8,12},{12,16},{16,20},{20,24},{24,28},{28,32},{32,36}... | collective-permute-start | bytes 122888 | tf_op jit(solution)/shard_map/ppermute | solution.py:326
  53.8 9.9 %collective-permute-start.7 = (f32[80,128]{1,0:T(8,128)S(1)}, f32[80,128]{1,0:T(8,128)S(1)}, u32[]{:S(2)}, u32[]{:S(2)}) collective-permute-start(f32[80,128]{1,0:T(8,128)S(1)} %get-tuple-element.25), channel_id=1, source_target_pairs={{4,0},{8,4},{12,8},{16,12},{20,16},{24,20},{28,24},{32,28},{36,32}... | collective-permute-start | bytes 122888 | tf_op jit(solution)/shard_map/ppermute | solution.py:326
  65.9 28.2 %all-to-all-start.2 = ((f32[4,80,640]{2,1,0:T(8,128)}), f32[4,80,640]{2,1,0:T(8,128)S(1)}, u32[]{:S(2)}, u32[]{:S(2)}) async-start(f32[4,80,640]{2,1,0:T(8,128)} %get-tuple-element.26), calls=%async_computation.2 | async-start | bytes 1638400 | tf_op jit(solution)/shard_map/all_to_all | solution.py:360
  71.1 2.5 %collective-permute-start = (f32[8,128]{1,0:T(8,128)S(1)}, f32[8,128]{1,0:T(8,128)S(1)}, u32[]{:S(2)}, u32[]{:S(2)}) collective-permute-start(f32[8,128]{1,0:T(8,128)S(1)} %get-tuple-element.19), channel_id=1, source_target_pairs={{0,64},{64,128},{128,192},{192,256},{256,320},{320,384},{384,448},... | collective-permute-start | bytes 12296 | tf_op jit(solution)/shard_map/ppermute | solution.py:326
  72.0 3.0 %collective-permute-start.1 = (f32[8,128]{1,0:T(8,128)S(1)}, f32[8,128]{1,0:T(8,128)S(1)}, u32[]{:S(2)}, u32[]{:S(2)}) collective-permute-start(f32[8,128]{1,0:T(8,128)S(1)} %get-tuple-element.21), channel_id=1, source_target_pairs={{64,0},{128,64},{192,128},{256,192},{320,256},{384,320},{448,384},... | collective-permute-start | bytes 12296 | tf_op jit(solution)/shard_map/ppermute | solution.py:326
  75.0 12.9 %collective-permute-start.3 = (f32[80,128]{1,0:T(8,128)S(1)}, f32[80,128]{1,0:T(8,128)S(1)}, u32[]{:S(2)}, u32[]{:S(2)}) collective-permute-start(f32[80,128]{1,0:T(8,128)S(1)} %shard_map.89.own_ref), channel_id=1, source_target_pairs={{1,0},{2,1},{3,2},{4,3},{5,4},{6,5},{7,6},{8,7},{9,8},{10,9},{11,1... | collective-permute-start | bytes 122888 | tf_op jit(solution)/shard_map/ppermute | solution.py:326
  86.0 8.1 %collective-permute-start.2 = (f32[80,128]{1,0:T(8,128)S(1)}, f32[80,128]{1,0:T(8,128)S(1)}, u32[]{:S(2)}, u32[]{:S(2)}) collective-permute-start(f32[80,128]{1,0:T(8,128)S(1)} %shard_map.89.own_ref), channel_id=1, source_target_pairs={{0,1},{1,2},{2,3},{3,4},{4,5},{5,6},{6,7},{7,8},{8,9},{9,10},{10,1... | collective-permute-start | bytes 122888 | tf_op jit(solution)/shard_map/ppermute | solution.py:326
  107.4 25.9 %copy-start.4 = (s32[2048,1]{0,1:T(1,128)S(1)}, s32[2048,1]{0,1:T(1,128)}, u32[]{:S(2)}) copy-start(s32[2048,1]{0,1:T(1,128)} %param.10) | copy-start | bytes 24580
  107.4 25.9 %copy-start.6 = (f32[2048]{0:T(1024)S(1)}, f32[2048]{0:T(1024)}, u32[]{:S(2)}) copy-start(f32[2048]{0:T(1024)} %param.12) | copy-start | bytes 24580

commit v2 on v1

--- a/solution.py
+++ b/solution.py
@@ -1,3 +1,5 @@
+import functools
+
 import jax
 import jax.numpy as jnp
 from jax import lax
@@ -14,14 +16,15 @@
 I32 = jnp.int32
 
 WHOLE = pl.BlockSpec(memory_space=pltpu.VMEM)
-
-
-def call(kernel, outs, scratch=(), limit=24 << 20):
+AWAY = pl.BlockSpec(memory_space=pl.ANY)
+
+
+def call(kernel, outs, scratch=(), limit=24 << 20, place=WHOLE):
     def run(*operands):
         return pl.pallas_call(
             kernel,
             out_shape=outs,
-            in_specs=[WHOLE] * len(operands),
+            in_specs=[place] * len(operands),
             out_specs=jax.tree.map(lambda _: WHOLE, outs),
             scratch_shapes=list(scratch),
             compiler_params=pltpu.CompilerParams(vmem_limit_bytes=limit),
@@ -39,7 +42,21 @@
     return lax.dot_general(a, b, (((1,), (1,)), ((), ())), preferred_element_type=F32)
 
 
-def pack_kernel(owner_ref, cell_ref, depart_ref, weight_ref, out_ref, rank_ref):
+def bring(away_refs, near_refs, sem_ref):
+    copies = [
+        pltpu.make_async_copy(away, near, sem_ref.at[i])
+        for i, (away, near) in enumerate(zip(away_refs, near_refs))
+    ]
+    for copy in copies:
+        copy.start()
+    for copy in copies:
+        copy.wait()
+
+
+def pack_kernel(*refs):
+    out_ref, rank_ref = refs[4:6]
+    owner_ref, cell_ref, depart_ref, weight_ref = refs[6:10]
+    bring(refs[:4], refs[6:10], refs[10])
     places = out_ref.shape[0]
     chunks = owner_ref.shape[0]
     dest_ids = lax.broadcasted_iota(I32, (places, LANES), 0)
@@ -107,91 +124,84 @@
         out_ref[q, :, width:] = weight[:, q * width : (q + 1) * width]
 
 
-def reduce_kernel(parts_ref, whole_ref, top_ref, bottom_ref):
-    whole = parts_ref[0]
-    for q in range(1, parts_ref.shape[0]):
-        whole = whole + parts_ref[q]
-    whole_ref[...] = whole
-    top_ref[...] = whole[:HALO]
-    bottom_ref[...] = whole[-HALO:]
-
-
-def rim_kernel(north_ref, whole_ref, south_ref, out_ref):
-    out_ref[:HALO] = north_ref[...]
-    out_ref[HALO:-HALO] = whole_ref[...]
-    out_ref[-HALO:] = south_ref[...]
-
-
-def row_rim_kernel(members_ref, rate_ref, sea_ref, top_ref, bottom_ref):
-    members, rows, _ = members_ref.shape
+def quarter_kernel(members_ref, own_ref, *rest):
+    sent_refs, kept_ref = rest[:-1], rest[-1]
+    members = members_ref.shape[0]
+    quarters = kept_ref.shape[0]
+    width = members_ref.shape[2] // quarters
     for k in range(members):
         value = members_ref[k].astype(F32)
-        top_ref[k] = value[:HALO]
-        bottom_ref[k] = value[rows - HALO :]
-    top_ref[members] = rate_ref[:HALO]
-    bottom_ref[members] = rate_ref[rows - HALO :]
-    top_ref[members + 1] = sea_ref[:HALO].astype(F32)
-    bottom_ref[members + 1] = sea_ref[rows - HALO :].astype(F32)
-
-
-def field_of(k, members_ref, rate_ref, sea_ref):
-    members = members_ref.shape[0]
-    if k < members:
-        return members_ref[k].astype(F32)
-    return rate_ref[...] if k == members else sea_ref[...].astype(F32)
-
-
-def col_rim_kernel(members_ref, rate_ref, sea_ref, north_ref, south_ref, first_ref, last_ref):
-    fields = members_ref.shape[0] + 2
-    rows, cols = rate_ref.shape
+        for q in range(quarters):
+            kept_ref[q, :, k * width : (k + 1) * width] = value[:, q * width : (q + 1) * width]
+    mine = lax.axis_index("mem")
+    own_ref[...] = kept_ref[mine]
+    for k, ref in enumerate(sent_refs):
+        ref[...] = kept_ref[(mine + k + 1) % quarters]
+
+
+def reduce_kernel(parts_ref, rate_ref, sea_ref, *rest):
+    quarters = parts_ref.shape[0]
+    piece_refs, (mid_ref, top_ref, bottom_ref, kept_ref) = rest[:quarters], rest[quarters:]
+    rows, lanes = piece_refs[0].shape
+    width = parts_ref.shape[2] // 2
+    mine = lax.axis_index("mem")
+    for k in range(quarters):
+        mid_ref[(mine - k + quarters) % quarters, :, :lanes] = piece_refs[k][...]
+    whole = parts_ref[0]
+    for q in range(1, quarters):
+        whole = whole + parts_ref[q]
+    mid_ref[0, :, lanes:] = whole
+    for q in range(quarters):
+        at = slice(q * width, (q + 1) * width)
+        kept_ref[q, :, :width] = rate_ref[:, at]
+        kept_ref[q, :, width:] = sea_ref[:, at].astype(F32)
+    mid_ref[1, :, lanes:] = kept_ref[mine]
+    for q in range(quarters):
+        size = lanes if q > 1 else lanes + 2 * width
+        top_ref[q, :, :size] = mid_ref[q, :HALO, :size]
+        bottom_ref[q, :, :size] = mid_ref[q, rows - HALO :, :size]
+        if size < top_ref.shape[2]:
+            top_ref[q, :, size:] = jnp.zeros((HALO, 2 * width), F32)
+            bottom_ref[q, :, size:] = jnp.zeros((HALO, 2 * width), F32)
+
+
+def fields_of(ref, width):
+    quarters, lanes = ref.shape[0], ref.shape[2] - 2 * width
+    places = [(q, k * width) for q in range(quarters) for k in range(lanes // width)]
+    return places + [(0, lanes), (0, lanes + width), (1, lanes), (1, lanes + width)]
+
+
+def outside_rows(rows):
+    lat = lax.axis_index("lat")
+    return lat == 0, lat == lax.axis_size("lat") - 1
+
+
+def rim_kernel(mid_ref, north_ref, south_ref, first_ref, last_ref, *, width):
+    rows = mid_ref.shape[1]
     first_ref[...] = jnp.zeros(first_ref.shape, F32)
     last_ref[...] = jnp.zeros(last_ref.shape, F32)
-    for k in range(fields):
-        value = field_of(k, members_ref, rate_ref, sea_ref)
+    places = fields_of(mid_ref, width)
+    no_north, no_south = outside_rows(rows)
+    for k, (q, lane) in enumerate(places):
         at = slice(k * HALO, (k + 1) * HALO)
-        for ref, cut in ((first_ref, slice(0, HALO)), (last_ref, slice(cols - HALO, cols))):
-            ref[:HALO, at] = north_ref[k, :, cut]
-            ref[HALO : HALO + rows, at] = value[:, cut]
-            ref[HALO + rows :, at] = south_ref[k, :, cut]
-
-
-def piece_kernel(
-    members_ref, rate_ref, sea_ref, north_ref, south_ref, west_ref, east_ref,
-    pieces_ref, coef_ref, wide_ref, kept_ref,
-):
-    members = members_ref.shape[0]
-    rows, cols = rate_ref.shape
-    quarters = pieces_ref.shape[0]
-    width = cols // quarters
-    span = width + 2 * HALO
-    for k in range(members + 2):
-        value = field_of(k, members_ref, rate_ref, sea_ref)
-        at = slice(k * HALO, (k + 1) * HALO)
-        wide_ref[:, :HALO] = west_ref[:, at]
-        wide_ref[:HALO, HALO : HALO + cols] = north_ref[k]
-        wide_ref[HALO : HALO + rows, HALO : HALO + cols] = value
-        wide_ref[HALO + rows :, HALO : HALO + cols] = south_ref[k]
-        wide_ref[:, HALO + cols : 2 * HALO + cols] = east_ref[:, at]
-        for q in range(quarters):
-            piece = wide_ref[:, q * width : q * width + span]
-            if k < members:
-                pieces_ref[q, :, k * span : (k + 1) * span] = piece
-            else:
-                kept_ref[q, k - members, :, :span] = piece
-    mine = lax.axis_index("mem")
-    lat, last = lax.axis_index("lat"), lax.axis_size("lat") - 1
-    coef_ref[0] = kept_ref[mine, 0]
-    row_ids = lax.broadcasted_iota(I32, (rows + 2 * HALO, coef_ref.shape[2]), 0)
-    outside = ((row_ids < HALO) & (lat == 0)) | ((row_ids >= HALO + rows) & (lat == last))
-    coef_ref[1] = jnp.where(outside, 0.0, kept_ref[mine, 1])
+        for ref, cut in ((first_ref, lane), (last_ref, lane + width - HALO)):
+            north = north_ref[q, :, cut : cut + HALO]
+            south = south_ref[q, :, cut : cut + HALO]
+            if k == len(places) - 1:
+                north = jnp.where(no_north, 0.0, north)
+                south = jnp.where(no_south, 0.0, south)
+            ref[:HALO, at] = north
+            ref[HALO : HALO + rows, at] = mid_ref[q, :, cut : cut + HALO]
+            ref[HALO + rows :, at] = south
 
 
 def product_kernel(
-    own_ref, west_ref, east_ref, members_ref, coef_ref, out_ref,
-    state_ref, weights_ref, tiled_ref, field_ref,
+    mid_ref, north_ref, south_ref, west_ref, east_ref, out_ref,
+    members_ref, state_ref, weights_ref, tiled_ref, field_ref,
 ):
     groups, height, lanes = members_ref.shape
-    width = own_ref.shape[1] // 2
+    rows = height - 2 * HALO
+    width = out_ref.shape[2] // 2
     span = width + 2 * HALO
     windows = lanes // span
     divisor = groups * windows - 1
@@ -202,16 +212,29 @@
             tiled_ref[:, k * span : (k + 1) * span] = value
         return tiled_ref[...]
 
-    for f in range(2):
-        low = f * width
-        field_ref[f, :, :HALO] = west_ref[:, low + width - HALO : low + width]
-        field_ref[f, :, HALO : HALO + width] = own_ref[:, low : low + width]
-        field_ref[f, :, HALO + width : span] = east_ref[:, low : low + HALO]
+    places = fields_of(mid_ref, width)
+    no_north, no_south = outside_rows(rows)
+    for k, (q, lane) in enumerate(places):
+        rim = slice(k * HALO, (k + 1) * HALO)
+        cut = slice(lane, lane + width)
+        north, south = north_ref[q, :, cut], south_ref[q, :, cut]
+        if k < groups * windows:
+            ref, low = members_ref.at[k // windows], k % windows * span
+        else:
+            ref, low = field_ref.at[k - groups * windows], 0
+        if k == len(places) - 1:
+            north = jnp.where(no_north, 0.0, north)
+            south = jnp.where(no_south, 0.0, south)
+        ref[:, low : low + HALO] = west_ref[:, rim]
+        ref[:HALO, low + HALO : low + HALO + width] = north
+        ref[HALO : HALO + rows, low + HALO : low + HALO + width] = mid_ref[q, :, cut]
+        ref[HALO + rows :, low + HALO : low + HALO + width] = south
+        ref[:, low + HALO + width : low + span] = east_ref[:, rim]
     innovation = field_ref[0, :, :span]
     weight_sum = field_ref[1, :, :span]
-    sea_cover = coef_ref[1, :, :span]
-
-    rate = tile_lanes(coef_ref[0, :, :span])
+    sea_cover = field_ref[3, :, :span]
+
+    rate = tile_lanes(field_ref[2, :, :span])
     sea = tile_lanes(sea_cover)
     north = 0.5 * (rate + pltpu.roll(rate, height - 1, 0)) * sea * pltpu.roll(sea, height - 1, 0)
     east = 0.5 * (rate + pltpu.roll(rate, lanes - 1, 1)) * sea * pltpu.roll(sea, lanes - 1, 1)
@@ -339,48 +362,52 @@
     )
     tiles = ("lat", "lon")
 
-    top, bottom = call(
-        row_rim_kernel, (shape(members + 2, HALO, cols), shape(members + 2, HALO, cols))
-    )(perturbations, diffusivity, sea_mask)
-    north, south = exchange(top, bottom, ("lat",))
-    outgoing, rank = call(pack_kernel, (shape(places, LANES), shape(chunks, LANES)))(
-        owner, cell, depart, weight
+    piece = shape(rows, members * width)
+    own, *sent = call(quarter_kernel, [piece] * quarters, [pltpu.VMEM((quarters, rows, members * width), F32)])(
+        perturbations
     )
+    ring = [
+        [(i, (i + k) % quarters) for i in range(quarters)] for k in range(1, quarters)
+    ]
+    outgoing, rank = call(
+        pack_kernel,
+        (shape(places, LANES), shape(chunks, LANES)),
+        [pltpu.VMEM((chunks, LANES), a.dtype) for a in (owner, cell, depart, weight)]
+        + [pltpu.SemaphoreType.DMA((4,))],
+        place=AWAY,
+    )(owner, cell, depart, weight)
     got = lax.all_to_all(outgoing, tiles, split_axis=0, concat_axis=0, tiled=True)
-
-    first, last = call(col_rim_kernel, (shape(height, LANES), shape(height, LANES)))(
-        perturbations, diffusivity, sea_mask, north, south
-    )
-    west, east = exchange(first, last, ("lon",))
-    pieces, coef = call(
-        piece_kernel,
-        (shape(quarters, height, members * span), shape(2, height, LANES)),
-        [pltpu.VMEM((height, cols + LANES), F32), pltpu.VMEM((quarters, 2, height, LANES), F32)],
-    )(perturbations, diffusivity, sea_mask, north, south, west, east)
-    all_members = lax.all_to_all(pieces, "mem", split_axis=0, concat_axis=0, tiled=True)
+    brought = [lax.ppermute(s, "mem", pairs) for s, pairs in zip(sent, ring)]
+    got, *brought = lax.optimization_barrier((got, *brought))
 
     parts, turned = call(
         scatter_kernel, (shape(quarters, rows, 2 * width), shape(LANES, places))
     )(got)
     parts = lax.all_to_all(parts, "mem", split_axis=0, concat_axis=0, tiled=True)
-    whole, top, bottom = call(
+    field_lanes = members * width + 2 * width
+    strip = shape(quarters, HALO, field_lanes)
+    mid, top, bottom = call(
         reduce_kernel,
-        (shape(rows, 2 * width), shape(HALO, 2 * width), shape(HALO, 2 * width)),
-    )(parts)
+        (shape(quarters, rows, field_lanes), strip, strip),
+        [pltpu.VMEM((quarters, rows, 2 * width), F32)],
+    )(parts, diffusivity, sea_mask, own, *brought)
     north, south = exchange(top, bottom, ("lat",))
-    own = call(rim_kernel, shape(height, 2 * width))(north, whole, south)
-    west, east = exchange(own, own, ("lon", "mem"))
+    rim_lanes = -(-(quarters * members + 4) * HALO // LANES) * LANES
+    rim = shape(height, rim_lanes)
+    first, last = call(functools.partial(rim_kernel, width=width), (rim, rim))(mid, north, south)
+    west, east = exchange(first, last, ("lon", "mem"))
     lanes = members * span
     quarter = call(
         product_kernel,
         shape(quarters, rows // 2, 2 * width),
         [
+            pltpu.VMEM((quarters, height, lanes), F32),
             pltpu.VMEM((2, quarters, height + 16, lanes), F32),
             pltpu.VMEM((5, height, lanes), F32),
             pltpu.VMEM((height, lanes), F32),
-            pltpu.VMEM((2, height, LANES), F32),
+            pltpu.VMEM((4, height, LANES), F32),
         ],
-    )(own, west, east, all_members, coef)
+    )(mid, north, south, west, east)
     quarter = lax.all_to_all(quarter, "mem", split_axis=0, concat_axis=0, tiled=True)
     increment, answers = call(
         answer_kernel, (shape(rows, cols), shape(places, SLOTS)), [pltpu.VMEM((LANES, places), F32)]

time: 135 us -> 120 us (0.89)
  starting transfers between devices: 36.6 us -> 23.5 us
  blocking collectives: 67.9 us -> 75.7 us
  waiting for transfers between devices: 13.4 us -> 6.01 us
  local copies, waits for them, and re-layouts: 2.84 us -> 0.97 us
    ppermute x8 -> x4, starting transfers between devices: 26.9 us -> 10.7 us  [exchange(): return (lax.ppermute(last, axes, up), lax.ppermute(first, axes, down))]
    ppermute x0 -> x3, starting transfers between devices: none -> 12.8 us  [per_device(): brought = [lax.ppermute(s, 'mem', pairs) for s, pairs in zip(sent, ring)]]
    all_to_all x2 -> x0, starting transfers between devices: 9.67 us -> none  [the longest x1 5.26 us: per_device(): lax.all_to_all(pieces, 'mem', split_axis=0, concat_axis=0, tiled=True)]
    ppermute x8 -> x4, waiting for transfers between devices: 13.4 us -> 6.01 us  [exchange(): return (lax.ppermute(last, axes, up), lax.ppermute(first, axes, down))]
    all_to_all x0 -> x1, blocking collectives: none -> 7.32 us  [per_device(): lax.all_to_all(parts, 'mem', split_axis=0, concat_axis=0, tiled=True)]
    all_to_all x1, blocking collectives: 25.9 us -> 28.2 us  [per_device(): lax.all_to_all(answers, tiles, split_axis=0, concat_axis=0, tiled=True)]
    unnamed x18 -> x14, local copies, waits for them, and re-layouts: 2.84 us -> 0.97 us
    all_to_all x1, blocking collectives: 35 us -> 33.2 us  [per_device(): lax.all_to_all(outgoing, tiles, split_axis=0, concat_axis=0, tiled=True)]
  transfers between devices with their start and end apart: 10 -> 7, of which waited for: 6 -> 4; matrix products, arithmetic and copies ran while one was open for 0% -> 0% of each run, Pallas kernels for 2% -> 1%
where the time goes in v2:
time: 120 us; the launch traced here: 119 us
  blocking collectives  75.7 us (63%)
  starting transfers between devices  23.5 us (20%)
  Pallas kernels  12.1 us (10%)
  waiting for transfers between devices  6.01 us (5%)
    all_to_all x1, blocking collectives, per_device(): lax.all_to_all(outgoing, tiles, split_axis=0, concat_axis=0, tiled=True)  33.2 us
    all_to_all x1, blocking collectives, per_device(): lax.all_to_all(answers, tiles, split_axis=0, concat_axis=0, tiled=True)  28.2 us
    ppermute x3, starting transfers between devices, per_device(): brought = [lax.ppermute(s, 'mem', pairs) for s, pairs in zip(sent, ring)]  12.8 us
    pallas_call x8, Pallas kernels, run(): pl.pallas_call(kernel, out_shape=outs, in_specs=[place] * len(operands),...  12.1 us
    ppermute x4, starting transfers between devices, exchange(): return (lax.ppermute(last, axes, up), lax.ppermute(first, axes, down))  10.7 us
    all_to_all x1, blocking collectives, per_device(): lax.all_to_all(parts, 'mem', split_axis=0, concat_axis=0, tiled=True)  7.32 us
    all_to_all x1, blocking collectives, per_device(): lax.all_to_all(quarter, 'mem', split_axis=0, concat_axis=0, tiled=True)  6.96 us
    ppermute x4, waiting for transfers between devices, exchange(): return (lax.ppermute(last, axes, up), lax.ppermute(first, axes, down))  6.01 us
  transfers between devices with their start and end apart: 7, of which 4 were waited for; matrix products, arithmetic and copies ran while one was open for 0% of the time, Pallas kernels for 1%

profile of v2, /device:TPU:1, one launch (start us, length us, event | category | flops | bytes accessed | tf_op | source)
XLA Modules:
  0.0 119.1 jit_solution(18152910121097755634)
XLA Ops:
  0.6 0.9 copy-done
  1.6 0.2 shard_map.87
  1.8 4.8 %collective-permute-start = (f32[64,512]{1,0:T(8,128)S(1)}, f32[64,512]{1,0:T(8,128)S(1)}, u32[]{:S(2)}, u32[]{:S(2)}) collective-permute-start(f32[64,512]{1,0:T(8,128)S(1)} %get-tuple-element.22), channel_id=1, source_target_pairs={{0,1},{1,2},{2,3},{3,0},{4,5},{5,6},{6,7},{7,4},{8,9},{9,10},{10,1... | collective-permute-start | bytes 393224 | tf_op jit(solution)/shard_map/ppermute | solution.py:380
  6.7 5.8 %collective-permute-start.1 = (f32[64,512]{1,0:T(8,128)S(1)}, f32[64,512]{1,0:T(8,128)S(1)}, u32[]{:S(2)}, u32[]{:S(2)}) collective-permute-start(f32[64,512]{1,0:T(8,128)S(1)} %get-tuple-element.23), channel_id=1, source_target_pairs={{0,2},{1,3},{2,0},{3,1},{4,6},{5,7},{6,4},{7,5},{8,10},{9,11},{10,... | collective-permute-start | bytes 393224 | tf_op jit(solution)/shard_map/ppermute | solution.py:380
  12.5 2.2 %collective-permute-start.2 = (f32[64,512]{1,0:T(8,128)S(1)}, f32[64,512]{1,0:T(8,128)S(1)}, u32[]{:S(2)}, u32[]{:S(2)}) collective-permute-start(f32[64,512]{1,0:T(8,128)S(1)} %get-tuple-element.24), channel_id=1, source_target_pairs={{0,3},{1,0},{2,1},{3,2},{4,7},{5,4},{6,5},{7,6},{8,11},{9,8},{10,9... | collective-permute-start | bytes 393224 | tf_op jit(solution)/shard_map/ppermute | solution.py:380
  14.7 1.6 %shard_map.86 = (f32[128,128]{1,0:T(8,128)S(1)}, f32[16,128]{1,0:T(8,128)S(1)}) custom-call(s32[16,128]{1,0:T(8,128)S(1)} %bitcast.17, s32[16,128]{1,0:T(8,128)S(1)} %bitcast.21, f32[16,128]{1,0:T(8,128)S(1)} %bitcast.19, f32[16,128]{1,0:T(8,128)S(1)} %bitcast.22), custom_call_target="tpu_custom_call" | custom-call | tf_op jit(solution)/shard_map/pallas_call | solution.py:24
  16.4 33.2 %all_to_all.33 = f32[128,1,128]{2,1,0:T(1,128)S(1)} all-to-all(f32[128,1,128]{2,1,0:T(1,128)S(1)} %bitcast.16), channel_id=1, replica_groups=mesh['lat'=8,'lon'=16,'mem'=4] {'lat','lon'}, dimensions={0} | all-to-all | bytes 131072 | tf_op jit(solution)/shard_map/all_to_all | solution.py:379
  49.6 0.9 shard_map.88
  50.6 0.0 copy-start.2
  50.6 7.3 %all_to_all.34.parts_ref = f32[4,64,128]{2,1,0:T(8,128)S(1)} all-to-all(f32[4,64,128]{2,1,0:T(8,128)S(1)} %get-tuple-element.26), channel_id=1, replica_groups=mesh['lat'=8,'lon'=16,'mem'=4] {'mem'}, dimensions={0} | all-to-all | bytes 262144 | tf_op jit(solution)/shard_map/all_to_all | solution.py:386
  57.9 0.1 shard_map.89
  58.0 2.1 %collective-permute-start.3 = (f32[4,8,640]{2,1,0:T(8,128)S(1)}, f32[4,8,640]{2,1,0:T(8,128)S(1)}, u32[]{:S(2)}, u32[]{:S(2)}) collective-permute-start(f32[4,8,640]{2,1,0:T(8,128)S(1)} %get-tuple-element.32), channel_id=1, source_target_pairs={{0,64},{64,128},{128,192},{192,256},{256,320},{320,384},{384,448},... | collective-permute-start | bytes 245768 | tf_op jit(solution)/shard_map/ppermute | solution.py:349
  60.1 1.5 %collective-permute-done.3.north_ref = f32[4,8,640]{2,1,0:T(8,128)S(1)} collective-permute-done((f32[4,8,640]{2,1,0:T(8,128)S(1)}, f32[4,8,640]{2,1,0:T(8,128)S(1)}, u32[]{:S(2)}, u32[]{:S(2)}) %collective-permute-start.3) | collective-permute-done | bytes 81952 | tf_op jit(solution)/shard_map/ppermute | solution.py:349
  61.6 2.7 %collective-permute-done.4.south_ref = f32[4,8,640]{2,1,0:T(8,128)S(1)} collective-permute-done((f32[4,8,640]{2,1,0:T(8,128)S(1)}, f32[4,8,640]{2,1,0:T(8,128)S(1)}, u32[]{:S(2)}, u32[]{:S(2)}) %collective-permute-start.4) | collective-permute-done | bytes 81952 | tf_op jit(solution)/shard_map/ppermute | solution.py:349
  64.3 0.8 shard_map.90
  65.1 2.5 %collective-permute-start.5 = (f32[80,384]{1,0:T(8,128)S(1)}, f32[80,384]{1,0:T(8,128)S(1)}, u32[]{:S(2)}, u32[]{:S(2)}) collective-permute-start(f32[80,384]{1,0:T(8,128)S(1)} %get-tuple-element.34), channel_id=1, source_target_pairs={{0,1},{1,2},{2,3},{3,4},{4,5},{5,6},{6,7},{7,8},{8,9},{9,10},{10,1... | collective-permute-start | bytes 368648 | tf_op jit(solution)/shard_map/ppermute | solution.py:349
  67.6 6.1 %collective-permute-start.6 = (f32[80,384]{1,0:T(8,128)S(1)}, f32[80,384]{1,0:T(8,128)S(1)}, u32[]{:S(2)}, u32[]{:S(2)}) collective-permute-start(f32[80,384]{1,0:T(8,128)S(1)} %get-tuple-element.35), channel_id=1, source_target_pairs={{1,0},{2,1},{3,2},{4,3},{5,4},{6,5},{7,6},{8,7},{9,8},{10,9},{11,1... | collective-permute-start | bytes 368648 | tf_op jit(solution)/shard_map/ppermute | solution.py:349
  73.7 0.3 collective-permute-done.5.west_ref
  74.0 1.5 %collective-permute-done.6.east_ref = f32[80,384]{1,0:T(8,128)S(1)} collective-permute-done((f32[80,384]{1,0:T(8,128)S(1)}, f32[80,384]{1,0:T(8,128)S(1)}, u32[]{:S(2)}, u32[]{:S(2)}) %collective-permute-start.6) | collective-permute-done | bytes 122912 | tf_op jit(solution)/shard_map/ppermute | solution.py:349
  75.5 6.1 %shard_map.91 = f32[4,32,128]{2,1,0:T(8,128)S(1)} custom-call(f32[4,64,640]{2,1,0:T(8,128)S(1)} %get-tuple-element.31.mid_ref, f32[4,8,640]{2,1,0:T(8,128)S(1)} %collective-permute-done.3.north_ref, f32[4,8,640]{2,1,0:T(8,128)S(1)} %collective-permute-done.4.south_ref, f32[80,384]{1,0:T(8,128)S(1)} %collective-permute-done.5.west_ref, ...), custom_call_target="tpu_custom_call" | custom-call | tf_op jit(solution)/shard_map/pallas_call | solution.py:24
  81.6 7.0 %all_to_all.35.pieces_ref = f32[4,32,128]{2,1,0:T(8,128)S(1)} all-to-all(f32[4,32,128]{2,1,0:T(8,128)S(1)} %shard_map.91), channel_id=1, replica_groups=mesh['lat'=8,'lon'=16,'mem'=4] {'mem'}, dimensions={0} | all-to-all | bytes 131072 | tf_op jit(solution)/shard_map/all_to_all | solution.py:411
  88.6 1.4 %shard_map.92 = (f32[64,256]{1,0:T(8,128)}, f32[128,32]{1,0:T(8,128)S(1)}) custom-call(f32[4,32,128]{2,1,0:T(8,128)S(1)} %all_to_all.35.pieces_ref, f32[128,128]{1,0:T(8,128)S(1)} %get-tuple-element.36.turned_ref), custom_call_target="tpu_custom_call" | custom-call | tf_op jit(solution)/shard_map/pallas_call | solution.py:24
  90.0 28.2 %all_to_all.36 = f32[128,1,32]{2,1,0:T(1,128)S(1)} all-to-all(f32[128,1,32]{2,1,0:T(1,128)S(1)} %bitcast.15), channel_id=1, replica_groups=mesh['lat'=8,'lon'=16,'mem'=4] {'lat','lon'}, dimensions={0} | all-to-all | bytes 32768 | tf_op jit(solution)/shard_map/all_to_all | solution.py:415
  118.1 1.0 shard_map.93
  (16 shorter events, 0.0 us)
Async XLA Ops:
  0.6 1.0 copy-start
  1.6 13.1 %copy-start.4 = (f32[2048]{0:T(1024)S(1)}, f32[2048]{0:T(1024)}, u32[]{:S(2)}) copy-start(f32[2048]{0:T(1024)} %param.12) | copy-start | bytes 24580
  1.6 13.1 %copy-start.5 = (s32[2048]{0:T(1024)S(1)}, s32[2048]{0:T(1024)}, u32[]{:S(2)}) copy-start(s32[2048]{0:T(1024)} %param.11) | copy-start | bytes 24580
  1.6 13.1 %copy-start.6 = (f32[2048]{0:T(1024)S(1)}, f32[2048]{0:T(1024)}, u32[]{:S(2)}) copy-start(f32[2048]{0:T(1024)} %param.13) | copy-start | bytes 24580
  1.8 12.9 %copy-start.3 = (s32[2048,1]{0,1:T(1,128)S(1)}, s32[2048,1]{0,1:T(1,128)}, u32[]{:S(2)}) copy-start(s32[2048,1]{0,1:T(1,128)} %param.10) | copy-start | bytes 24580
  1.8 47.8 %collective-permute-start = (f32[64,512]{1,0:T(8,128)S(1)}, f32[64,512]{1,0:T(8,128)S(1)}, u32[]{:S(2)}, u32[]{:S(2)}) collective-permute-start(f32[64,512]{1,0:T(8,128)S(1)} %get-tuple-element.22), channel_id=1, source_target_pairs={{0,1},{1,2},{2,3},{3,0},{4,5},{5,6},{6,7},{7,4},{8,9},{9,10},{10,1... | collective-permute-start | bytes 393224 | tf_op jit(solution)/shard_map/ppermute | solution.py:380
  6.7 43.0 %collective-permute-start.1 = (f32[64,512]{1,0:T(8,128)S(1)}, f32[64,512]{1,0:T(8,128)S(1)}, u32[]{:S(2)}, u32[]{:S(2)}) collective-permute-start(f32[64,512]{1,0:T(8,128)S(1)} %get-tuple-element.23), channel_id=1, source_target_pairs={{0,2},{1,3},{2,0},{3,1},{4,6},{5,7},{6,4},{7,5},{8,10},{9,11},{10,... | collective-permute-start | bytes 393224 | tf_op jit(solution)/shard_map/ppermute | solution.py:380
  12.5 37.1 %collective-permute-start.2 = (f32[64,512]{1,0:T(8,128)S(1)}, f32[64,512]{1,0:T(8,128)S(1)}, u32[]{:S(2)}, u32[]{:S(2)}) collective-permute-start(f32[64,512]{1,0:T(8,128)S(1)} %get-tuple-element.24), channel_id=1, source_target_pairs={{0,3},{1,0},{2,1},{3,2},{4,7},{5,4},{6,5},{7,6},{8,11},{9,8},{10,9... | collective-permute-start | bytes 393224 | tf_op jit(solution)/shard_map/ppermute | solution.py:380
  50.6 7.3 %copy-start.1 = (f32[64,256]{1,0:T(8,128)S(1)}, f32[64,256]{1,0:T(8,128)}, u32[]{:S(2)}) copy-start(f32[64,256]{1,0:T(8,128)} %rate_ref.1) | copy-start | bytes 196612
  50.6 7.3 %copy-start.2 = (s32[64,256]{1,0:T(8,128)S(1)}, s32[64,256]{1,0:T(8,128)}, u32[]{:S(2)}) copy-start(s32[64,256]{1,0:T(8,128)} %sea_ref.1) | copy-start | bytes 196612
  58.0 3.6 %collective-permute-start.3 = (f32[4,8,640]{2,1,0:T(8,128)S(1)}, f32[4,8,640]{2,1,0:T(8,128)S(1)}, u32[]{:S(2)}, u32[]{:S(2)}) collective-permute-start(f32[4,8,640]{2,1,0:T(8,128)S(1)} %get-tuple-element.32), channel_id=1, source_target_pairs={{0,64},{64,128},{128,192},{192,256},{256,320},{320,384},{384,448},... | collective-permute-start | bytes 245768 | tf_op jit(solution)/shard_map/ppermute | solution.py:349
  60.1 4.2 %collective-permute-start.4 = (f32[4,8,640]{2,1,0:T(8,128)S(1)}, f32[4,8,640]{2,1,0:T(8,128)S(1)}, u32[]{:S(2)}, u32[]{:S(2)}) collective-permute-start(f32[4,8,640]{2,1,0:T(8,128)S(1)} %get-tuple-element.33), channel_id=1, source_target_pairs={{64,0},{128,64},{192,128},{256,192},{320,256},{384,320},{448,384},... | collective-permute-start | bytes 245768 | tf_op jit(solution)/shard_map/ppermute | solution.py:349
  65.1 8.9 %collective-permute-start.5 = (f32[80,384]{1,0:T(8,128)S(1)}, f32[80,384]{1,0:T(8,128)S(1)}, u32[]{:S(2)}, u32[]{:S(2)}) collective-permute-start(f32[80,384]{1,0:T(8,128)S(1)} %get-tuple-element.34), channel_id=1, source_target_pairs={{0,1},{1,2},{2,3},{3,4},{4,5},{5,6},{6,7},{7,8},{8,9},{9,10},{10,1... | collective-permute-start | bytes 368648 | tf_op jit(solution)/shard_map/ppermute | solution.py:349
  67.6 7.9 %collective-permute-start.6 = (f32[80,384]{1,0:T(8,128)S(1)}, f32[80,384]{1,0:T(8,128)S(1)}, u32[]{:S(2)}, u32[]{:S(2)}) collective-permute-start(f32[80,384]{1,0:T(8,128)S(1)} %get-tuple-element.35), channel_id=1, source_target_pairs={{1,0},{2,1},{3,2},{4,3},{5,4},{6,5},{7,6},{8,7},{9,8},{10,9},{11,1... | collective-permute-start | bytes 368648 | tf_op jit(solution)/shard_map/ppermute | solution.py:349

commit v3 on v2

--- a/solution.py
+++ b/solution.py
@@ -141,7 +141,7 @@
 
 def reduce_kernel(parts_ref, rate_ref, sea_ref, *rest):
     quarters = parts_ref.shape[0]
-    piece_refs, (mid_ref, top_ref, bottom_ref, kept_ref) = rest[:quarters], rest[quarters:]
+    piece_refs, (mid_ref, one_ref, two_ref, kept_ref) = rest[:quarters], rest[quarters:]
     rows, lanes = piece_refs[0].shape
     width = parts_ref.shape[2] // 2
     mine = lax.axis_index("mem")
@@ -156,13 +156,15 @@
         kept_ref[q, :, :width] = rate_ref[:, at]
         kept_ref[q, :, width:] = sea_ref[:, at].astype(F32)
     mid_ref[1, :, lanes:] = kept_ref[mine]
+    even = lax.axis_index("lat") % 2 == 0
     for q in range(quarters):
         size = lanes if q > 1 else lanes + 2 * width
-        top_ref[q, :, :size] = mid_ref[q, :HALO, :size]
-        bottom_ref[q, :, :size] = mid_ref[q, rows - HALO :, :size]
-        if size < top_ref.shape[2]:
-            top_ref[q, :, size:] = jnp.zeros((HALO, 2 * width), F32)
-            bottom_ref[q, :, size:] = jnp.zeros((HALO, 2 * width), F32)
+        top, bottom = mid_ref[q, :HALO, :size], mid_ref[q, rows - HALO :, :size]
+        one_ref[q, :, :size] = jnp.where(even, bottom, top)
+        two_ref[q, :, :size] = jnp.where(even, top, bottom)
+        if size < one_ref.shape[2]:
+            one_ref[q, :, size:] = jnp.zeros((HALO, 2 * width), F32)
+            two_ref[q, :, size:] = jnp.zeros((HALO, 2 * width), F32)
 
 
 def fields_of(ref, width):
@@ -171,33 +173,33 @@
     return places + [(0, lanes), (0, lanes + width), (1, lanes), (1, lanes + width)]
 
 
-def outside_rows(rows):
+def rim_kernel(
+    mid_ref, got_one_ref, got_two_ref, one_ref, two_ref, north_ref, south_ref, first_ref, last_ref, *, width
+):
+    rows, lanes = mid_ref.shape[1], mid_ref.shape[2]
     lat = lax.axis_index("lat")
-    return lat == 0, lat == lax.axis_size("lat") - 1
-
-
-def rim_kernel(mid_ref, north_ref, south_ref, first_ref, last_ref, *, width):
-    rows = mid_ref.shape[1]
+    even = lat % 2 == 0
+    north_ref[...] = jnp.where(even, got_two_ref[...], got_one_ref[...])
+    south_ref[...] = jnp.where(even, got_one_ref[...], got_two_ref[...])
+    sea = slice(lanes - width, lanes)
+    north_ref[1, :, sea] = jnp.where(lat == 0, 0.0, north_ref[1, :, sea])
+    south_ref[1, :, sea] = jnp.where(lat == lax.axis_size("lat") - 1, 0.0, south_ref[1, :, sea])
     first_ref[...] = jnp.zeros(first_ref.shape, F32)
     last_ref[...] = jnp.zeros(last_ref.shape, F32)
-    places = fields_of(mid_ref, width)
-    no_north, no_south = outside_rows(rows)
-    for k, (q, lane) in enumerate(places):
+    for k, (q, lane) in enumerate(fields_of(mid_ref, width)):
         at = slice(k * HALO, (k + 1) * HALO)
         for ref, cut in ((first_ref, lane), (last_ref, lane + width - HALO)):
-            north = north_ref[q, :, cut : cut + HALO]
-            south = south_ref[q, :, cut : cut + HALO]
-            if k == len(places) - 1:
-                north = jnp.where(no_north, 0.0, north)
-                south = jnp.where(no_south, 0.0, south)
-            ref[:HALO, at] = north
+            ref[:HALO, at] = north_ref[q, :, cut : cut + HALO]
             ref[HALO : HALO + rows, at] = mid_ref[q, :, cut : cut + HALO]
-            ref[HALO + rows :, at] = south
+            ref[HALO + rows :, at] = south_ref[q, :, cut : cut + HALO]
+    even = lax.axis_index("mem") % 2 == 0
+    one_ref[...] = jnp.where(even, last_ref[...], first_ref[...])
+    two_ref[...] = jnp.where(even, first_ref[...], last_ref[...])
 
 
 def product_kernel(
-    mid_ref, north_ref, south_ref, west_ref, east_ref, out_ref,
-    members_ref, state_ref, weights_ref, tiled_ref, field_ref,
+    mid_ref, north_ref, south_ref, one_ref, two_ref, out_ref,
+    members_ref, state_ref, weights_ref, tiled_ref, field_ref, west_ref, east_ref,
 ):
     groups, height, lanes = members_ref.shape
     rows = height - 2 * HALO
@@ -212,9 +214,10 @@
             tiled_ref[:, k * span : (k + 1) * span] = value
         return tiled_ref[...]
 
-    places = fields_of(mid_ref, width)
-    no_north, no_south = outside_rows(rows)
-    for k, (q, lane) in enumerate(places):
+    even = lax.axis_index("mem") % 2 == 0
+    west_ref[...] = jnp.where(even, two_ref[...], one_ref[...])
+    east_ref[...] = jnp.where(even, one_ref[...], two_ref[...])
+    for k, (q, lane) in enumerate(fields_of(mid_ref, width)):
         rim = slice(k * HALO, (k + 1) * HALO)
         cut = slice(lane, lane + width)
         north, south = north_ref[q, :, cut], south_ref[q, :, cut]
@@ -222,9 +225,6 @@
             ref, low = members_ref.at[k // windows], k % windows * span
         else:
             ref, low = field_ref.at[k - groups * windows], 0
-        if k == len(places) - 1:
-            north = jnp.where(no_north, 0.0, north)
-            south = jnp.where(no_south, 0.0, south)
         ref[:, low : low + HALO] = west_ref[:, rim]
         ref[:HALO, low + HALO : low + HALO + width] = north
         ref[HALO : HALO + rows, low + HALO : low + HALO + width] = mid_ref[q, :, cut]
@@ -336,17 +336,13 @@
     return jax.ShapeDtypeStruct(dims, dtype)
 
 
-def neighbours(axes):
+def exchange(first, second, axes):
     size = 1
     for axis in axes:
         size *= lax.axis_size(axis)
-    up = [(i, (i + 1) % size) for i in range(size)]
-    return up, [(j, i) for i, j in up]
-
-
-def exchange(first, last, axes):
-    up, down = neighbours(axes)
-    return lax.ppermute(last, axes, up), lax.ppermute(first, axes, down)
+    swaps = [[(i + k, (i + k + 1) % size) for i in range(0, size, 2)] for k in range(2)]
+    both = [pairs + [(j, i) for i, j in pairs] for pairs in swaps]
+    return lax.ppermute(first, axes, both[0]), lax.ppermute(second, axes, both[1])
 
 
 def per_device(perturbations, diffusivity, sea_mask, obs_owner, obs_cell, obs_depart, obs_weight):
@@ -386,16 +382,20 @@
     parts = lax.all_to_all(parts, "mem", split_axis=0, concat_axis=0, tiled=True)
     field_lanes = members * width + 2 * width
     strip = shape(quarters, HALO, field_lanes)
-    mid, top, bottom = call(
+    mid, one, two = call(
         reduce_kernel,
         (shape(quarters, rows, field_lanes), strip, strip),
         [pltpu.VMEM((quarters, rows, 2 * width), F32)],
     )(parts, diffusivity, sea_mask, own, *brought)
-    north, south = exchange(top, bottom, ("lat",))
+    one, two = exchange(one, two, ("lat",))
     rim_lanes = -(-(quarters * members + 4) * HALO // LANES) * LANES
     rim = shape(height, rim_lanes)
-    first, last = call(functools.partial(rim_kernel, width=width), (rim, rim))(mid, north, south)
-    west, east = exchange(first, last, ("lon", "mem"))
+    one, two, north, south = call(
+        functools.partial(rim_kernel, width=width),
+        (rim, rim, strip, strip),
+        [pltpu.VMEM((height, rim_lanes), F32)] * 2,
+    )(mid, one, two)
+    one, two = exchange(one, two, ("lon", "mem"))
     lanes = members * span
     quarter = call(
         product_kernel,
@@ -406,8 +406,10 @@
             pltpu.VMEM((5, height, lanes), F32),
             pltpu.VMEM((height, lanes), F32),
             pltpu.VMEM((4, height, LANES), F32),
+            pltpu.VMEM((height, rim_lanes), F32),
+            pltpu.VMEM((height, rim_lanes), F32),
         ],
-    )(mid, north, south, west, east)
+    )(mid, north, south, one, two)
     quarter = lax.all_to_all(quarter, "mem", split_axis=0, concat_axis=0, tiled=True)
     increment, answers = call(
         answer_kernel, (shape(rows, cols), shape(places, SLOTS)), [pltpu.VMEM((LANES, places), F32)]

time: 120 us -> 119 us (level)
  blocking collectives: 75.7 us -> 70.4 us
  waiting for transfers between devices: 6.01 us -> 11.1 us
    all_to_all x1, blocking collectives: 28.2 us -> 22.8 us  [per_device(): lax.all_to_all(answers, tiles, split_axis=0, concat_axis=0, tiled=True)]
    ppermute x4, waiting for transfers between devices: 6.01 us -> 11.1 us  [the longest x2 9.94 us: exchange(): lax.ppermute(second, axes, both[1])]
  transfers between devices with their start and end apart: 7 -> 7, of which waited for: 4 -> 3; matrix products, arithmetic and copies ran while one was open for 0% -> 0% of each run, Pallas kernels for 1% -> 1%
where the time goes in v3:
time: 119 us
  blocking collectives  70.4 us (59%)
  starting transfers between devices  23.2 us (19%)
  Pallas kernels  12.1 us (10%)
  waiting for transfers between devices  11.1 us (9%)
    all_to_all x1, blocking collectives, per_device(): lax.all_to_all(outgoing, tiles, split_axis=0, concat_axis=0, tiled=True)  33.2 us
    all_to_all x1, blocking collectives, per_device(): lax.all_to_all(answers, tiles, split_axis=0, concat_axis=0, tiled=True)  22.8 us
    ppermute x3, starting transfers between devices, per_device(): brought = [lax.ppermute(s, 'mem', pairs) for s, pairs in zip(sent, ring)]  12.8 us
    pallas_call x8, Pallas kernels, run(): pl.pallas_call(kernel, out_shape=outs, in_specs=[place] * len(operands),...  12.1 us
    ppermute x2, waiting for transfers between devices, exchange(): lax.ppermute(second, axes, both[1])  9.94 us
    all_to_all x1, blocking collectives, per_device(): lax.all_to_all(parts, 'mem', split_axis=0, concat_axis=0, tiled=True)  7.32 us
    all_to_all x1, blocking collectives, per_device(): lax.all_to_all(quarter, 'mem', split_axis=0, concat_axis=0, tiled=True)  6.96 us
    ppermute x2, starting transfers between devices, exchange(): lax.ppermute(first, axes, both[0])  6.51 us
  transfers between devices with their start and end apart: 7, of which 3 were waited for; matrix products, arithmetic and copies ran while one was open for 0% of the time, Pallas kernels for 1%

profile of v3, /device:TPU:1, one launch (start us, length us, event | category | flops | bytes accessed | tf_op | source)
XLA Modules:
  0.0 118.6 jit_solution(1940399823419581663)
XLA Ops:
  0.6 0.9 copy-done
  1.6 0.2 shard_map.87
  1.8 4.8 %collective-permute-start = (f32[64,512]{1,0:T(8,128)S(1)}, f32[64,512]{1,0:T(8,128)S(1)}, u32[]{:S(2)}, u32[]{:S(2)}) collective-permute-start(f32[64,512]{1,0:T(8,128)S(1)} %get-tuple-element.24), channel_id=1, source_target_pairs={{0,1},{1,2},{2,3},{3,0},{4,5},{5,6},{6,7},{7,4},{8,9},{9,10},{10,1... | collective-permute-start | bytes 393224 | tf_op jit(solution)/shard_map/ppermute | solution.py:376
  6.7 5.8 %collective-permute-start.1 = (f32[64,512]{1,0:T(8,128)S(1)}, f32[64,512]{1,0:T(8,128)S(1)}, u32[]{:S(2)}, u32[]{:S(2)}) collective-permute-start(f32[64,512]{1,0:T(8,128)S(1)} %get-tuple-element.25), channel_id=1, source_target_pairs={{0,2},{1,3},{2,0},{3,1},{4,6},{5,7},{6,4},{7,5},{8,10},{9,11},{10,... | collective-permute-start | bytes 393224 | tf_op jit(solution)/shard_map/ppermute | solution.py:376
  12.5 2.2 %collective-permute-start.2 = (f32[64,512]{1,0:T(8,128)S(1)}, f32[64,512]{1,0:T(8,128)S(1)}, u32[]{:S(2)}, u32[]{:S(2)}) collective-permute-start(f32[64,512]{1,0:T(8,128)S(1)} %get-tuple-element.26), channel_id=1, source_target_pairs={{0,3},{1,0},{2,1},{3,2},{4,7},{5,4},{6,5},{7,6},{8,11},{9,8},{10,9... | collective-permute-start | bytes 393224 | tf_op jit(solution)/shard_map/ppermute | solution.py:376
  14.7 1.6 %shard_map.86 = (f32[128,128]{1,0:T(8,128)S(1)}, f32[16,128]{1,0:T(8,128)S(1)}) custom-call(s32[16,128]{1,0:T(8,128)S(1)} %bitcast.17, s32[16,128]{1,0:T(8,128)S(1)} %bitcast.21, f32[16,128]{1,0:T(8,128)S(1)} %bitcast.19, f32[16,128]{1,0:T(8,128)S(1)} %bitcast.22), custom_call_target="tpu_custom_call" | custom-call | tf_op jit(solution)/shard_map/pallas_call | solution.py:24
  16.4 33.2 %all_to_all.33 = f32[128,1,128]{2,1,0:T(1,128)S(1)} all-to-all(f32[128,1,128]{2,1,0:T(1,128)S(1)} %bitcast.16), channel_id=1, replica_groups=mesh['lat'=8,'lon'=16,'mem'=4] {'lat','lon'}, dimensions={0} | all-to-all | bytes 131072 | tf_op jit(solution)/shard_map/all_to_all | solution.py:375
  49.6 0.9 shard_map.88
  50.6 0.0 copy-start.2
  50.6 7.3 %all_to_all.34.parts_ref = f32[4,64,128]{2,1,0:T(8,128)S(1)} all-to-all(f32[4,64,128]{2,1,0:T(8,128)S(1)} %get-tuple-element.28), channel_id=1, replica_groups=mesh['lat'=8,'lon'=16,'mem'=4] {'mem'}, dimensions={0} | all-to-all | bytes 262144 | tf_op jit(solution)/shard_map/all_to_all | solution.py:382
  57.9 0.1 shard_map.89
  58.0 4.0 %collective-permute-start.3 = (f32[4,8,640]{2,1,0:T(8,128)S(1)}, f32[4,8,640]{2,1,0:T(8,128)S(1)}, u32[]{:S(2)}, u32[]{:S(2)}) collective-permute-start(f32[4,8,640]{2,1,0:T(8,128)S(1)} %get-tuple-element.34), channel_id=1, source_target_pairs={{0,64},{128,192},{256,320},{384,448},{64,0},{192,128},{320,256},{4... | collective-permute-start | bytes 245768 | tf_op jit(solution)/shard_map/ppermute | solution.py:345
  62.0 2.0 %collective-permute-start.4 = (f32[4,8,640]{2,1,0:T(8,128)S(1)}, f32[4,8,640]{2,1,0:T(8,128)S(1)}, u32[]{:S(2)}, u32[]{:S(2)}) collective-permute-start(f32[4,8,640]{2,1,0:T(8,128)S(1)} %get-tuple-element.35), channel_id=1, source_target_pairs={{64,128},{192,256},{320,384},{448,0},{128,64},{256,192},{384,320},... | collective-permute-start | bytes 245768 | tf_op jit(solution)/shard_map/ppermute | solution.py:345
  64.0 4.1 %collective-permute-done.4.got_two_ref = f32[4,8,640]{2,1,0:T(8,128)S(1)} collective-permute-done((f32[4,8,640]{2,1,0:T(8,128)S(1)}, f32[4,8,640]{2,1,0:T(8,128)S(1)}, u32[]{:S(2)}, u32[]{:S(2)}) %collective-permute-start.4) | collective-permute-done | bytes 81952 | tf_op jit(solution)/shard_map/ppermute | solution.py:345
  68.1 0.8 shard_map.90
  68.9 2.5 %collective-permute-start.5 = (f32[80,384]{1,0:T(8,128)S(1)}, f32[80,384]{1,0:T(8,128)S(1)}, u32[]{:S(2)}, u32[]{:S(2)}) collective-permute-start(f32[80,384]{1,0:T(8,128)S(1)} %get-tuple-element.38), channel_id=1, source_target_pairs={{0,1},{2,3},{4,5},{6,7},{8,9},{10,11},{12,13},{14,15},{16,17},{18,... | collective-permute-start | bytes 368648 | tf_op jit(solution)/shard_map/ppermute | solution.py:345
  71.4 1.9 %collective-permute-start.6 = (f32[80,384]{1,0:T(8,128)S(1)}, f32[80,384]{1,0:T(8,128)S(1)}, u32[]{:S(2)}, u32[]{:S(2)}) collective-permute-start(f32[80,384]{1,0:T(8,128)S(1)} %get-tuple-element.39), channel_id=1, source_target_pairs={{1,2},{3,4},{5,6},{7,8},{9,10},{11,12},{13,14},{15,16},{17,18},{19... | collective-permute-start | bytes 368648 | tf_op jit(solution)/shard_map/ppermute | solution.py:345
  73.3 1.1 collective-permute-done.5.one_ref
  74.5 5.9 %collective-permute-done.6.two_ref = f32[80,384]{1,0:T(8,128)S(1)} collective-permute-done((f32[80,384]{1,0:T(8,128)S(1)}, f32[80,384]{1,0:T(8,128)S(1)}, u32[]{:S(2)}, u32[]{:S(2)}) %collective-permute-start.6) | collective-permute-done | bytes 122912 | tf_op jit(solution)/shard_map/ppermute | solution.py:345
  80.4 6.1 %shard_map.91 = f32[4,32,128]{2,1,0:T(8,128)S(1)} custom-call(f32[4,64,640]{2,1,0:T(8,128)S(1)} %get-tuple-element.33.mid_ref, f32[4,8,640]{2,1,0:T(8,128)S(1)} %get-tuple-element.36.north_ref, f32[4,8,640]{2,1,0:T(8,128)S(1)} %get-tuple-element.37.south_ref, f32[80,384]{1,0:T(8,128)S(1)} %collective-permute-done.5.one_ref, ...), custom_call_target="tpu_custom_call" | custom-call | tf_op jit(solution)/shard_map/pallas_call | solution.py:24
  86.5 7.0 %all_to_all.35.pieces_ref = f32[4,32,128]{2,1,0:T(8,128)S(1)} all-to-all(f32[4,32,128]{2,1,0:T(8,128)S(1)} %shard_map.91), channel_id=1, replica_groups=mesh['lat'=8,'lon'=16,'mem'=4] {'mem'}, dimensions={0} | all-to-all | bytes 131072 | tf_op jit(solution)/shard_map/all_to_all | solution.py:413
  93.4 1.4 %shard_map.92 = (f32[64,256]{1,0:T(8,128)}, f32[128,32]{1,0:T(8,128)S(1)}) custom-call(f32[4,32,128]{2,1,0:T(8,128)S(1)} %all_to_all.35.pieces_ref, f32[128,128]{1,0:T(8,128)S(1)} %get-tuple-element.40.turned_ref), custom_call_target="tpu_custom_call" | custom-call | tf_op jit(solution)/shard_map/pallas_call | solution.py:24
  94.8 22.8 %all_to_all.36 = f32[128,1,32]{2,1,0:T(1,128)S(1)} all-to-all(f32[128,1,32]{2,1,0:T(1,128)S(1)} %bitcast.15), channel_id=1, replica_groups=mesh['lat'=8,'lon'=16,'mem'=4] {'lat','lon'}, dimensions={0} | all-to-all | bytes 32768 | tf_op jit(solution)/shard_map/all_to_all | solution.py:417
  117.6 1.0 shard_map.93
  (16 shorter events, 0.0 us)
Async XLA Ops:
  0.6 1.0 copy-start
  1.6 13.1 %copy-start.4 = (f32[2048]{0:T(1024)S(1)}, f32[2048]{0:T(1024)}, u32[]{:S(2)}) copy-start(f32[2048]{0:T(1024)} %param.12) | copy-start | bytes 24580
  1.6 13.1 %copy-start.5 = (s32[2048]{0:T(1024)S(1)}, s32[2048]{0:T(1024)}, u32[]{:S(2)}) copy-start(s32[2048]{0:T(1024)} %param.11) | copy-start | bytes 24580
  1.6 13.1 %copy-start.6 = (f32[2048]{0:T(1024)S(1)}, f32[2048]{0:T(1024)}, u32[]{:S(2)}) copy-start(f32[2048]{0:T(1024)} %param.13) | copy-start | bytes 24580
  1.8 12.9 %copy-start.3 = (s32[2048,1]{0,1:T(1,128)S(1)}, s32[2048,1]{0,1:T(1,128)}, u32[]{:S(2)}) copy-start(s32[2048,1]{0,1:T(1,128)} %param.10) | copy-start | bytes 24580
  1.8 47.8 %collective-permute-start = (f32[64,512]{1,0:T(8,128)S(1)}, f32[64,512]{1,0:T(8,128)S(1)}, u32[]{:S(2)}, u32[]{:S(2)}) collective-permute-start(f32[64,512]{1,0:T(8,128)S(1)} %get-tuple-element.24), channel_id=1, source_target_pairs={{0,1},{1,2},{2,3},{3,0},{4,5},{5,6},{6,7},{7,4},{8,9},{9,10},{10,1... | collective-permute-start | bytes 393224 | tf_op jit(solution)/shard_map/ppermute | solution.py:376
  6.7 43.0 %collective-permute-start.1 = (f32[64,512]{1,0:T(8,128)S(1)}, f32[64,512]{1,0:T(8,128)S(1)}, u32[]{:S(2)}, u32[]{:S(2)}) collective-permute-start(f32[64,512]{1,0:T(8,128)S(1)} %get-tuple-element.25), channel_id=1, source_target_pairs={{0,2},{1,3},{2,0},{3,1},{4,6},{5,7},{6,4},{7,5},{8,10},{9,11},{10,... | collective-permute-start | bytes 393224 | tf_op jit(solution)/shard_map/ppermute | solution.py:376
  12.5 37.1 %collective-permute-start.2 = (f32[64,512]{1,0:T(8,128)S(1)}, f32[64,512]{1,0:T(8,128)S(1)}, u32[]{:S(2)}, u32[]{:S(2)}) collective-permute-start(f32[64,512]{1,0:T(8,128)S(1)} %get-tuple-element.26), channel_id=1, source_target_pairs={{0,3},{1,0},{2,1},{3,2},{4,7},{5,4},{6,5},{7,6},{8,11},{9,8},{10,9... | collective-permute-start | bytes 393224 | tf_op jit(solution)/shard_map/ppermute | solution.py:376
  50.6 7.3 %copy-start.1 = (f32[64,256]{1,0:T(8,128)S(1)}, f32[64,256]{1,0:T(8,128)}, u32[]{:S(2)}) copy-start(f32[64,256]{1,0:T(8,128)} %rate_ref.1) | copy-start | bytes 196612
  50.6 7.3 %copy-start.2 = (s32[64,256]{1,0:T(8,128)S(1)}, s32[64,256]{1,0:T(8,128)}, u32[]{:S(2)}) copy-start(s32[64,256]{1,0:T(8,128)} %sea_ref.1) | copy-start | bytes 196612
  58.0 6.0 %collective-permute-start.3 = (f32[4,8,640]{2,1,0:T(8,128)S(1)}, f32[4,8,640]{2,1,0:T(8,128)S(1)}, u32[]{:S(2)}, u32[]{:S(2)}) collective-permute-start(f32[4,8,640]{2,1,0:T(8,128)S(1)} %get-tuple-element.34), channel_id=1, source_target_pairs={{0,64},{128,192},{256,320},{384,448},{64,0},{192,128},{320,256},{4... | collective-permute-start | bytes 245768 | tf_op jit(solution)/shard_map/ppermute | solution.py:345
  62.0 6.1 %collective-permute-start.4 = (f32[4,8,640]{2,1,0:T(8,128)S(1)}, f32[4,8,640]{2,1,0:T(8,128)S(1)}, u32[]{:S(2)}, u32[]{:S(2)}) collective-permute-start(f32[4,8,640]{2,1,0:T(8,128)S(1)} %get-tuple-element.35), channel_id=1, source_target_pairs={{64,128},{192,256},{320,384},{448,0},{128,64},{256,192},{384,320},... | collective-permute-start | bytes 245768 | tf_op jit(solution)/shard_map/ppermute | solution.py:345
  68.9 5.6 %collective-permute-start.5 = (f32[80,384]{1,0:T(8,128)S(1)}, f32[80,384]{1,0:T(8,128)S(1)}, u32[]{:S(2)}, u32[]{:S(2)}) collective-permute-start(f32[80,384]{1,0:T(8,128)S(1)} %get-tuple-element.38), channel_id=1, source_target_pairs={{0,1},{2,3},{4,5},{6,7},{8,9},{10,11},{12,13},{14,15},{16,17},{18,... | collective-permute-start | bytes 368648 | tf_op jit(solution)/shard_map/ppermute | solution.py:345
  71.4 8.9 %collective-permute-start.6 = (f32[80,384]{1,0:T(8,128)S(1)}, f32[80,384]{1,0:T(8,128)S(1)}, u32[]{:S(2)}, u32[]{:S(2)}) collective-permute-start(f32[80,384]{1,0:T(8,128)S(1)} %get-tuple-element.39), channel_id=1, source_target_pairs={{1,2},{3,4},{5,6},{7,8},{9,10},{11,12},{13,14},{15,16},{17,18},{19... | collective-permute-start | bytes 368648 | tf_op jit(solution)/shard_map/ppermute | solution.py:345

commit v4 on v3

--- a/solution.py
+++ b/solution.py
@@ -141,7 +141,7 @@
 
 def reduce_kernel(parts_ref, rate_ref, sea_ref, *rest):
     quarters = parts_ref.shape[0]
-    piece_refs, (mid_ref, one_ref, two_ref, kept_ref) = rest[:quarters], rest[quarters:]
+    piece_refs, (mid_ref, top_ref, bottom_ref, kept_ref) = rest[:quarters], rest[quarters:]
     rows, lanes = piece_refs[0].shape
     width = parts_ref.shape[2] // 2
     mine = lax.axis_index("mem")
@@ -156,15 +156,13 @@
         kept_ref[q, :, :width] = rate_ref[:, at]
         kept_ref[q, :, width:] = sea_ref[:, at].astype(F32)
     mid_ref[1, :, lanes:] = kept_ref[mine]
-    even = lax.axis_index("lat") % 2 == 0
     for q in range(quarters):
         size = lanes if q > 1 else lanes + 2 * width
-        top, bottom = mid_ref[q, :HALO, :size], mid_ref[q, rows - HALO :, :size]
-        one_ref[q, :, :size] = jnp.where(even, bottom, top)
-        two_ref[q, :, :size] = jnp.where(even, top, bottom)
-        if size < one_ref.shape[2]:
-            one_ref[q, :, size:] = jnp.zeros((HALO, 2 * width), F32)
-            two_ref[q, :, size:] = jnp.zeros((HALO, 2 * width), F32)
+        top_ref[q, :, :size] = mid_ref[q, :HALO, :size]
+        bottom_ref[q, :, :size] = mid_ref[q, rows - HALO :, :size]
+        if size < top_ref.shape[2]:
+            top_ref[q, :, size:] = jnp.zeros((HALO, 2 * width), F32)
+            bottom_ref[q, :, size:] = jnp.zeros((HALO, 2 * width), F32)
 
 
 def fields_of(ref, width):
@@ -174,13 +172,12 @@
 
 
 def rim_kernel(
-    mid_ref, got_one_ref, got_two_ref, one_ref, two_ref, north_ref, south_ref, first_ref, last_ref, *, width
+    mid_ref, before_ref, after_ref, one_ref, two_ref, north_ref, south_ref, first_ref, last_ref, *, width
 ):
     rows, lanes = mid_ref.shape[1], mid_ref.shape[2]
     lat = lax.axis_index("lat")
-    even = lat % 2 == 0
-    north_ref[...] = jnp.where(even, got_two_ref[...], got_one_ref[...])
-    south_ref[...] = jnp.where(even, got_one_ref[...], got_two_ref[...])
+    north_ref[...] = before_ref[...]
+    south_ref[...] = after_ref[...]
     sea = slice(lanes - width, lanes)
     north_ref[1, :, sea] = jnp.where(lat == 0, 0.0, north_ref[1, :, sea])
     south_ref[1, :, sea] = jnp.where(lat == lax.axis_size("lat") - 1, 0.0, south_ref[1, :, sea])
@@ -336,6 +333,12 @@
     return jax.ShapeDtypeStruct(dims, dtype)
 
 
+def shift(first, last, axis):
+    size = lax.axis_size(axis)
+    up = [(i, (i + 1) % size) for i in range(size)]
+    return lax.ppermute(last, axis, up), lax.ppermute(first, axis, [(j, i) for i, j in up])
+
+
 def exchange(first, second, axes):
     size = 1
     for axis in axes:
@@ -382,19 +385,19 @@
     parts = lax.all_to_all(parts, "mem", split_axis=0, concat_axis=0, tiled=True)
     field_lanes = members * width + 2 * width
     strip = shape(quarters, HALO, field_lanes)
-    mid, one, two = call(
+    mid, top, bottom = call(
         reduce_kernel,
         (shape(quarters, rows, field_lanes), strip, strip),
         [pltpu.VMEM((quarters, rows, 2 * width), F32)],
     )(parts, diffusivity, sea_mask, own, *brought)
-    one, two = exchange(one, two, ("lat",))
+    north, south = shift(top, bottom, "lat")
     rim_lanes = -(-(quarters * members + 4) * HALO // LANES) * LANES
     rim = shape(height, rim_lanes)
     one, two, north, south = call(
         functools.partial(rim_kernel, width=width),
         (rim, rim, strip, strip),
         [pltpu.VMEM((height, rim_lanes), F32)] * 2,
-    )(mid, one, two)
+    )(mid, north, south)
     one, two = exchange(one, two, ("lon", "mem"))
     lanes = members * span
     quarter = call(

time: 119 us -> 115 us (0.966)
  starting transfers between devices: 23.2 us -> 19.4 us
    ppermute x0 -> x2, waiting for transfers between devices: none -> 4.16 us  [the longest x1 2.67 us: shift(): lax.ppermute(first, axis, [(j, i) for i, j in up])]
    ppermute x2 -> x1, waiting for transfers between devices: 9.94 us -> 5.87 us  [exchange(): lax.ppermute(second, axes, both[1])]
    ppermute x2 -> x1, starting transfers between devices: 6.51 us -> 2.54 us  [exchange(): lax.ppermute(first, axes, both[0])]
    ppermute x0 -> x2, starting transfers between devices: none -> 2.12 us  [the longest x1 2.12 us: shift(): lax.ppermute(last, axis, up)]
    ppermute x2 -> x1, starting transfers between devices: 3.89 us -> 1.92 us  [exchange(): lax.ppermute(second, axes, both[1])]
  transfers between devices with their start and end apart: 7 -> 7, of which waited for: 3 -> 4; matrix products, arithmetic and copies ran while one was open for 0% -> 0% of each run, Pallas kernels for 1% -> 1%
where the time goes in v4:
time: 115 us
  blocking collectives  70.5 us (61%)
  starting transfers between devices  19.4 us (17%)
  Pallas kernels  12.1 us (11%)
  waiting for transfers between devices  11.2 us (10%)
    all_to_all x1, blocking collectives, per_device(): lax.all_to_all(outgoing, tiles, split_axis=0, concat_axis=0, tiled=True)  33.2 us
    all_to_all x1, blocking collectives, per_device(): lax.all_to_all(answers, tiles, split_axis=0, concat_axis=0, tiled=True)  23 us
    ppermute x3, starting transfers between devices, per_device(): brought = [lax.ppermute(s, 'mem', pairs) for s, pairs in zip(sent, ring)]  12.8 us
    pallas_call x8, Pallas kernels, run(): pl.pallas_call(kernel, out_shape=outs, in_specs=[place] * len(operands),...  12.1 us
    all_to_all x1, blocking collectives, per_device(): lax.all_to_all(parts, 'mem', split_axis=0, concat_axis=0, tiled=True)  7.32 us
    all_to_all x1, blocking collectives, per_device(): lax.all_to_all(quarter, 'mem', split_axis=0, concat_axis=0, tiled=True)  6.96 us
    ppermute x1, waiting for transfers between devices, exchange(): lax.ppermute(second, axes, both[1])  5.87 us
    ppermute x1, waiting for transfers between devices, shift(): lax.ppermute(first, axis, [(j, i) for i, j in up])  2.67 us
  transfers between devices with their start and end apart: 7, of which 4 were waited for; matrix products, arithmetic and copies ran while one was open for 0% of the time, Pallas kernels for 1%

profile of v4, /device:TPU:1, one launch (start us, length us, event | category | flops | bytes accessed | tf_op | source)
XLA Modules:
  0.0 115.0 jit_solution(32285129264436145)
XLA Ops:
  0.6 0.9 copy-done
  1.6 0.2 shard_map.87
  1.8 4.8 %collective-permute-start = (f32[64,512]{1,0:T(8,128)S(1)}, f32[64,512]{1,0:T(8,128)S(1)}, u32[]{:S(2)}, u32[]{:S(2)}) collective-permute-start(f32[64,512]{1,0:T(8,128)S(1)} %get-tuple-element.24), channel_id=1, source_target_pairs={{0,1},{1,2},{2,3},{3,0},{4,5},{5,6},{6,7},{7,4},{8,9},{9,10},{10,1... | collective-permute-start | bytes 393224 | tf_op jit(solution)/shard_map/ppermute | solution.py:379
  6.7 5.8 %collective-permute-start.1 = (f32[64,512]{1,0:T(8,128)S(1)}, f32[64,512]{1,0:T(8,128)S(1)}, u32[]{:S(2)}, u32[]{:S(2)}) collective-permute-start(f32[64,512]{1,0:T(8,128)S(1)} %get-tuple-element.25), channel_id=1, source_target_pairs={{0,2},{1,3},{2,0},{3,1},{4,6},{5,7},{6,4},{7,5},{8,10},{9,11},{10,... | collective-permute-start | bytes 393224 | tf_op jit(solution)/shard_map/ppermute | solution.py:379
  12.5 2.2 %collective-permute-start.2 = (f32[64,512]{1,0:T(8,128)S(1)}, f32[64,512]{1,0:T(8,128)S(1)}, u32[]{:S(2)}, u32[]{:S(2)}) collective-permute-start(f32[64,512]{1,0:T(8,128)S(1)} %get-tuple-element.26), channel_id=1, source_target_pairs={{0,3},{1,0},{2,1},{3,2},{4,7},{5,4},{6,5},{7,6},{8,11},{9,8},{10,9... | collective-permute-start | bytes 393224 | tf_op jit(solution)/shard_map/ppermute | solution.py:379
  14.7 1.6 %shard_map.86 = (f32[128,128]{1,0:T(8,128)S(1)}, f32[16,128]{1,0:T(8,128)S(1)}) custom-call(s32[16,128]{1,0:T(8,128)S(1)} %bitcast.17, s32[16,128]{1,0:T(8,128)S(1)} %bitcast.21, f32[16,128]{1,0:T(8,128)S(1)} %bitcast.19, f32[16,128]{1,0:T(8,128)S(1)} %bitcast.22), custom_call_target="tpu_custom_call" | custom-call | tf_op jit(solution)/shard_map/pallas_call | solution.py:24
  16.4 33.2 %all_to_all.33 = f32[128,1,128]{2,1,0:T(1,128)S(1)} all-to-all(f32[128,1,128]{2,1,0:T(1,128)S(1)} %bitcast.16), channel_id=1, replica_groups=mesh['lat'=8,'lon'=16,'mem'=4] {'lat','lon'}, dimensions={0} | all-to-all | bytes 131072 | tf_op jit(solution)/shard_map/all_to_all | solution.py:378
  49.6 0.9 shard_map.88
  50.6 0.0 copy-start.2
  50.6 7.3 %all_to_all.34.parts_ref = f32[4,64,128]{2,1,0:T(8,128)S(1)} all-to-all(f32[4,64,128]{2,1,0:T(8,128)S(1)} %get-tuple-element.28), channel_id=1, replica_groups=mesh['lat'=8,'lon'=16,'mem'=4] {'mem'}, dimensions={0} | all-to-all | bytes 262144 | tf_op jit(solution)/shard_map/all_to_all | solution.py:385
  57.9 0.1 shard_map.89
  58.0 2.1 %collective-permute-start.3 = (f32[4,8,640]{2,1,0:T(8,128)S(1)}, f32[4,8,640]{2,1,0:T(8,128)S(1)}, u32[]{:S(2)}, u32[]{:S(2)}) collective-permute-start(f32[4,8,640]{2,1,0:T(8,128)S(1)} %get-tuple-element.34), channel_id=1, source_target_pairs={{0,64},{64,128},{128,192},{192,256},{256,320},{320,384},{384,448},... | collective-permute-start | bytes 245768 | tf_op jit(solution)/shard_map/ppermute | solution.py:339
  60.1 1.5 %collective-permute-done.3.before_ref = f32[4,8,640]{2,1,0:T(8,128)S(1)} collective-permute-done((f32[4,8,640]{2,1,0:T(8,128)S(1)}, f32[4,8,640]{2,1,0:T(8,128)S(1)}, u32[]{:S(2)}, u32[]{:S(2)}) %collective-permute-start.3) | collective-permute-done | bytes 81952 | tf_op jit(solution)/shard_map/ppermute | solution.py:339
  61.6 2.7 %collective-permute-done.4.after_ref = f32[4,8,640]{2,1,0:T(8,128)S(1)} collective-permute-done((f32[4,8,640]{2,1,0:T(8,128)S(1)}, f32[4,8,640]{2,1,0:T(8,128)S(1)}, u32[]{:S(2)}, u32[]{:S(2)}) %collective-permute-start.4) | collective-permute-done | bytes 81952 | tf_op jit(solution)/shard_map/ppermute | solution.py:339
  64.3 0.8 shard_map.90
  65.1 2.5 %collective-permute-start.5 = (f32[80,384]{1,0:T(8,128)S(1)}, f32[80,384]{1,0:T(8,128)S(1)}, u32[]{:S(2)}, u32[]{:S(2)}) collective-permute-start(f32[80,384]{1,0:T(8,128)S(1)} %get-tuple-element.38), channel_id=1, source_target_pairs={{0,1},{2,3},{4,5},{6,7},{8,9},{10,11},{12,13},{14,15},{16,17},{18,... | collective-permute-start | bytes 368648 | tf_op jit(solution)/shard_map/ppermute | solution.py:348
  67.7 1.9 %collective-permute-start.6 = (f32[80,384]{1,0:T(8,128)S(1)}, f32[80,384]{1,0:T(8,128)S(1)}, u32[]{:S(2)}, u32[]{:S(2)}) collective-permute-start(f32[80,384]{1,0:T(8,128)S(1)} %get-tuple-element.39), channel_id=1, source_target_pairs={{1,2},{3,4},{5,6},{7,8},{9,10},{11,12},{13,14},{15,16},{17,18},{19... | collective-permute-start | bytes 368648 | tf_op jit(solution)/shard_map/ppermute | solution.py:348
  69.6 1.1 collective-permute-done.5.one_ref
  70.7 5.9 %collective-permute-done.6.two_ref = f32[80,384]{1,0:T(8,128)S(1)} collective-permute-done((f32[80,384]{1,0:T(8,128)S(1)}, f32[80,384]{1,0:T(8,128)S(1)}, u32[]{:S(2)}, u32[]{:S(2)}) %collective-permute-start.6) | collective-permute-done | bytes 122912 | tf_op jit(solution)/shard_map/ppermute | solution.py:348
  76.6 6.1 %shard_map.91 = f32[4,32,128]{2,1,0:T(8,128)S(1)} custom-call(f32[4,64,640]{2,1,0:T(8,128)S(1)} %get-tuple-element.33.mid_ref, f32[4,8,640]{2,1,0:T(8,128)S(1)} %get-tuple-element.36.north_ref, f32[4,8,640]{2,1,0:T(8,128)S(1)} %get-tuple-element.37.south_ref, f32[80,384]{1,0:T(8,128)S(1)} %collective-permute-done.5.one_ref, ...), custom_call_target="tpu_custom_call" | custom-call | tf_op jit(solution)/shard_map/pallas_call | solution.py:24
  82.7 7.0 %all_to_all.35.pieces_ref = f32[4,32,128]{2,1,0:T(8,128)S(1)} all-to-all(f32[4,32,128]{2,1,0:T(8,128)S(1)} %shard_map.91), channel_id=1, replica_groups=mesh['lat'=8,'lon'=16,'mem'=4] {'mem'}, dimensions={0} | all-to-all | bytes 131072 | tf_op jit(solution)/shard_map/all_to_all | solution.py:416
  89.7 1.4 %shard_map.92 = (f32[64,256]{1,0:T(8,128)}, f32[128,32]{1,0:T(8,128)S(1)}) custom-call(f32[4,32,128]{2,1,0:T(8,128)S(1)} %all_to_all.35.pieces_ref, f32[128,128]{1,0:T(8,128)S(1)} %get-tuple-element.40.turned_ref), custom_call_target="tpu_custom_call" | custom-call | tf_op jit(solution)/shard_map/pallas_call | solution.py:24
  91.0 23.0 %all_to_all.36 = f32[128,1,32]{2,1,0:T(1,128)S(1)} all-to-all(f32[128,1,32]{2,1,0:T(1,128)S(1)} %bitcast.15), channel_id=1, replica_groups=mesh['lat'=8,'lon'=16,'mem'=4] {'lat','lon'}, dimensions={0} | all-to-all | bytes 32768 | tf_op jit(solution)/shard_map/all_to_all | solution.py:420
  114.0 1.0 shard_map.93
  (16 shorter events, 0.0 us)
Async XLA Ops:
  0.6 1.0 copy-start
  1.6 13.1 %copy-start.4 = (f32[2048]{0:T(1024)S(1)}, f32[2048]{0:T(1024)}, u32[]{:S(2)}) copy-start(f32[2048]{0:T(1024)} %param.12) | copy-start | bytes 24580
  1.6 13.1 %copy-start.5 = (s32[2048]{0:T(1024)S(1)}, s32[2048]{0:T(1024)}, u32[]{:S(2)}) copy-start(s32[2048]{0:T(1024)} %param.11) | copy-start | bytes 24580
  1.6 13.1 %copy-start.6 = (f32[2048]{0:T(1024)S(1)}, f32[2048]{0:T(1024)}, u32[]{:S(2)}) copy-start(f32[2048]{0:T(1024)} %param.13) | copy-start | bytes 24580
  1.8 12.9 %copy-start.3 = (s32[2048,1]{0,1:T(1,128)S(1)}, s32[2048,1]{0,1:T(1,128)}, u32[]{:S(2)}) copy-start(s32[2048,1]{0,1:T(1,128)} %param.10) | copy-start | bytes 24580
  1.8 47.8 %collective-permute-start = (f32[64,512]{1,0:T(8,128)S(1)}, f32[64,512]{1,0:T(8,128)S(1)}, u32[]{:S(2)}, u32[]{:S(2)}) collective-permute-start(f32[64,512]{1,0:T(8,128)S(1)} %get-tuple-element.24), channel_id=1, source_target_pairs={{0,1},{1,2},{2,3},{3,0},{4,5},{5,6},{6,7},{7,4},{8,9},{9,10},{10,1... | collective-permute-start | bytes 393224 | tf_op jit(solution)/shard_map/ppermute | solution.py:379
  6.7 43.0 %collective-permute-start.1 = (f32[64,512]{1,0:T(8,128)S(1)}, f32[64,512]{1,0:T(8,128)S(1)}, u32[]{:S(2)}, u32[]{:S(2)}) collective-permute-start(f32[64,512]{1,0:T(8,128)S(1)} %get-tuple-element.25), channel_id=1, source_target_pairs={{0,2},{1,3},{2,0},{3,1},{4,6},{5,7},{6,4},{7,5},{8,10},{9,11},{10,... | collective-permute-start | bytes 393224 | tf_op jit(solution)/shard_map/ppermute | solution.py:379
  12.5 37.1 %collective-permute-start.2 = (f32[64,512]{1,0:T(8,128)S(1)}, f32[64,512]{1,0:T(8,128)S(1)}, u32[]{:S(2)}, u32[]{:S(2)}) collective-permute-start(f32[64,512]{1,0:T(8,128)S(1)} %get-tuple-element.26), channel_id=1, source_target_pairs={{0,3},{1,0},{2,1},{3,2},{4,7},{5,4},{6,5},{7,6},{8,11},{9,8},{10,9... | collective-permute-start | bytes 393224 | tf_op jit(solution)/shard_map/ppermute | solution.py:379
  50.6 7.3 %copy-start.1 = (f32[64,256]{1,0:T(8,128)S(1)}, f32[64,256]{1,0:T(8,128)}, u32[]{:S(2)}) copy-start(f32[64,256]{1,0:T(8,128)} %rate_ref.1) | copy-start | bytes 196612
  50.6 7.3 %copy-start.2 = (s32[64,256]{1,0:T(8,128)S(1)}, s32[64,256]{1,0:T(8,128)}, u32[]{:S(2)}) copy-start(s32[64,256]{1,0:T(8,128)} %sea_ref.1) | copy-start | bytes 196612
  58.0 3.6 %collective-permute-start.3 = (f32[4,8,640]{2,1,0:T(8,128)S(1)}, f32[4,8,640]{2,1,0:T(8,128)S(1)}, u32[]{:S(2)}, u32[]{:S(2)}) collective-permute-start(f32[4,8,640]{2,1,0:T(8,128)S(1)} %get-tuple-element.34), channel_id=1, source_target_pairs={{0,64},{64,128},{128,192},{192,256},{256,320},{320,384},{384,448},... | collective-permute-start | bytes 245768 | tf_op jit(solution)/shard_map/ppermute | solution.py:339
  60.1 4.2 %collective-permute-start.4 = (f32[4,8,640]{2,1,0:T(8,128)S(1)}, f32[4,8,640]{2,1,0:T(8,128)S(1)}, u32[]{:S(2)}, u32[]{:S(2)}) collective-permute-start(f32[4,8,640]{2,1,0:T(8,128)S(1)} %get-tuple-element.35), channel_id=1, source_target_pairs={{64,0},{128,64},{192,128},{256,192},{320,256},{384,320},{448,384},... | collective-permute-start | bytes 245768 | tf_op jit(solution)/shard_map/ppermute | solution.py:339
  65.1 5.6 %collective-permute-start.5 = (f32[80,384]{1,0:T(8,128)S(1)}, f32[80,384]{1,0:T(8,128)S(1)}, u32[]{:S(2)}, u32[]{:S(2)}) collective-permute-start(f32[80,384]{1,0:T(8,128)S(1)} %get-tuple-element.38), channel_id=1, source_target_pairs={{0,1},{2,3},{4,5},{6,7},{8,9},{10,11},{12,13},{14,15},{16,17},{18,... | collective-permute-start | bytes 368648 | tf_op jit(solution)/shard_map/ppermute | solution.py:348
  67.7 8.9 %collective-permute-start.6 = (f32[80,384]{1,0:T(8,128)S(1)}, f32[80,384]{1,0:T(8,128)S(1)}, u32[]{:S(2)}, u32[]{:S(2)}) collective-permute-start(f32[80,384]{1,0:T(8,128)S(1)} %get-tuple-element.39), channel_id=1, source_target_pairs={{1,2},{3,4},{5,6},{7,8},{9,10},{11,12},{13,14},{15,16},{17,18},{19... | collective-permute-start | bytes 368648 | tf_op jit(solution)/shard_map/ppermute | solution.py:348

commit v5 on v4

--- a/solution.py
+++ b/solution.py
@@ -91,8 +91,10 @@
     out_ref[...] = packed[:, : 4 * SLOTS] + low
 
 
-def scatter_kernel(got_ref, out_ref, turned_ref):
+def scatter_kernel(got_ref, near_ref, far_ref, out_ref, turned_ref, passed_ref):
     rows, cols = 64, 256
+    passed_ref[0] = near_ref[...]
+    passed_ref[1] = far_ref[1]
     turned_ref[...] = got_ref[...].T
     width = turned_ref.shape[1]
     row_ids = lax.broadcasted_iota(I32, (rows, width), 0).astype(F32)
@@ -124,8 +126,7 @@
         out_ref[q, :, width:] = weight[:, q * width : (q + 1) * width]
 
 
-def quarter_kernel(members_ref, own_ref, *rest):
-    sent_refs, kept_ref = rest[:-1], rest[-1]
+def quarter_kernel(members_ref, own_ref, near_ref, far_ref, kept_ref):
     members = members_ref.shape[0]
     quarters = kept_ref.shape[0]
     width = members_ref.shape[2] // quarters
@@ -135,18 +136,20 @@
             kept_ref[q, :, k * width : (k + 1) * width] = value[:, q * width : (q + 1) * width]
     mine = lax.axis_index("mem")
     own_ref[...] = kept_ref[mine]
-    for k, ref in enumerate(sent_refs):
-        ref[...] = kept_ref[(mine + k + 1) % quarters]
+    near_ref[...] = kept_ref[mine ^ 1]
+    far_ref[0] = kept_ref[mine ^ 2]
+    far_ref[1] = kept_ref[mine ^ 3]
 
 
 def reduce_kernel(parts_ref, rate_ref, sea_ref, *rest):
     quarters = parts_ref.shape[0]
-    piece_refs, (mid_ref, top_ref, bottom_ref, kept_ref) = rest[:quarters], rest[quarters:]
-    rows, lanes = piece_refs[0].shape
+    own_ref, far_ref, near_ref, mid_ref, top_ref, bottom_ref, kept_ref = rest
+    piece_refs = (own_ref, near_ref.at[0], far_ref.at[0], near_ref.at[1])
+    rows, lanes = own_ref.shape
     width = parts_ref.shape[2] // 2
     mine = lax.axis_index("mem")
     for k in range(quarters):
-        mid_ref[(mine - k + quarters) % quarters, :, :lanes] = piece_refs[k][...]
+        mid_ref[mine ^ k, :, :lanes] = piece_refs[k][...]
     whole = parts_ref[0]
     for q in range(1, quarters):
         whole = whole + parts_ref[q]
@@ -362,12 +365,10 @@
     tiles = ("lat", "lon")
 
     piece = shape(rows, members * width)
-    own, *sent = call(quarter_kernel, [piece] * quarters, [pltpu.VMEM((quarters, rows, members * width), F32)])(
-        perturbations
-    )
-    ring = [
-        [(i, (i + k) % quarters) for i in range(quarters)] for k in range(1, quarters)
-    ]
+    pair = shape(2, rows, members * width)
+    own, near, far = call(
+        quarter_kernel, (piece, piece, pair), [pltpu.VMEM((quarters, rows, members * width), F32)]
+    )(perturbations)
     outgoing, rank = call(
         pack_kernel,
         (shape(places, LANES), shape(chunks, LANES)),
@@ -376,12 +377,13 @@
         place=AWAY,
     )(owner, cell, depart, weight)
     got = lax.all_to_all(outgoing, tiles, split_axis=0, concat_axis=0, tiled=True)
-    brought = [lax.ppermute(s, "mem", pairs) for s, pairs in zip(sent, ring)]
-    got, *brought = lax.optimization_barrier((got, *brought))
-
-    parts, turned = call(
-        scatter_kernel, (shape(quarters, rows, 2 * width), shape(LANES, places))
-    )(got)
+    far = lax.ppermute(far, "mem", [(i, i ^ 2) for i in range(quarters)])
+    got, far = lax.optimization_barrier((got, far))
+
+    parts, turned, passed = call(
+        scatter_kernel, (shape(quarters, rows, 2 * width), shape(LANES, places), pair)
+    )(got, near, far)
+    near = lax.ppermute(passed, "mem", [(i, i ^ 1) for i in range(quarters)])
     parts = lax.all_to_all(parts, "mem", split_axis=0, concat_axis=0, tiled=True)
     field_lanes = members * width + 2 * width
     strip = shape(quarters, HALO, field_lanes)
@@ -389,7 +391,7 @@
         reduce_kernel,
         (shape(quarters, rows, field_lanes), strip, strip),
         [pltpu.VMEM((quarters, rows, 2 * width), F32)],
-    )(parts, diffusivity, sea_mask, own, *brought)
+    )(parts, diffusivity, sea_mask, own, far, near)
     north, south = shift(top, bottom, "lat")
     rim_lanes = -(-(quarters * members + 4) * HALO // LANES) * LANES
     rim = shape(height, rim_lanes)

time: 115 us -> 112 us (0.974)
  starting transfers between devices: 19.4 us -> 16.7 us
    ppermute x3 -> x2, starting transfers between devices: 12.8 us -> 9.74 us  [the longest x1 6.64 us: per_device(): far = lax.ppermute(far, 'mem', [(i, i ^ 2) for i in range(quarters)])]
  transfers between devices with their start and end apart: 7 -> 6, of which waited for: 4 -> 4; matrix products, arithmetic and copies ran while one was open for 0% -> 0% of each run, Pallas kernels for 1% -> 1%
where the time goes in v5:
time: 112 us
  blocking collectives  70.4 us (63%)
  starting transfers between devices  16.7 us (15%)
  Pallas kernels  12.1 us (11%)
  waiting for transfers between devices  11 us (10%)
    all_to_all x1, blocking collectives, per_device(): lax.all_to_all(outgoing, tiles, split_axis=0, concat_axis=0, tiled=True)  32.7 us
    all_to_all x1, blocking collectives, per_device(): lax.all_to_all(answers, tiles, split_axis=0, concat_axis=0, tiled=True)  23.5 us
    pallas_call x8, Pallas kernels, run(): pl.pallas_call(kernel, out_shape=outs, in_specs=[place] * len(operands),...  12.1 us
    all_to_all x1, blocking collectives, per_device(): lax.all_to_all(parts, 'mem', split_axis=0, concat_axis=0, tiled=True)  7.33 us
    all_to_all x1, blocking collectives, per_device(): lax.all_to_all(quarter, 'mem', split_axis=0, concat_axis=0, tiled=True)  6.96 us
    ppermute x1, starting transfers between devices, per_device(): far = lax.ppermute(far, 'mem', [(i, i ^ 2) for i in range(quarters)])  6.64 us
    ppermute x1, waiting for transfers between devices, exchange(): lax.ppermute(second, axes, both[1])  5.84 us
    ppermute x1, starting transfers between devices, per_device(): near = lax.ppermute(passed, 'mem', [(i, i ^ 1) for i in range(quarters)])  3.1 us
  transfers between devices with their start and end apart: 6, of which 4 were waited for; matrix products, arithmetic and copies ran while one was open for 0% of the time, Pallas kernels for 1%

profile of v5, /device:TPU:1, one launch (start us, length us, event | category | flops | bytes accessed | tf_op | source)
XLA Modules:
  0.0 112.0 jit_solution(11678539543149800323)
XLA Ops:
  0.6 0.9 copy-done
  1.6 0.2 shard_map.87
  1.8 0.0 copy-start.3
  1.8 6.6 %collective-permute-start = (f32[2,64,512]{2,1,0:T(8,128)S(1)}, f32[2,64,512]{2,1,0:T(8,128)S(1)}, u32[]{:S(2)}, u32[]{:S(2)}) collective-permute-start(f32[2,64,512]{2,1,0:T(8,128)S(1)} %get-tuple-element.22), channel_id=1, source_target_pairs={{0,2},{1,3},{2,0},{3,1},{4,6},{5,7},{6,4},{7,5},{8,10},{9,11},{10,... | collective-permute-start | bytes 786440 | tf_op jit(solution)/shard_map/ppermute | solution.py:380
  8.5 1.6 %shard_map.86 = (f32[128,128]{1,0:T(8,128)S(1)}, f32[16,128]{1,0:T(8,128)S(1)}) custom-call(s32[16,128]{1,0:T(8,128)S(1)} %bitcast.17, s32[16,128]{1,0:T(8,128)S(1)} %bitcast.21, f32[16,128]{1,0:T(8,128)S(1)} %bitcast.19, f32[16,128]{1,0:T(8,128)S(1)} %bitcast.22), custom_call_target="tpu_custom_call" | custom-call | tf_op jit(solution)/shard_map/pallas_call | solution.py:24
  10.2 32.7 %all_to_all.33 = f32[128,1,128]{2,1,0:T(1,128)S(1)} all-to-all(f32[128,1,128]{2,1,0:T(1,128)S(1)} %bitcast.16), channel_id=1, replica_groups=mesh['lat'=8,'lon'=16,'mem'=4] {'lat','lon'}, dimensions={0} | all-to-all | bytes 131072 | tf_op jit(solution)/shard_map/all_to_all | solution.py:379
  42.9 0.9 shard_map.88
  43.8 3.1 %collective-permute-start.1 = (f32[2,64,512]{2,1,0:T(8,128)S(1)}, f32[2,64,512]{2,1,0:T(8,128)S(1)}, u32[]{:S(2)}, u32[]{:S(2)}) collective-permute-start(f32[2,64,512]{2,1,0:T(8,128)S(1)} %get-tuple-element.28), channel_id=1, source_target_pairs={{0,1},{1,0},{2,3},{3,2},{4,5},{5,4},{6,7},{7,6},{8,9},{9,8},{10,11... | collective-permute-start | bytes 786440 | tf_op jit(solution)/shard_map/ppermute | solution.py:386
  46.9 0.0 copy-start.1
  46.9 7.3 %all_to_all.34.parts_ref = f32[4,64,128]{2,1,0:T(8,128)S(1)} all-to-all(f32[4,64,128]{2,1,0:T(8,128)S(1)} %get-tuple-element.26), channel_id=1, replica_groups=mesh['lat'=8,'lon'=16,'mem'=4] {'mem'}, dimensions={0} | all-to-all | bytes 262144 | tf_op jit(solution)/shard_map/all_to_all | solution.py:387
  54.3 0.1 shard_map.89
  54.4 2.3 %collective-permute-start.2 = (f32[4,8,640]{2,1,0:T(8,128)S(1)}, f32[4,8,640]{2,1,0:T(8,128)S(1)}, u32[]{:S(2)}, u32[]{:S(2)}) collective-permute-start(f32[4,8,640]{2,1,0:T(8,128)S(1)} %get-tuple-element.30), channel_id=1, source_target_pairs={{0,64},{64,128},{128,192},{192,256},{256,320},{320,384},{384,448},... | collective-permute-start | bytes 245768 | tf_op jit(solution)/shard_map/ppermute | solution.py:342
  56.7 1.5 %collective-permute-done.2.before_ref = f32[4,8,640]{2,1,0:T(8,128)S(1)} collective-permute-done((f32[4,8,640]{2,1,0:T(8,128)S(1)}, f32[4,8,640]{2,1,0:T(8,128)S(1)}, u32[]{:S(2)}, u32[]{:S(2)}) %collective-permute-start.2) | collective-permute-done | bytes 81952 | tf_op jit(solution)/shard_map/ppermute | solution.py:342
  58.2 2.7 %collective-permute-done.3.after_ref = f32[4,8,640]{2,1,0:T(8,128)S(1)} collective-permute-done((f32[4,8,640]{2,1,0:T(8,128)S(1)}, f32[4,8,640]{2,1,0:T(8,128)S(1)}, u32[]{:S(2)}, u32[]{:S(2)}) %collective-permute-start.3) | collective-permute-done | bytes 81952 | tf_op jit(solution)/shard_map/ppermute | solution.py:342
  60.9 0.8 shard_map.90
  61.7 2.5 %collective-permute-start.4 = (f32[80,384]{1,0:T(8,128)S(1)}, f32[80,384]{1,0:T(8,128)S(1)}, u32[]{:S(2)}, u32[]{:S(2)}) collective-permute-start(f32[80,384]{1,0:T(8,128)S(1)} %get-tuple-element.34), channel_id=1, source_target_pairs={{0,1},{2,3},{4,5},{6,7},{8,9},{10,11},{12,13},{14,15},{16,17},{18,... | collective-permute-start | bytes 368648 | tf_op jit(solution)/shard_map/ppermute | solution.py:351
  64.2 2.1 %collective-permute-start.5 = (f32[80,384]{1,0:T(8,128)S(1)}, f32[80,384]{1,0:T(8,128)S(1)}, u32[]{:S(2)}, u32[]{:S(2)}) collective-permute-start(f32[80,384]{1,0:T(8,128)S(1)} %get-tuple-element.35), channel_id=1, source_target_pairs={{1,2},{3,4},{5,6},{7,8},{9,10},{11,12},{13,14},{15,16},{17,18},{19... | collective-permute-start | bytes 368648 | tf_op jit(solution)/shard_map/ppermute | solution.py:351
  66.3 1.0 collective-permute-done.4.one_ref
  67.3 5.8 %collective-permute-done.5.two_ref = f32[80,384]{1,0:T(8,128)S(1)} collective-permute-done((f32[80,384]{1,0:T(8,128)S(1)}, f32[80,384]{1,0:T(8,128)S(1)}, u32[]{:S(2)}, u32[]{:S(2)}) %collective-permute-start.5) | collective-permute-done | bytes 122912 | tf_op jit(solution)/shard_map/ppermute | solution.py:351
  73.1 6.1 %shard_map.91 = f32[4,32,128]{2,1,0:T(8,128)S(1)} custom-call(f32[4,64,640]{2,1,0:T(8,128)S(1)} %get-tuple-element.29.mid_ref, f32[4,8,640]{2,1,0:T(8,128)S(1)} %get-tuple-element.32.north_ref, f32[4,8,640]{2,1,0:T(8,128)S(1)} %get-tuple-element.33.south_ref, f32[80,384]{1,0:T(8,128)S(1)} %collective-permute-done.4.one_ref, ...), custom_call_target="tpu_custom_call" | custom-call | tf_op jit(solution)/shard_map/pallas_call | solution.py:24
  79.2 7.0 %all_to_all.35.pieces_ref = f32[4,32,128]{2,1,0:T(8,128)S(1)} all-to-all(f32[4,32,128]{2,1,0:T(8,128)S(1)} %shard_map.91), channel_id=1, replica_groups=mesh['lat'=8,'lon'=16,'mem'=4] {'mem'}, dimensions={0} | all-to-all | bytes 131072 | tf_op jit(solution)/shard_map/all_to_all | solution.py:418
  86.2 1.4 %shard_map.92 = (f32[64,256]{1,0:T(8,128)}, f32[128,32]{1,0:T(8,128)S(1)}) custom-call(f32[4,32,128]{2,1,0:T(8,128)S(1)} %all_to_all.35.pieces_ref, f32[128,128]{1,0:T(8,128)S(1)} %get-tuple-element.36.turned_ref), custom_call_target="tpu_custom_call" | custom-call | tf_op jit(solution)/shard_map/pallas_call | solution.py:24
  87.6 23.5 %all_to_all.36 = f32[128,1,32]{2,1,0:T(1,128)S(1)} all-to-all(f32[128,1,32]{2,1,0:T(1,128)S(1)} %bitcast.15), channel_id=1, replica_groups=mesh['lat'=8,'lon'=16,'mem'=4] {'lat','lon'}, dimensions={0} | all-to-all | bytes 32768 | tf_op jit(solution)/shard_map/all_to_all | solution.py:422
  111.0 1.0 shard_map.93
  (14 shorter events, 0.0 us)
Async XLA Ops:
  0.6 1.0 copy-start
  1.6 6.9 %copy-start.4 = (f32[2048]{0:T(1024)S(1)}, f32[2048]{0:T(1024)}, u32[]{:S(2)}) copy-start(f32[2048]{0:T(1024)} %param.12) | copy-start | bytes 24580
  1.6 6.9 %copy-start.5 = (s32[2048]{0:T(1024)S(1)}, s32[2048]{0:T(1024)}, u32[]{:S(2)}) copy-start(s32[2048]{0:T(1024)} %param.11) | copy-start | bytes 24580
  1.6 6.9 %copy-start.6 = (f32[2048]{0:T(1024)S(1)}, f32[2048]{0:T(1024)}, u32[]{:S(2)}) copy-start(f32[2048]{0:T(1024)} %param.13) | copy-start | bytes 24580
  1.8 6.7 %copy-start.3 = (s32[2048,1]{0,1:T(1,128)S(1)}, s32[2048,1]{0,1:T(1,128)}, u32[]{:S(2)}) copy-start(s32[2048,1]{0,1:T(1,128)} %param.10) | copy-start | bytes 24580
  1.8 41.0 %collective-permute-start = (f32[2,64,512]{2,1,0:T(8,128)S(1)}, f32[2,64,512]{2,1,0:T(8,128)S(1)}, u32[]{:S(2)}, u32[]{:S(2)}) collective-permute-start(f32[2,64,512]{2,1,0:T(8,128)S(1)} %get-tuple-element.22), channel_id=1, source_target_pairs={{0,2},{1,3},{2,0},{3,1},{4,6},{5,7},{6,4},{7,5},{8,10},{9,11},{10,... | collective-permute-start | bytes 786440 | tf_op jit(solution)/shard_map/ppermute | solution.py:380
  43.8 10.5 %collective-permute-start.1 = (f32[2,64,512]{2,1,0:T(8,128)S(1)}, f32[2,64,512]{2,1,0:T(8,128)S(1)}, u32[]{:S(2)}, u32[]{:S(2)}) collective-permute-start(f32[2,64,512]{2,1,0:T(8,128)S(1)} %get-tuple-element.28), channel_id=1, source_target_pairs={{0,1},{1,0},{2,3},{3,2},{4,5},{5,4},{6,7},{7,6},{8,9},{9,8},{10,11... | collective-permute-start | bytes 786440 | tf_op jit(solution)/shard_map/ppermute | solution.py:386
  46.9 7.4 %copy-start.1 = (f32[64,256]{1,0:T(8,128)S(1)}, f32[64,256]{1,0:T(8,128)}, u32[]{:S(2)}) copy-start(f32[64,256]{1,0:T(8,128)} %rate_ref.1) | copy-start | bytes 196612
  46.9 7.3 %copy-start.2 = (s32[64,256]{1,0:T(8,128)S(1)}, s32[64,256]{1,0:T(8,128)}, u32[]{:S(2)}) copy-start(s32[64,256]{1,0:T(8,128)} %sea_ref.1) | copy-start | bytes 196612
  54.4 3.8 %collective-permute-start.2 = (f32[4,8,640]{2,1,0:T(8,128)S(1)}, f32[4,8,640]{2,1,0:T(8,128)S(1)}, u32[]{:S(2)}, u32[]{:S(2)}) collective-permute-start(f32[4,8,640]{2,1,0:T(8,128)S(1)} %get-tuple-element.30), channel_id=1, source_target_pairs={{0,64},{64,128},{128,192},{192,256},{256,320},{320,384},{384,448},... | collective-permute-start | bytes 245768 | tf_op jit(solution)/shard_map/ppermute | solution.py:342
  56.7 4.2 %collective-permute-start.3 = (f32[4,8,640]{2,1,0:T(8,128)S(1)}, f32[4,8,640]{2,1,0:T(8,128)S(1)}, u32[]{:S(2)}, u32[]{:S(2)}) collective-permute-start(f32[4,8,640]{2,1,0:T(8,128)S(1)} %get-tuple-element.31), channel_id=1, source_target_pairs={{64,0},{128,64},{192,128},{256,192},{320,256},{384,320},{448,384},... | collective-permute-start | bytes 245768 | tf_op jit(solution)/shard_map/ppermute | solution.py:342
  61.7 5.6 %collective-permute-start.4 = (f32[80,384]{1,0:T(8,128)S(1)}, f32[80,384]{1,0:T(8,128)S(1)}, u32[]{:S(2)}, u32[]{:S(2)}) collective-permute-start(f32[80,384]{1,0:T(8,128)S(1)} %get-tuple-element.34), channel_id=1, source_target_pairs={{0,1},{2,3},{4,5},{6,7},{8,9},{10,11},{12,13},{14,15},{16,17},{18,... | collective-permute-start | bytes 368648 | tf_op jit(solution)/shard_map/ppermute | solution.py:351
  64.2 8.9 %collective-permute-start.5 = (f32[80,384]{1,0:T(8,128)S(1)}, f32[80,384]{1,0:T(8,128)S(1)}, u32[]{:S(2)}, u32[]{:S(2)}) collective-permute-start(f32[80,384]{1,0:T(8,128)S(1)} %get-tuple-element.35), channel_id=1, source_target_pairs={{1,2},{3,4},{5,6},{7,8},{9,10},{11,12},{13,14},{15,16},{17,18},{19... | collective-permute-start | bytes 368648 | tf_op jit(solution)/shard_map/ppermute | solution.py:351

commit v6 on v5

--- a/solution.py
+++ b/solution.py
@@ -91,7 +91,7 @@
     out_ref[...] = packed[:, : 4 * SLOTS] + low
 
 
-def scatter_kernel(got_ref, near_ref, far_ref, out_ref, turned_ref, passed_ref):
+def scatter_kernel(got_ref, near_ref, far_ref, out_ref, turned_ref, passed_ref, wide_ref):
     rows, cols = 64, 256
     passed_ref[0] = near_ref[...]
     passed_ref[1] = far_ref[1]
@@ -120,20 +120,35 @@
         total = total + nt_dot(jnp.concatenate(left, axis=1), jnp.concatenate(right, axis=1))
     product = total[:rows] + total[rows : 2 * rows]
     weight = total[2 * rows : 3 * rows] + total[3 * rows :]
-    quarters, width = out_ref.shape[0], out_ref.shape[2] // 2
+    quarters = out_ref.shape[0]
+    width = cols // quarters
+    wide_ref[...] = jnp.zeros(wide_ref.shape, F32)
+    for f, field in enumerate((product, weight)):
+        wide_ref[f, :, HALO : HALO + cols] = field
+        for q in range(quarters):
+            out_ref[q, :rows, f * width : (f + 1) * width] = field[:, q * width : (q + 1) * width]
+            low, high = q * width, (q + 1) * width + HALO
+            for b in range(4):
+                block, lane = slice(16 * b, 16 * (b + 1)), 32 * b + 2 * HALO * f
+                out_ref[q, rows:, lane : lane + HALO] = wide_ref[f, block, low : low + HALO]
+                out_ref[q, rows:, lane + HALO : lane + 2 * HALO] = wide_ref[f, block, high : high + HALO]
+
+
+def cut_quarters(value, wide_ref, kept_ref, low):
+    quarters, cols = kept_ref.shape[0], value.shape[1]
+    width = cols // quarters
+    span = width + 2 * HALO
+    wide_ref[:, HALO : HALO + cols] = value
     for q in range(quarters):
-        out_ref[q, :, :width] = product[:, q * width : (q + 1) * width]
-        out_ref[q, :, width:] = weight[:, q * width : (q + 1) * width]
-
-
-def quarter_kernel(members_ref, own_ref, near_ref, far_ref, kept_ref):
+        kept_ref[q, :, low : low + span] = wide_ref[:, q * width : q * width + span]
+
+
+def quarter_kernel(members_ref, own_ref, near_ref, far_ref, kept_ref, wide_ref):
     members = members_ref.shape[0]
-    quarters = kept_ref.shape[0]
-    width = members_ref.shape[2] // quarters
+    span = kept_ref.shape[2] // members
+    wide_ref[...] = jnp.zeros(wide_ref.shape, F32)
     for k in range(members):
-        value = members_ref[k].astype(F32)
-        for q in range(quarters):
-            kept_ref[q, :, k * width : (k + 1) * width] = value[:, q * width : (q + 1) * width]
+        cut_quarters(members_ref[k].astype(F32), wide_ref, kept_ref, k * span)
     mine = lax.axis_index("mem")
     own_ref[...] = kept_ref[mine]
     near_ref[...] = kept_ref[mine ^ 1]
@@ -143,63 +158,63 @@
 
 def reduce_kernel(parts_ref, rate_ref, sea_ref, *rest):
     quarters = parts_ref.shape[0]
-    own_ref, far_ref, near_ref, mid_ref, top_ref, bottom_ref, kept_ref = rest
+    own_ref, far_ref, near_ref, mid_ref, top_ref, bottom_ref, kept_ref, wide_ref, whole_ref = rest
     piece_refs = (own_ref, near_ref.at[0], far_ref.at[0], near_ref.at[1])
     rows, lanes = own_ref.shape
-    width = parts_ref.shape[2] // 2
+    width = rate_ref.shape[1] // quarters
+    span = width + 2 * HALO
     mine = lax.axis_index("mem")
+    mid_ref[:, :, lanes:] = jnp.zeros((quarters, rows, mid_ref.shape[2] - lanes), F32)
     for k in range(quarters):
         mid_ref[mine ^ k, :, :lanes] = piece_refs[k][...]
     whole = parts_ref[0]
     for q in range(1, quarters):
         whole = whole + parts_ref[q]
-    mid_ref[0, :, lanes:] = whole
+    whole_ref[...] = whole
+    for f in range(2):
+        low = lanes + f * span
+        mid_ref[0, :, low + HALO : low + HALO + width] = whole_ref[:rows, f * width : (f + 1) * width]
+        for b in range(4):
+            block, lane = slice(16 * b, 16 * (b + 1)), 32 * b + 2 * HALO * f
+            mid_ref[0, block, low : low + HALO] = whole_ref[rows:, lane : lane + HALO]
+            mid_ref[0, block, low + HALO + width : low + span] = whole_ref[rows:, lane + HALO : lane + 2 * HALO]
+    wide_ref[...] = jnp.zeros(wide_ref.shape, F32)
+    cut_quarters(rate_ref[...], wide_ref, kept_ref, 0)
+    cut_quarters(sea_ref[...].astype(F32), wide_ref, kept_ref, span)
+    mid_ref[1, :, lanes : lanes + 2 * span] = kept_ref[mine, :, : 2 * span]
     for q in range(quarters):
-        at = slice(q * width, (q + 1) * width)
-        kept_ref[q, :, :width] = rate_ref[:, at]
-        kept_ref[q, :, width:] = sea_ref[:, at].astype(F32)
-    mid_ref[1, :, lanes:] = kept_ref[mine]
-    for q in range(quarters):
-        size = lanes if q > 1 else lanes + 2 * width
-        top_ref[q, :, :size] = mid_ref[q, :HALO, :size]
-        bottom_ref[q, :, :size] = mid_ref[q, rows - HALO :, :size]
-        if size < top_ref.shape[2]:
-            top_ref[q, :, size:] = jnp.zeros((HALO, 2 * width), F32)
-            bottom_ref[q, :, size:] = jnp.zeros((HALO, 2 * width), F32)
-
-
-def fields_of(ref, width):
-    quarters, lanes = ref.shape[0], ref.shape[2] - 2 * width
-    places = [(q, k * width) for q in range(quarters) for k in range(lanes // width)]
-    return places + [(0, lanes), (0, lanes + width), (1, lanes), (1, lanes + width)]
-
-
-def rim_kernel(
-    mid_ref, before_ref, after_ref, one_ref, two_ref, north_ref, south_ref, first_ref, last_ref, *, width
-):
-    rows, lanes = mid_ref.shape[1], mid_ref.shape[2]
-    lat = lax.axis_index("lat")
+        top_ref[q] = mid_ref[q, :HALO, :]
+        bottom_ref[q] = mid_ref[q, rows - HALO :, :]
+
+
+def fields_of(quarters, lanes, span):
+    places = [(q, k) for q in range(quarters) for k in range(0, lanes, span)]
+    return places + [(0, lanes), (0, lanes + span), (1, lanes), (1, lanes + span)]
+
+
+def rim_kernel(mid_ref, before_ref, after_ref, out_ref, north_ref, south_ref, *, lanes, span):
+    quarters, rows = mid_ref.shape[:2]
+    lat, mine = lax.axis_index("lat"), lax.axis_index("mem")
     north_ref[...] = before_ref[...]
     south_ref[...] = after_ref[...]
-    sea = slice(lanes - width, lanes)
+    sea = slice(lanes + span, lanes + 2 * span)
     north_ref[1, :, sea] = jnp.where(lat == 0, 0.0, north_ref[1, :, sea])
     south_ref[1, :, sea] = jnp.where(lat == lax.axis_size("lat") - 1, 0.0, south_ref[1, :, sea])
-    first_ref[...] = jnp.zeros(first_ref.shape, F32)
-    last_ref[...] = jnp.zeros(last_ref.shape, F32)
-    for k, (q, lane) in enumerate(fields_of(mid_ref, width)):
-        at = slice(k * HALO, (k + 1) * HALO)
-        for ref, cut in ((first_ref, lane), (last_ref, lane + width - HALO)):
-            ref[:HALO, at] = north_ref[q, :, cut : cut + HALO]
-            ref[HALO : HALO + rows, at] = mid_ref[q, :, cut : cut + HALO]
-            ref[HALO + rows :, at] = south_ref[q, :, cut : cut + HALO]
-    even = lax.axis_index("mem") % 2 == 0
-    one_ref[...] = jnp.where(even, last_ref[...], first_ref[...])
-    two_ref[...] = jnp.where(even, first_ref[...], last_ref[...])
+    out_ref[...] = jnp.zeros(out_ref.shape, F32)
+    for edge, offset in ((0, HALO), (quarters - 1, span - 2 * HALO)):
+
+        @pl.when(mine == edge)
+        def _():
+            for k, (q, lane) in enumerate(fields_of(quarters, lanes, span)):
+                at, cut = slice(k * HALO, (k + 1) * HALO), slice(lane + offset, lane + offset + HALO)
+                out_ref[:HALO, at] = north_ref[q, :, cut]
+                out_ref[HALO : HALO + rows, at] = mid_ref[q, :, cut]
+                out_ref[HALO + rows :, at] = south_ref[q, :, cut]
 
 
 def product_kernel(
-    mid_ref, north_ref, south_ref, one_ref, two_ref, out_ref,
-    members_ref, state_ref, weights_ref, tiled_ref, field_ref, west_ref, east_ref,
+    mid_ref, north_ref, south_ref, got_ref, out_ref,
+    members_ref, state_ref, weights_ref, tiled_ref, field_ref,
 ):
     groups, height, lanes = members_ref.shape
     rows = height - 2 * HALO
@@ -214,22 +229,25 @@
             tiled_ref[:, k * span : (k + 1) * span] = value
         return tiled_ref[...]
 
-    even = lax.axis_index("mem") % 2 == 0
-    west_ref[...] = jnp.where(even, two_ref[...], one_ref[...])
-    east_ref[...] = jnp.where(even, one_ref[...], two_ref[...])
-    for k, (q, lane) in enumerate(fields_of(mid_ref, width)):
-        rim = slice(k * HALO, (k + 1) * HALO)
-        cut = slice(lane, lane + width)
-        north, south = north_ref[q, :, cut], south_ref[q, :, cut]
-        if k < groups * windows:
-            ref, low = members_ref.at[k // windows], k % windows * span
-        else:
-            ref, low = field_ref.at[k - groups * windows], 0
-        ref[:, low : low + HALO] = west_ref[:, rim]
-        ref[:HALO, low + HALO : low + HALO + width] = north
-        ref[HALO : HALO + rows, low + HALO : low + HALO + width] = mid_ref[q, :, cut]
-        ref[HALO + rows :, low + HALO : low + HALO + width] = south
-        ref[:, low + HALO + width : low + span] = east_ref[:, rim]
+    inner = slice(HALO, HALO + rows)
+    for g in range(groups):
+        for part_ref, at in ((north_ref, slice(0, HALO)), (mid_ref, inner), (south_ref, slice(HALO + rows, height))):
+            members_ref[g, at, :] = part_ref[g, :, :lanes]
+            if g < 2:
+                for f in range(2):
+                    low = lanes + f * span
+                    field_ref[2 * g + f, at, :span] = part_ref[g, :, low : low + span]
+    mine = lax.axis_index("mem")
+    for edge, offset in ((0, 0), (lax.axis_size("mem") - 1, span - HALO)):
+
+        @pl.when(mine == edge)
+        def _():
+            for k in range(groups * windows + 4):
+                other = k - groups * windows
+                ref = members_ref.at[k // windows] if other < 0 else field_ref.at[other]
+                low = (k % windows * span if other < 0 else 0) + offset
+                ref[:, low : low + HALO] = got_ref[:, k * HALO : (k + 1) * HALO]
+
     innovation = field_ref[0, :, :span]
     weight_sum = field_ref[1, :, :span]
     sea_cover = field_ref[3, :, :span]
@@ -342,15 +360,6 @@
     return lax.ppermute(last, axis, up), lax.ppermute(first, axis, [(j, i) for i, j in up])
 
 
-def exchange(first, second, axes):
-    size = 1
-    for axis in axes:
-        size *= lax.axis_size(axis)
-    swaps = [[(i + k, (i + k + 1) % size) for i in range(0, size, 2)] for k in range(2)]
-    both = [pairs + [(j, i) for i, j in pairs] for pairs in swaps]
-    return lax.ppermute(first, axes, both[0]), lax.ppermute(second, axes, both[1])
-
-
 def per_device(perturbations, diffusivity, sea_mask, obs_owner, obs_cell, obs_depart, obs_weight):
     members, rows, cols = perturbations.shape
     quarters = lax.axis_size("mem")
@@ -364,10 +373,12 @@
     )
     tiles = ("lat", "lon")
 
-    piece = shape(rows, members * width)
-    pair = shape(2, rows, members * width)
+    lanes = members * span
+    piece = shape(rows, lanes)
+    pair = shape(2, rows, lanes)
+    wide = pltpu.VMEM((rows, cols + LANES), F32)
     own, near, far = call(
-        quarter_kernel, (piece, piece, pair), [pltpu.VMEM((quarters, rows, members * width), F32)]
+        quarter_kernel, (piece, piece, pair), [pltpu.VMEM((quarters, rows, lanes), F32), wide]
     )(perturbations)
     outgoing, rank = call(
         pack_kernel,
@@ -381,27 +392,32 @@
     got, far = lax.optimization_barrier((got, far))
 
     parts, turned, passed = call(
-        scatter_kernel, (shape(quarters, rows, 2 * width), shape(LANES, places), pair)
+        scatter_kernel,
+        (shape(quarters, rows + 2 * HALO, 2 * width), shape(LANES, places), pair),
+        [pltpu.VMEM((2, rows, cols + LANES), F32)],
     )(got, near, far)
     near = lax.ppermute(passed, "mem", [(i, i ^ 1) for i in range(quarters)])
     parts = lax.all_to_all(parts, "mem", split_axis=0, concat_axis=0, tiled=True)
-    field_lanes = members * width + 2 * width
+    field_lanes = lanes + 2 * LANES
     strip = shape(quarters, HALO, field_lanes)
     mid, top, bottom = call(
         reduce_kernel,
         (shape(quarters, rows, field_lanes), strip, strip),
-        [pltpu.VMEM((quarters, rows, 2 * width), F32)],
+        [
+            pltpu.VMEM((quarters, rows, 2 * LANES), F32),
+            wide,
+            pltpu.VMEM((rows + 2 * HALO, 2 * width), F32),
+        ],
     )(parts, diffusivity, sea_mask, own, far, near)
     north, south = shift(top, bottom, "lat")
     rim_lanes = -(-(quarters * members + 4) * HALO // LANES) * LANES
-    rim = shape(height, rim_lanes)
-    one, two, north, south = call(
-        functools.partial(rim_kernel, width=width),
-        (rim, rim, strip, strip),
-        [pltpu.VMEM((height, rim_lanes), F32)] * 2,
+    edge, north, south = call(
+        functools.partial(rim_kernel, lanes=lanes, span=span),
+        (shape(height, rim_lanes), strip, strip),
     )(mid, north, south)
-    one, two = exchange(one, two, ("lon", "mem"))
-    lanes = members * span
+    devices = lax.axis_size("lon") * quarters
+    ends = [(i - 1, i % devices) for i in range(quarters, devices + 1, quarters)]
+    got = lax.ppermute(edge, ("lon", "mem"), ends + [(j, i) for i, j in ends])
     quarter = call(
         product_kernel,
         shape(quarters, rows // 2, 2 * width),
@@ -411,10 +427,8 @@
             pltpu.VMEM((5, height, lanes), F32),
             pltpu.VMEM((height, lanes), F32),
             pltpu.VMEM((4, height, LANES), F32),
-            pltpu.VMEM((height, rim_lanes), F32),
-            pltpu.VMEM((height, rim_lanes), F32),
         ],
-    )(mid, north, south, one, two)
+    )(mid, north, south, got)
     quarter = lax.all_to_all(quarter, "mem", split_axis=0, concat_axis=0, tiled=True)
     increment, answers = call(
         answer_kernel, (shape(rows, cols), shape(places, SLOTS)), [pltpu.VMEM((LANES, places), F32)]

time: 112 us -> 112 us (level)
  starting transfers between devices: 16.7 us -> 13.6 us
  blocking collectives: 70.4 us -> 73.1 us
    all_to_all x1, blocking collectives: 7.33 us -> 10 us  [per_device(): lax.all_to_all(parts, 'mem', split_axis=0, concat_axis=0, tiled=True)]
    ppermute x2 -> x1, starting transfers between devices: 4.62 us -> 2.34 us  [per_device(): got = lax.ppermute(edge, ('lon', 'mem'), ends + [(j, i) for i, j in ends])]
    ppermute x2 -> x1, waiting for transfers between devices: 6.83 us -> 6.59 us  [per_device(): got = lax.ppermute(edge, ('lon', 'mem'), ends + [(j, i) for i, j in ends])]
  transfers between devices with their start and end apart: 6 -> 5, of which waited for: 4 -> 3; matrix products, arithmetic and copies ran while one was open for 0% -> 0% of each run, Pallas kernels for 1% -> 1%
where the time goes in v6:
time: 112 us
  blocking collectives  73.1 us (65%)
  starting transfers between devices  13.6 us (12%)
  Pallas kernels  12.2 us (11%)
  waiting for transfers between devices  11.1 us (10%)
    all_to_all x1, blocking collectives, per_device(): lax.all_to_all(outgoing, tiles, split_axis=0, concat_axis=0, tiled=True)  32.7 us
    all_to_all x1, blocking collectives, per_device(): lax.all_to_all(answers, tiles, split_axis=0, concat_axis=0, tiled=True)  23.4 us
    pallas_call x8, Pallas kernels, run(): pl.pallas_call(kernel, out_shape=outs, in_specs=[place] * len(operands),...  12.2 us
    all_to_all x1, blocking collectives, per_device(): lax.all_to_all(parts, 'mem', split_axis=0, concat_axis=0, tiled=True)  10 us
    all_to_all x1, blocking collectives, per_device(): lax.all_to_all(quarter, 'mem', split_axis=0, concat_axis=0, tiled=True)  6.96 us
    ppermute x1, starting transfers between devices, per_device(): far = lax.ppermute(far, 'mem', [(i, i ^ 2) for i in range(quarters)])  6.64 us
    ppermute x1, waiting for transfers between devices, per_device(): got = lax.ppermute(edge, ('lon', 'mem'), ends + [(j, i) for i, j in ends])  6.59 us
    ppermute x1, starting transfers between devices, per_device(): near = lax.ppermute(passed, 'mem', [(i, i ^ 1) for i in range(quarters)])  3.1 us
  transfers between devices with their start and end apart: 5, of which 3 were waited for; matrix products, arithmetic and copies ran while one was open for 0% of the time, Pallas kernels for 1%

profile of v6, /device:TPU:1, one launch (start us, length us, event | category | flops | bytes accessed | tf_op | source)
XLA Modules:
  0.0 111.8 jit_solution(18009546391083118320)
XLA Ops:
  0.6 0.9 copy-done
  1.6 0.9 shard_map.87
  2.5 0.0 copy-start.3
  2.5 6.6 %collective-permute-start = (f32[2,64,640]{2,1,0:T(8,128)S(1)}, f32[2,64,640]{2,1,0:T(8,128)S(1)}, u32[]{:S(2)}, u32[]{:S(2)}) collective-permute-start(f32[2,64,640]{2,1,0:T(8,128)S(1)} %get-tuple-element.21), channel_id=1, source_target_pairs={{0,2},{1,3},{2,0},{3,1},{4,6},{5,7},{6,4},{7,5},{8,10},{9,11},{10,... | collective-permute-start | bytes 983048 | tf_op jit(solution)/shard_map/ppermute | solution.py:391
  9.2 1.6 %shard_map.86 = (f32[128,128]{1,0:T(8,128)S(1)}, f32[16,128]{1,0:T(8,128)S(1)}) custom-call(s32[16,128]{1,0:T(8,128)S(1)} %bitcast.17, s32[16,128]{1,0:T(8,128)S(1)} %bitcast.21, f32[16,128]{1,0:T(8,128)S(1)} %bitcast.19, f32[16,128]{1,0:T(8,128)S(1)} %bitcast.22), custom_call_target="tpu_custom_call" | custom-call | tf_op jit(solution)/shard_map/pallas_call | solution.py:24
  10.9 32.7 %all_to_all.33 = f32[128,1,128]{2,1,0:T(1,128)S(1)} all-to-all(f32[128,1,128]{2,1,0:T(1,128)S(1)} %bitcast.16), channel_id=1, replica_groups=mesh['lat'=8,'lon'=16,'mem'=4] {'lat','lon'}, dimensions={0} | all-to-all | bytes 131072 | tf_op jit(solution)/shard_map/all_to_all | solution.py:390
  43.6 0.0 collective-permute-done.far_ref.rest_1_
  43.6 1.1 shard_map.88
  44.7 3.1 %collective-permute-start.1 = (f32[2,64,640]{2,1,0:T(8,128)S(1)}, f32[2,64,640]{2,1,0:T(8,128)S(1)}, u32[]{:S(2)}, u32[]{:S(2)}) collective-permute-start(f32[2,64,640]{2,1,0:T(8,128)S(1)} %get-tuple-element.27), channel_id=1, source_target_pairs={{0,1},{1,0},{2,3},{3,2},{4,5},{5,4},{6,7},{7,6},{8,9},{9,8},{10,11... | collective-permute-start | bytes 983048 | tf_op jit(solution)/shard_map/ppermute | solution.py:399
  47.8 0.0 copy-start.1
  47.8 0.0 copy-start.2
  47.8 10.0 %all_to_all.34.parts_ref = f32[4,80,128]{2,1,0:T(8,128)S(1)} all-to-all(f32[4,80,128]{2,1,0:T(8,128)S(1)} %get-tuple-element.25), channel_id=1, replica_groups=mesh['lat'=8,'lon'=16,'mem'=4] {'mem'}, dimensions={0} | all-to-all | bytes 327680 | tf_op jit(solution)/shard_map/all_to_all | solution.py:400
  57.8 0.4 shard_map.89
  58.2 1.6 %collective-permute-start.2 = (f32[4,8,896]{2,1,0:T(8,128)S(1)}, f32[4,8,896]{2,1,0:T(8,128)S(1)}, u32[]{:S(2)}, u32[]{:S(2)}) collective-permute-start(f32[4,8,896]{2,1,0:T(8,128)S(1)} %get-tuple-element.29), channel_id=1, source_target_pairs={{0,64},{64,128},{128,192},{192,256},{256,320},{320,384},{384,448},... | collective-permute-start | bytes 344072 | tf_op jit(solution)/shard_map/ppermute | solution.py:360
  59.8 1.8 %collective-permute-done.2.before_ref = f32[4,8,896]{2,1,0:T(8,128)S(1)} collective-permute-done((f32[4,8,896]{2,1,0:T(8,128)S(1)}, f32[4,8,896]{2,1,0:T(8,128)S(1)}, u32[]{:S(2)}, u32[]{:S(2)}) %collective-permute-start.2) | collective-permute-done | bytes 114720 | tf_op jit(solution)/shard_map/ppermute | solution.py:360
  61.6 2.7 %collective-permute-done.3.after_ref = f32[4,8,896]{2,1,0:T(8,128)S(1)} collective-permute-done((f32[4,8,896]{2,1,0:T(8,128)S(1)}, f32[4,8,896]{2,1,0:T(8,128)S(1)}, u32[]{:S(2)}, u32[]{:S(2)}) %collective-permute-start.3) | collective-permute-done | bytes 114720 | tf_op jit(solution)/shard_map/ppermute | solution.py:360
  64.3 0.4 shard_map.90
  64.7 2.3 %collective-permute-start.4 = (f32[80,384]{1,0:T(8,128)S(1)}, f32[80,384]{1,0:T(8,128)S(1)}, u32[]{:S(2)}, u32[]{:S(2)}) collective-permute-start(f32[80,384]{1,0:T(8,128)S(1)} %get-tuple-element.33), channel_id=1, source_target_pairs={{3,4},{7,8},{11,12},{15,16},{19,20},{23,24},{27,28},{31,32},{35,36... | collective-permute-start | bytes 368648 | tf_op jit(solution)/shard_map/ppermute | solution.py:420
  67.1 6.6 %collective-permute-done.4.got_ref = f32[80,384]{1,0:T(8,128)S(1)} collective-permute-done((f32[80,384]{1,0:T(8,128)S(1)}, f32[80,384]{1,0:T(8,128)S(1)}, u32[]{:S(2)}, u32[]{:S(2)}) %collective-permute-start.4) | collective-permute-done | bytes 122912 | tf_op jit(solution)/shard_map/ppermute | solution.py:420
  73.7 5.4 %shard_map.91 = f32[4,32,128]{2,1,0:T(8,128)S(1)} custom-call(f32[4,64,896]{2,1,0:T(8,128)S(1)} %get-tuple-element.28.mid_ref, f32[4,8,896]{2,1,0:T(8,128)S(1)} %get-tuple-element.31.north_ref, f32[4,8,896]{2,1,0:T(8,128)S(1)} %get-tuple-element.32.south_ref, f32[80,384]{1,0:T(8,128)S(1)} %collective-permute-done.4.got_ref), custom_call_target="tpu_custom_call" | custom-call | tf_op jit(solution)/shard_map/pallas_call | solution.py:24
  79.1 7.0 %all_to_all.35.pieces_ref = f32[4,32,128]{2,1,0:T(8,128)S(1)} all-to-all(f32[4,32,128]{2,1,0:T(8,128)S(1)} %shard_map.91), channel_id=1, replica_groups=mesh['lat'=8,'lon'=16,'mem'=4] {'mem'}, dimensions={0} | all-to-all | bytes 131072 | tf_op jit(solution)/shard_map/all_to_all | solution.py:432
  86.1 1.4 %shard_map.92 = (f32[64,256]{1,0:T(8,128)}, f32[128,32]{1,0:T(8,128)S(1)}) custom-call(f32[4,32,128]{2,1,0:T(8,128)S(1)} %all_to_all.35.pieces_ref, f32[128,128]{1,0:T(8,128)S(1)} %get-tuple-element.34.turned_ref), custom_call_target="tpu_custom_call" | custom-call | tf_op jit(solution)/shard_map/pallas_call | solution.py:24
  87.5 23.4 %all_to_all.36 = f32[128,1,32]{2,1,0:T(1,128)S(1)} all-to-all(f32[128,1,32]{2,1,0:T(1,128)S(1)} %bitcast.15), channel_id=1, replica_groups=mesh['lat'=8,'lon'=16,'mem'=4] {'lat','lon'}, dimensions={0} | all-to-all | bytes 32768 | tf_op jit(solution)/shard_map/all_to_all | solution.py:436
  110.9 1.0 shard_map.93
  (12 shorter events, 0.0 us)
Async XLA Ops:
  0.6 1.0 copy-start
  1.6 7.6 %copy-start.4 = (f32[2048]{0:T(1024)S(1)}, f32[2048]{0:T(1024)}, u32[]{:S(2)}) copy-start(f32[2048]{0:T(1024)} %param.12) | copy-start | bytes 24580
  1.6 7.6 %copy-start.5 = (s32[2048]{0:T(1024)S(1)}, s32[2048]{0:T(1024)}, u32[]{:S(2)}) copy-start(s32[2048]{0:T(1024)} %param.11) | copy-start | bytes 24580
  1.6 7.6 %copy-start.6 = (f32[2048]{0:T(1024)S(1)}, f32[2048]{0:T(1024)}, u32[]{:S(2)}) copy-start(f32[2048]{0:T(1024)} %param.13) | copy-start | bytes 24580
  2.5 6.7 %copy-start.3 = (s32[2048,1]{0,1:T(1,128)S(1)}, s32[2048,1]{0,1:T(1,128)}, u32[]{:S(2)}) copy-start(s32[2048,1]{0,1:T(1,128)} %param.10) | copy-start | bytes 24580
  2.5 41.0 %collective-permute-start = (f32[2,64,640]{2,1,0:T(8,128)S(1)}, f32[2,64,640]{2,1,0:T(8,128)S(1)}, u32[]{:S(2)}, u32[]{:S(2)}) collective-permute-start(f32[2,64,640]{2,1,0:T(8,128)S(1)} %get-tuple-element.21), channel_id=1, source_target_pairs={{0,2},{1,3},{2,0},{3,1},{4,6},{5,7},{6,4},{7,5},{8,10},{9,11},{10,... | collective-permute-start | bytes 983048 | tf_op jit(solution)/shard_map/ppermute | solution.py:391
  44.7 13.2 %collective-permute-start.1 = (f32[2,64,640]{2,1,0:T(8,128)S(1)}, f32[2,64,640]{2,1,0:T(8,128)S(1)}, u32[]{:S(2)}, u32[]{:S(2)}) collective-permute-start(f32[2,64,640]{2,1,0:T(8,128)S(1)} %get-tuple-element.27), channel_id=1, source_target_pairs={{0,1},{1,0},{2,3},{3,2},{4,5},{5,4},{6,7},{7,6},{8,9},{9,8},{10,11... | collective-permute-start | bytes 983048 | tf_op jit(solution)/shard_map/ppermute | solution.py:399
  47.8 10.1 %copy-start.1 = (f32[64,256]{1,0:T(8,128)S(1)}, f32[64,256]{1,0:T(8,128)}, u32[]{:S(2)}) copy-start(f32[64,256]{1,0:T(8,128)} %rate_ref.1) | copy-start | bytes 196612
  47.8 10.0 %copy-start.2 = (s32[64,256]{1,0:T(8,128)S(1)}, s32[64,256]{1,0:T(8,128)}, u32[]{:S(2)}) copy-start(s32[64,256]{1,0:T(8,128)} %sea_ref.1) | copy-start | bytes 196612
  58.2 3.3 %collective-permute-start.2 = (f32[4,8,896]{2,1,0:T(8,128)S(1)}, f32[4,8,896]{2,1,0:T(8,128)S(1)}, u32[]{:S(2)}, u32[]{:S(2)}) collective-permute-start(f32[4,8,896]{2,1,0:T(8,128)S(1)} %get-tuple-element.29), channel_id=1, source_target_pairs={{0,64},{64,128},{128,192},{192,256},{256,320},{320,384},{384,448},... | collective-permute-start | bytes 344072 | tf_op jit(solution)/shard_map/ppermute | solution.py:360
  59.8 4.5 %collective-permute-start.3 = (f32[4,8,896]{2,1,0:T(8,128)S(1)}, f32[4,8,896]{2,1,0:T(8,128)S(1)}, u32[]{:S(2)}, u32[]{:S(2)}) collective-permute-start(f32[4,8,896]{2,1,0:T(8,128)S(1)} %get-tuple-element.30), channel_id=1, source_target_pairs={{64,0},{128,64},{192,128},{256,192},{320,256},{384,320},{448,384},... | collective-permute-start | bytes 344072 | tf_op jit(solution)/shard_map/ppermute | solution.py:360
  64.7 8.9 %collective-permute-start.4 = (f32[80,384]{1,0:T(8,128)S(1)}, f32[80,384]{1,0:T(8,128)S(1)}, u32[]{:S(2)}, u32[]{:S(2)}) collective-permute-start(f32[80,384]{1,0:T(8,128)S(1)} %get-tuple-element.33), channel_id=1, source_target_pairs={{3,4},{7,8},{11,12},{15,16},{19,20},{23,24},{27,28},{31,32},{35,36... | collective-permute-start | bytes 368648 | tf_op jit(solution)/shard_map/ppermute | solution.py:420

commit v7 on v6

--- a/solution.py
+++ b/solution.py
@@ -158,7 +158,7 @@
 
 def reduce_kernel(parts_ref, rate_ref, sea_ref, *rest):
     quarters = parts_ref.shape[0]
-    own_ref, far_ref, near_ref, mid_ref, top_ref, bottom_ref, kept_ref, wide_ref, whole_ref = rest
+    own_ref, far_ref, near_ref, mid_ref, out_ref, kept_ref, wide_ref, whole_ref = rest
     piece_refs = (own_ref, near_ref.at[0], far_ref.at[0], near_ref.at[1])
     rows, lanes = own_ref.shape
     width = rate_ref.shape[1] // quarters
@@ -182,34 +182,34 @@
     cut_quarters(rate_ref[...], wide_ref, kept_ref, 0)
     cut_quarters(sea_ref[...].astype(F32), wide_ref, kept_ref, span)
     mid_ref[1, :, lanes : lanes + 2 * span] = kept_ref[mine, :, : 2 * span]
+    out_ref[...] = jnp.zeros(out_ref.shape, F32)
+    for edge, offset in ((0, HALO), (quarters - 1, span - 2 * HALO)):
+
+        @pl.when(mine == edge)
+        def _():
+            for k, (q, lane) in enumerate(fields_of(quarters, lanes, span)):
+                out_ref[:, k * HALO : (k + 1) * HALO] = mid_ref[q, :, lane + offset : lane + offset + HALO]
+
+
+def fields_of(quarters, lanes, span):
+    places = [(q, k) for q in range(quarters) for k in range(0, lanes, span)]
+    return places + [(0, lanes), (0, lanes + span), (1, lanes), (1, lanes + span)]
+
+
+def rim_kernel(mid_ref, got_ref, top_ref, bottom_ref, *, lanes, span):
+    quarters, rows = mid_ref.shape[:2]
+    mine = lax.axis_index("mem")
     for q in range(quarters):
         top_ref[q] = mid_ref[q, :HALO, :]
         bottom_ref[q] = mid_ref[q, rows - HALO :, :]
-
-
-def fields_of(quarters, lanes, span):
-    places = [(q, k) for q in range(quarters) for k in range(0, lanes, span)]
-    return places + [(0, lanes), (0, lanes + span), (1, lanes), (1, lanes + span)]
-
-
-def rim_kernel(mid_ref, before_ref, after_ref, out_ref, north_ref, south_ref, *, lanes, span):
-    quarters, rows = mid_ref.shape[:2]
-    lat, mine = lax.axis_index("lat"), lax.axis_index("mem")
-    north_ref[...] = before_ref[...]
-    south_ref[...] = after_ref[...]
-    sea = slice(lanes + span, lanes + 2 * span)
-    north_ref[1, :, sea] = jnp.where(lat == 0, 0.0, north_ref[1, :, sea])
-    south_ref[1, :, sea] = jnp.where(lat == lax.axis_size("lat") - 1, 0.0, south_ref[1, :, sea])
-    out_ref[...] = jnp.zeros(out_ref.shape, F32)
-    for edge, offset in ((0, HALO), (quarters - 1, span - 2 * HALO)):
+    for edge, offset in ((0, 0), (quarters - 1, span - HALO)):
 
         @pl.when(mine == edge)
         def _():
             for k, (q, lane) in enumerate(fields_of(quarters, lanes, span)):
                 at, cut = slice(k * HALO, (k + 1) * HALO), slice(lane + offset, lane + offset + HALO)
-                out_ref[:HALO, at] = north_ref[q, :, cut]
-                out_ref[HALO : HALO + rows, at] = mid_ref[q, :, cut]
-                out_ref[HALO + rows :, at] = south_ref[q, :, cut]
+                top_ref[q, :, cut] = got_ref[:HALO, at]
+                bottom_ref[q, :, cut] = got_ref[rows - HALO :, at]
 
 
 def product_kernel(
@@ -246,7 +246,11 @@
                 other = k - groups * windows
                 ref = members_ref.at[k // windows] if other < 0 else field_ref.at[other]
                 low = (k % windows * span if other < 0 else 0) + offset
-                ref[:, low : low + HALO] = got_ref[:, k * HALO : (k + 1) * HALO]
+                ref[inner, low : low + HALO] = got_ref[:, k * HALO : (k + 1) * HALO]
+
+    lat = lax.axis_index("lat")
+    for at, end in ((slice(0, HALO), 0), (slice(HALO + rows, height), lax.axis_size("lat") - 1)):
+        field_ref[3, at, :span] = jnp.where(lat == end, 0.0, field_ref[3, at, :span])
 
     innovation = field_ref[0, :, :span]
     weight_sum = field_ref[1, :, :span]
@@ -400,24 +404,21 @@
     parts = lax.all_to_all(parts, "mem", split_axis=0, concat_axis=0, tiled=True)
     field_lanes = lanes + 2 * LANES
     strip = shape(quarters, HALO, field_lanes)
-    mid, top, bottom = call(
+    rim_lanes = -(-(quarters * members + 4) * HALO // LANES) * LANES
+    mid, edge = call(
         reduce_kernel,
-        (shape(quarters, rows, field_lanes), strip, strip),
+        (shape(quarters, rows, field_lanes), shape(rows, rim_lanes)),
         [
             pltpu.VMEM((quarters, rows, 2 * LANES), F32),
             wide,
             pltpu.VMEM((rows + 2 * HALO, 2 * width), F32),
         ],
     )(parts, diffusivity, sea_mask, own, far, near)
-    north, south = shift(top, bottom, "lat")
-    rim_lanes = -(-(quarters * members + 4) * HALO // LANES) * LANES
-    edge, north, south = call(
-        functools.partial(rim_kernel, lanes=lanes, span=span),
-        (shape(height, rim_lanes), strip, strip),
-    )(mid, north, south)
     devices = lax.axis_size("lon") * quarters
     ends = [(i - 1, i % devices) for i in range(quarters, devices + 1, quarters)]
     got = lax.ppermute(edge, ("lon", "mem"), ends + [(j, i) for i, j in ends])
+    top, bottom = call(functools.partial(rim_kernel, lanes=lanes, span=span), (strip, strip))(mid, got)
+    north, south = shift(top, bottom, "lat")
     quarter = call(
         product_kernel,
         shape(quarters, rows // 2, 2 * width),

time: 112 us -> 112 us (level)
    ppermute x1, starting transfers between devices: 1.55 us -> 2.7 us  [shift(): lax.ppermute(last, axis, up)]
where the time goes in v7:
time: 112 us
  blocking collectives  72.1 us (64%)
  starting transfers between devices  14.5 us (13%)
  Pallas kernels  12.2 us (11%)
  waiting for transfers between devices  11.1 us (10%)
    all_to_all x1, blocking collectives, per_device(): lax.all_to_all(outgoing, tiles, split_axis=0, concat_axis=0, tiled=True)  32.7 us
    all_to_all x1, blocking collectives, per_device(): lax.all_to_all(answers, tiles, split_axis=0, concat_axis=0, tiled=True)  22.5 us
    pallas_call x8, Pallas kernels, run(): pl.pallas_call(kernel, out_shape=outs, in_specs=[place] * len(operands),...  12.2 us
    all_to_all x1, blocking collectives, per_device(): lax.all_to_all(parts, 'mem', split_axis=0, concat_axis=0, tiled=True)  10 us
    all_to_all x1, blocking collectives, per_device(): lax.all_to_all(quarter, 'mem', split_axis=0, concat_axis=0, tiled=True)  6.96 us
    ppermute x1, starting transfers between devices, per_device(): far = lax.ppermute(far, 'mem', [(i, i ^ 2) for i in range(quarters)])  6.64 us
    ppermute x1, waiting for transfers between devices, per_device(): got = lax.ppermute(edge, ('lon', 'mem'), ends + [(j, i) for i, j in ends])  6.59 us
    ppermute x1, starting transfers between devices, per_device(): near = lax.ppermute(passed, 'mem', [(i, i ^ 1) for i in range(quarters)])  3.1 us
  transfers between devices with their start and end apart: 5, of which 3 were waited for; matrix products, arithmetic and copies ran while one was open for 0% of the time, Pallas kernels for 1%

profile of v7, /device:TPU:1, one launch (start us, length us, event | category | flops | bytes accessed | tf_op | source)
XLA Modules:
  0.0 111.7 jit_solution(13114307609045508814)
XLA Ops:
  0.6 0.9 copy-done
  1.6 0.9 shard_map.87
  2.5 0.0 copy-start.3
  2.5 6.6 %collective-permute-start = (f32[2,64,640]{2,1,0:T(8,128)S(1)}, f32[2,64,640]{2,1,0:T(8,128)S(1)}, u32[]{:S(2)}, u32[]{:S(2)}) collective-permute-start(f32[2,64,640]{2,1,0:T(8,128)S(1)} %get-tuple-element.19), channel_id=1, source_target_pairs={{0,2},{1,3},{2,0},{3,1},{4,6},{5,7},{6,4},{7,5},{8,10},{9,11},{10,... | collective-permute-start | bytes 983048 | tf_op jit(solution)/shard_map/ppermute | solution.py:395
  9.2 1.6 %shard_map.86 = (f32[128,128]{1,0:T(8,128)S(1)}, f32[16,128]{1,0:T(8,128)S(1)}) custom-call(s32[16,128]{1,0:T(8,128)S(1)} %bitcast.17, s32[16,128]{1,0:T(8,128)S(1)} %bitcast.21, f32[16,128]{1,0:T(8,128)S(1)} %bitcast.19, f32[16,128]{1,0:T(8,128)S(1)} %bitcast.22), custom_call_target="tpu_custom_call" | custom-call | tf_op jit(solution)/shard_map/pallas_call | solution.py:24
  10.9 32.7 %all_to_all.33 = f32[128,1,128]{2,1,0:T(1,128)S(1)} all-to-all(f32[128,1,128]{2,1,0:T(1,128)S(1)} %bitcast.16), channel_id=1, replica_groups=mesh['lat'=8,'lon'=16,'mem'=4] {'lat','lon'}, dimensions={0} | all-to-all | bytes 131072 | tf_op jit(solution)/shard_map/all_to_all | solution.py:394
  43.6 0.0 collective-permute-done.far_ref.rest_1_
  43.6 1.1 shard_map.88
  44.7 3.1 %collective-permute-start.1 = (f32[2,64,640]{2,1,0:T(8,128)S(1)}, f32[2,64,640]{2,1,0:T(8,128)S(1)}, u32[]{:S(2)}, u32[]{:S(2)}) collective-permute-start(f32[2,64,640]{2,1,0:T(8,128)S(1)} %get-tuple-element.25), channel_id=1, source_target_pairs={{0,1},{1,0},{2,3},{3,2},{4,5},{5,4},{6,7},{7,6},{8,9},{9,8},{10,11... | collective-permute-start | bytes 983048 | tf_op jit(solution)/shard_map/ppermute | solution.py:403
  47.8 0.0 copy-start.1
  47.8 0.0 copy-start.2
  47.8 10.0 %all_to_all.34.parts_ref = f32[4,80,128]{2,1,0:T(8,128)S(1)} all-to-all(f32[4,80,128]{2,1,0:T(8,128)S(1)} %get-tuple-element.23), channel_id=1, replica_groups=mesh['lat'=8,'lon'=16,'mem'=4] {'mem'}, dimensions={0} | all-to-all | bytes 327680 | tf_op jit(solution)/shard_map/all_to_all | solution.py:404
  57.8 0.7 shard_map.89
  58.6 2.1 %collective-permute-start.2 = (f32[64,384]{1,0:T(8,128)S(1)}, f32[64,384]{1,0:T(8,128)S(1)}, u32[]{:S(2)}, u32[]{:S(2)}) collective-permute-start(f32[64,384]{1,0:T(8,128)S(1)} %get-tuple-element.27), channel_id=1, source_target_pairs={{3,4},{7,8},{11,12},{15,16},{19,20},{23,24},{27,28},{31,32},{35,36... | collective-permute-start | bytes 294920 | tf_op jit(solution)/shard_map/ppermute | solution.py:419
  60.7 6.6 %collective-permute-done.2.got_ref = f32[64,384]{1,0:T(8,128)S(1)} collective-permute-done((f32[64,384]{1,0:T(8,128)S(1)}, f32[64,384]{1,0:T(8,128)S(1)}, u32[]{:S(2)}, u32[]{:S(2)}) %collective-permute-start.2) | collective-permute-done | bytes 98336 | tf_op jit(solution)/shard_map/ppermute | solution.py:419
  67.2 0.1 shard_map.90
  67.4 2.7 %collective-permute-start.3 = (f32[4,8,896]{2,1,0:T(8,128)S(1)}, f32[4,8,896]{2,1,0:T(8,128)S(1)}, u32[]{:S(2)}, u32[]{:S(2)}) collective-permute-start(f32[4,8,896]{2,1,0:T(8,128)S(1)} %get-tuple-element.28), channel_id=1, source_target_pairs={{0,64},{64,128},{128,192},{192,256},{256,320},{320,384},{384,448},... | collective-permute-start | bytes 344072 | tf_op jit(solution)/shard_map/ppermute | solution.py:364
  70.1 1.8 %collective-permute-done.3.north_ref = f32[4,8,896]{2,1,0:T(8,128)S(1)} collective-permute-done((f32[4,8,896]{2,1,0:T(8,128)S(1)}, f32[4,8,896]{2,1,0:T(8,128)S(1)}, u32[]{:S(2)}, u32[]{:S(2)}) %collective-permute-start.3) | collective-permute-done | bytes 114720 | tf_op jit(solution)/shard_map/ppermute | solution.py:364
  71.9 2.7 %collective-permute-done.4.south_ref = f32[4,8,896]{2,1,0:T(8,128)S(1)} collective-permute-done((f32[4,8,896]{2,1,0:T(8,128)S(1)}, f32[4,8,896]{2,1,0:T(8,128)S(1)}, u32[]{:S(2)}, u32[]{:S(2)}) %collective-permute-start.4) | collective-permute-done | bytes 114720 | tf_op jit(solution)/shard_map/ppermute | solution.py:364
  74.6 5.4 %shard_map.91 = f32[4,32,128]{2,1,0:T(8,128)S(1)} custom-call(f32[4,64,896]{2,1,0:T(8,128)S(1)} %get-tuple-element.26.mid_ref, f32[4,8,896]{2,1,0:T(8,128)S(1)} %collective-permute-done.3.north_ref, f32[4,8,896]{2,1,0:T(8,128)S(1)} %collective-permute-done.4.south_ref, f32[64,384]{1,0:T(8,128)S(1)} %collective-permute-done.2.got_ref), custom_call_target="tpu_custom_call" | custom-call | tf_op jit(solution)/shard_map/pallas_call | solution.py:24
  80.0 7.0 %all_to_all.35.pieces_ref = f32[4,32,128]{2,1,0:T(8,128)S(1)} all-to-all(f32[4,32,128]{2,1,0:T(8,128)S(1)} %shard_map.91), channel_id=1, replica_groups=mesh['lat'=8,'lon'=16,'mem'=4] {'mem'}, dimensions={0} | all-to-all | bytes 131072 | tf_op jit(solution)/shard_map/all_to_all | solution.py:433
  87.0 1.4 %shard_map.92 = (f32[64,256]{1,0:T(8,128)}, f32[128,32]{1,0:T(8,128)S(1)}) custom-call(f32[4,32,128]{2,1,0:T(8,128)S(1)} %all_to_all.35.pieces_ref, f32[128,128]{1,0:T(8,128)S(1)} %get-tuple-element.30.turned_ref), custom_call_target="tpu_custom_call" | custom-call | tf_op jit(solution)/shard_map/pallas_call | solution.py:24
  88.3 22.5 %all_to_all.36 = f32[128,1,32]{2,1,0:T(1,128)S(1)} all-to-all(f32[128,1,32]{2,1,0:T(1,128)S(1)} %bitcast.15), channel_id=1, replica_groups=mesh['lat'=8,'lon'=16,'mem'=4] {'lat','lon'}, dimensions={0} | all-to-all | bytes 32768 | tf_op jit(solution)/shard_map/all_to_all | solution.py:437
  110.8 1.0 shard_map.93
  (12 shorter events, 0.0 us)
Async XLA Ops:
  0.6 1.0 copy-start
  1.6 7.6 %copy-start.4 = (f32[2048]{0:T(1024)S(1)}, f32[2048]{0:T(1024)}, u32[]{:S(2)}) copy-start(f32[2048]{0:T(1024)} %param.12) | copy-start | bytes 24580
  1.6 7.6 %copy-start.5 = (s32[2048]{0:T(1024)S(1)}, s32[2048]{0:T(1024)}, u32[]{:S(2)}) copy-start(s32[2048]{0:T(1024)} %param.11) | copy-start | bytes 24580
  1.6 7.6 %copy-start.6 = (f32[2048]{0:T(1024)S(1)}, f32[2048]{0:T(1024)}, u32[]{:S(2)}) copy-start(f32[2048]{0:T(1024)} %param.13) | copy-start | bytes 24580
  2.5 6.7 %copy-start.3 = (s32[2048,1]{0,1:T(1,128)S(1)}, s32[2048,1]{0,1:T(1,128)}, u32[]{:S(2)}) copy-start(s32[2048,1]{0,1:T(1,128)} %param.10) | copy-start | bytes 24580
  2.5 41.0 %collective-permute-start = (f32[2,64,640]{2,1,0:T(8,128)S(1)}, f32[2,64,640]{2,1,0:T(8,128)S(1)}, u32[]{:S(2)}, u32[]{:S(2)}) collective-permute-start(f32[2,64,640]{2,1,0:T(8,128)S(1)} %get-tuple-element.19), channel_id=1, source_target_pairs={{0,2},{1,3},{2,0},{3,1},{4,6},{5,7},{6,4},{7,5},{8,10},{9,11},{10,... | collective-permute-start | bytes 983048 | tf_op jit(solution)/shard_map/ppermute | solution.py:395
  44.7 13.2 %collective-permute-start.1 = (f32[2,64,640]{2,1,0:T(8,128)S(1)}, f32[2,64,640]{2,1,0:T(8,128)S(1)}, u32[]{:S(2)}, u32[]{:S(2)}) collective-permute-start(f32[2,64,640]{2,1,0:T(8,128)S(1)} %get-tuple-element.25), channel_id=1, source_target_pairs={{0,1},{1,0},{2,3},{3,2},{4,5},{5,4},{6,7},{7,6},{8,9},{9,8},{10,11... | collective-permute-start | bytes 983048 | tf_op jit(solution)/shard_map/ppermute | solution.py:403
  47.8 10.1 %copy-start.1 = (f32[64,256]{1,0:T(8,128)S(1)}, f32[64,256]{1,0:T(8,128)}, u32[]{:S(2)}) copy-start(f32[64,256]{1,0:T(8,128)} %rate_ref.1) | copy-start | bytes 196612
  47.8 10.0 %copy-start.2 = (s32[64,256]{1,0:T(8,128)S(1)}, s32[64,256]{1,0:T(8,128)}, u32[]{:S(2)}) copy-start(s32[64,256]{1,0:T(8,128)} %sea_ref.1) | copy-start | bytes 196612
  58.6 8.7 %collective-permute-start.2 = (f32[64,384]{1,0:T(8,128)S(1)}, f32[64,384]{1,0:T(8,128)S(1)}, u32[]{:S(2)}, u32[]{:S(2)}) collective-permute-start(f32[64,384]{1,0:T(8,128)S(1)} %get-tuple-element.27), channel_id=1, source_target_pairs={{3,4},{7,8},{11,12},{15,16},{19,20},{23,24},{27,28},{31,32},{35,36... | collective-permute-start | bytes 294920 | tf_op jit(solution)/shard_map/ppermute | solution.py:419
  67.4 4.5 %collective-permute-start.3 = (f32[4,8,896]{2,1,0:T(8,128)S(1)}, f32[4,8,896]{2,1,0:T(8,128)S(1)}, u32[]{:S(2)}, u32[]{:S(2)}) collective-permute-start(f32[4,8,896]{2,1,0:T(8,128)S(1)} %get-tuple-element.28), channel_id=1, source_target_pairs={{0,64},{64,128},{128,192},{192,256},{256,320},{320,384},{384,448},... | collective-permute-start | bytes 344072 | tf_op jit(solution)/shard_map/ppermute | solution.py:364
  70.1 4.5 %collective-permute-start.4 = (f32[4,8,896]{2,1,0:T(8,128)S(1)}, f32[4,8,896]{2,1,0:T(8,128)S(1)}, u32[]{:S(2)}, u32[]{:S(2)}) collective-permute-start(f32[4,8,896]{2,1,0:T(8,128)S(1)} %get-tuple-element.29), channel_id=1, source_target_pairs={{64,0},{128,64},{192,128},{256,192},{320,256},{384,320},{448,384},... | collective-permute-start | bytes 344072 | tf_op jit(solution)/shard_map/ppermute | solution.py:364
